TPU v7x, 1024 devices: a whole 4x8x16 slice. The times are simulated.
1024 devices in a mesh: rep: 8 (over z_lo), node: 16 (over y, core), local: 8 (over x, z_hi).
Axes of the slice: x: 4, y: 8, z: 16 (z_hi: 2, z_lo: 8; z = z_hi * 8 + z_lo), core: 2. Of those that a mesh axis runs over, the one named last changes fastest.
Arguments:
- activations: bfloat16 [16384, 3584], P(('rep', 'node', 'local')), may hold values from -6 to 6
- cotangent: bfloat16 [16384, 1024], P(('rep', 'node', 'local')), may hold values from -6 to 6
- gates: bfloat16 [16384, 8], P(('rep', 'node', 'local')), may hold values from 0.049804688 to 0.5
- experts: int32 [16384, 8], P(('rep', 'node', 'local')), may hold values from 0 to 7, as said below
- groups: int32 [16384, 4], P(('rep', 'node', 'local')), may hold values from 0 to 15, as said below
- weights: bfloat16 [128, 3584, 1024], P(('node', 'local')), may hold values from -0.09375 to 0.09375
Outputs:
- output: bfloat16 [16384, 1024], P(('rep', 'node', 'local'))
- grad_activations: bfloat16 [16384, 3584], P(('rep', 'node', 'local'))
- grad_gates: bfloat16 [16384, 8], P(('rep', 'node', 'local'))
- grad_weights: float32 [128, 3584, 1024], P(('node', 'local'), 'rep')
Inputs may be any that keep to these rules, and one draw needn't show every extreme that they name: Each token names 4 different groups. The tokens of one device fall into aligned blocks of 4 consecutive tokens, and in every block each group is named by exactly one token. experts[n, 2k] and experts[n, 2k + 1] differ. Consider the rows that reach the device of local index l in group g: one for every token, on a device of local index l of the same replica, that names g, taken in the order of the source group g2 and then of the token's block b (place g2 * 4 + b). At most 21 of these 64 rows name any one expert of group g, and for every such device one expert is named by exactly 21 of them.
All inputs are finite; a program needn't handle non-finite values.
Results may differ from a plain program's by a relative error of at most 0.013.
Values may be sent and summed in bfloat16 or wider, within the bound.
No kernel may reach another device: no remote copies, remote signals or barrier semaphores. Data moves between devices by JAX's collectives and lax.ppermute only.
A program may use at most 64 MiB of HBM per device.

v0:
```python
import jax
import jax.numpy as jnp
from jax import lax
from jax.sharding import PartitionSpec as P


def on_device(activations, cotangent, gates, experts, groups, weights):
    node_count = lax.axis_size("node")
    local_count = lax.axis_size("local")
    rep_count = lax.axis_size("rep")
    tokens_here = activations.shape[0]
    feature_width = activations.shape[1]
    hidden = weights.shape[2]
    group_count = groups.shape[1]
    slot_total = experts.shape[1]
    per_group = slot_total // group_count
    block_size = node_count // group_count
    cap_node = tokens_here // block_size
    rows_two = node_count * cap_node
    cap_local = max(rows_two // 3, (per_group * rows_two + local_count - 1) // local_count)
    group_hit = (
        groups[:, :, None] == jnp.arange(node_count, dtype=jnp.int32)[None, None, :]
    ).astype(jnp.float32)
    block_hit = (
        (jnp.arange(tokens_here, dtype=jnp.int32) // block_size)[:, None]
        == jnp.arange(cap_node, dtype=jnp.int32)[None, :]
    ).astype(jnp.float32)
    placing = jnp.einsum("tkg,tb->gbtk", group_hit, block_hit)
    token_place = jnp.sum(placing, axis=3).astype(jnp.bfloat16)
    local_hit = (
        (experts % local_count)[:, :, None]
        == jnp.arange(local_count, dtype=jnp.int32)[None, None, :]
    ).astype(jnp.float32)
    pair_of = (
        jnp.arange(slot_total, dtype=jnp.int32)[None, :] // per_group
        == jnp.arange(group_count, dtype=jnp.int32)[:, None]
    ).astype(jnp.float32)
    token_weight = jnp.einsum("tj,kj,tjl->tkl", gates.astype(jnp.float32), pair_of, local_hit)
    send_x = jnp.einsum(
        "gbt,td->gbd", token_place, activations, preferred_element_type=jnp.float32
    ).astype(jnp.bfloat16)
    send_dy = jnp.einsum(
        "gbt,th->gbh", token_place, cotangent, preferred_element_type=jnp.float32
    ).astype(jnp.bfloat16)
    send_gate = jnp.einsum("gbtk,tkl->gbl", placing, token_weight).astype(jnp.bfloat16)
    got_x, got_dy, got_gate = (
        lax.all_to_all(send_x, "node", split_axis=0, concat_axis=0, tiled=True),
        lax.all_to_all(send_dy, "node", split_axis=0, concat_axis=0, tiled=True),
        lax.all_to_all(send_gate, "node", split_axis=0, concat_axis=0, tiled=True),
    )
    row_x = got_x.reshape(rows_two, feature_width)
    row_dy = got_dy.reshape(rows_two, hidden)
    row_gate = got_gate.reshape(rows_two, local_count)
    live_mask = row_gate != 0
    slot_rank = jnp.cumsum(live_mask.astype(jnp.int32), axis=0) - 1
    picker = live_mask[None, :, :] & (
        slot_rank[None, :, :] == jnp.arange(cap_local, dtype=jnp.int32)[:, None, None]
    )
    picker = jnp.transpose(picker, (2, 0, 1)).astype(jnp.float32)
    picker_half = picker.astype(jnp.bfloat16)
    slot_x = jnp.einsum(
        "lcs,sd->lcd", picker_half, row_x, preferred_element_type=jnp.float32
    ).astype(jnp.bfloat16)
    slot_dy = jnp.einsum(
        "lcs,sh->lch", picker_half, row_dy, preferred_element_type=jnp.float32
    ).astype(jnp.bfloat16)
    slot_gate = jnp.einsum("lcs,sl->lc", picker, row_gate.astype(jnp.float32))
    in_x, in_dy, in_gate = (
        lax.all_to_all(slot_x, "local", split_axis=0, concat_axis=0, tiled=True),
        lax.all_to_all(slot_dy, "local", split_axis=0, concat_axis=0, tiled=True),
        lax.all_to_all(
            slot_gate.astype(jnp.bfloat16), "local", split_axis=0, concat_axis=0, tiled=True
        ),
    )
    expert_rows = local_count * cap_local
    exp_x = in_x.reshape(expert_rows, feature_width)
    exp_dy = in_dy.reshape(expert_rows, hidden)
    exp_gate = in_gate.reshape(expert_rows)
    expert_weight = weights[0]
    pre_act = jnp.dot(exp_x, expert_weight, preferred_element_type=jnp.float32)
    sigmoid_pre = jax.nn.sigmoid(pre_act)
    activated = (pre_act * sigmoid_pre).astype(jnp.bfloat16)
    slope_term = sigmoid_pre * (1.0 + pre_act * (1.0 - sigmoid_pre))
    grad_pre = (
        exp_gate.astype(jnp.float32)[:, None] * exp_dy.astype(jnp.float32) * slope_term
    ).astype(jnp.bfloat16)
    grad_in = lax.dot_general(
        grad_pre, expert_weight, (((1,), (1,)), ((), ())), preferred_element_type=jnp.float32
    ).astype(jnp.bfloat16)
    back_act, back_grad = (
        lax.all_to_all(
            activated.reshape(local_count, cap_local, hidden),
            "local",
            split_axis=0,
            concat_axis=0,
            tiled=True,
        ),
        lax.all_to_all(
            grad_in.reshape(local_count, cap_local, feature_width),
            "local",
            split_axis=0,
            concat_axis=0,
            tiled=True,
        ),
    )
    weighted = picker * slot_gate[:, :, None]
    part_y = jnp.einsum(
        "lcs,lch->sh", weighted, back_act.astype(jnp.float32), precision=lax.Precision.HIGHEST
    ).astype(jnp.bfloat16)
    part_dx = jnp.einsum(
        "lcs,lcd->sd", picker_half, back_grad, preferred_element_type=jnp.float32
    ).astype(jnp.bfloat16)
    slot_dg = jnp.sum(slot_dy.astype(jnp.float32) * back_act.astype(jnp.float32), axis=2)
    part_dg = jnp.einsum("lcs,lc->sl", picker, slot_dg).astype(jnp.bfloat16)
    returned_y, returned_dx, returned_dg = (
        lax.all_to_all(
            part_y.reshape(node_count, cap_node, hidden),
            "node",
            split_axis=0,
            concat_axis=0,
            tiled=True,
        ),
        lax.all_to_all(
            part_dx.reshape(node_count, cap_node, feature_width),
            "node",
            split_axis=0,
            concat_axis=0,
            tiled=True,
        ),
        lax.all_to_all(
            part_dg.reshape(node_count, cap_node, local_count),
            "node",
            split_axis=0,
            concat_axis=0,
            tiled=True,
        ),
    )
    output = jnp.einsum(
        "gbt,gbh->th", token_place, returned_y, preferred_element_type=jnp.float32
    ).astype(jnp.bfloat16)
    grad_activations = jnp.einsum(
        "gbt,gbd->td", token_place, returned_dx, preferred_element_type=jnp.float32
    ).astype(jnp.bfloat16)
    grad_gates = jnp.einsum(
        "gbtk,kj,gbl,tjl->tj", placing, pair_of, returned_dg.astype(jnp.float32), local_hit
    ).astype(jnp.bfloat16)
    share_rows = feature_width // rep_count
    first_row = lax.axis_index("rep") * share_rows
    x_cols = lax.dynamic_slice_in_dim(
        lax.all_gather(exp_x, "rep", axis=0, tiled=True), first_row, share_rows, 1
    )
    grad_share = lax.dot_general(
        x_cols,
        lax.all_gather(grad_pre, "rep", axis=0, tiled=True),
        (((0,), (0,)), ((), ())),
        preferred_element_type=jnp.float32,
    )
    return (output, grad_activations, grad_gates, grad_share[None])


def solution(mesh):
    placed = (
        P(("rep", "node", "local"), None),
        P(("rep", "node", "local"), None),
        P(("rep", "node", "local"), None),
        P(("rep", "node", "local"), None),
        P(("rep", "node", "local"), None),
        P(("node", "local"), None, None),
    )
    return jax.shard_map(
        on_device,
        mesh=mesh,
        in_specs=placed,
        out_specs=(
            P(("rep", "node", "local"), None),
            P(("rep", "node", "local"), None),
            P(("rep", "node", "local"), None),
            P(("node", "local"), "rep", None),
        ),
        check_vma=False,
    )
```

profile of v0, /device:TPU:1, one launch (start us, length us, event | category | flops | bytes accessed | tf_op | source)
XLA Modules:
  0.0 565.5 jit_solution(336748499605826423)
XLA Ops:
  7.2 0.7 fusion.52
  7.9 0.7 add_select_fusion
  8.7 0.7 convert_bitcast_fusion
  9.5 0.2 fusion.29
  9.7 0.1 copy.62
  9.8 0.2 fusion.14
  9.9 0.7 copy.63
  10.7 17.4 %all-to-all-start = ((bf16[16,4,8]{2,1,0:T(4,128)(2,1)}), bf16[16,4,8]{2,1,0:T(4,128)(2,1)S(1)}, u32[]{:S(2)}, u32[]{:S(2)}) async-start(bf16[16,4,8]{2,1,0:T(4,128)(2,1)} %copy.63), calls=%async_computation | async-start | bytes 32768 | tf_op jit(solution)/shard_map/all_to_all | solution.py:49
  28.1 7.4 %all-to-all-done = bf16[16,4,8]{2,1,0:T(4,128)(2,1)S(1)} async-done(((bf16[16,4,8]{2,1,0:T(4,128)(2,1)}), bf16[16,4,8]{2,1,0:T(4,128)(2,1)S(1)}, u32[]{:S(2)}, u32[]{:S(2)}) %all-to-all-start) | async-done | bytes 1056 | tf_op jit(solution)/shard_map/all_to_all | solution.py:49
  35.5 0.1 reduce_window_sum.11
  35.8 0.1 copy.77
  35.9 0.2 fusion.27
  36.0 0.6 copy.69
  36.6 12.0 %all-to-all-start.5 = ((bf16[8,1,21]{2,1,0:T(2,128)(2,1)}), bf16[8,1,21]{2,1,0:T(2,128)(2,1)S(1)}, u32[]{:S(2)}, u32[]{:S(2)}) async-start(bf16[8,1,21]{2,1,0:T(2,128)(2,1)} %copy.69), calls=%async_computation.5 | async-start | bytes 8192 | tf_op jit(solution)/shard_map/all_to_all | solution.py:71
  48.6 0.9 convolution_convert_fusion.3
  49.6 0.8 copy.70
  50.3 12.0 %all-to-all-done.5 = bf16[8,1,21]{2,1,0:T(2,128)(2,1)S(1)} async-done(((bf16[8,1,21]{2,1,0:T(2,128)(2,1)}), bf16[8,1,21]{2,1,0:T(2,128)(2,1)S(1)}, u32[]{:S(2)}, u32[]{:S(2)}) %all-to-all-start.5) | async-done | bytes 368 | tf_op jit(solution)/shard_map/all_to_all | solution.py:71
  62.3 5.1 all-to-all-start.6
  67.4 0.2 convolution_convert_fusion.1
  67.7 1.1 copy.66
  68.8 7.8 %all-to-all-done.6 = bf16[16,4,1024]{2,1,0:T(4,128)(2,1)S(1)} async-done(((bf16[16,4,1024]{2,1,0:T(4,128)(2,1)}), bf16[16,4,1024]{2,1,0:T(4,128)(2,1)S(1)}, u32[]{:S(2)}, u32[]{:S(2)}) %all-to-all-start.6) | async-done | bytes 131104 | tf_op jit(solution)/shard_map/all_to_all | solution.py:48
  76.6 3.5 all-to-all-start.1
  80.1 1.0 convolution_convert_fusion.2
  81.1 14.5 %all-to-all-done.1 = bf16[16,4,3584]{2,1,0:T(4,128)(2,1)S(1)} async-done(((bf16[16,4,3584]{2,1,0:T(4,128)(2,1)}), bf16[16,4,3584]{2,1,0:T(4,128)(2,1)S(1)}, u32[]{:S(2)}, u32[]{:S(2)}) %all-to-all-start.1) | async-done | bytes 458784 | tf_op jit(solution)/shard_map/all_to_all | solution.py:47
  95.7 3.5 all-to-all-start.7
  99.1 0.1 reshape.135
  99.2 1.6 convolution_convert_fusion
  100.8 15.9 %all-to-all-done.7 = bf16[8,21,1024]{2,1,0:T(8,128)(2,1)S(1)} async-done(((bf16[8,21,1024]{2,1,0:T(8,128)(2,1)}), bf16[8,21,1024]{2,1,0:T(8,128)(2,1)S(1)}, u32[]{:S(2)}, u32[]{:S(2)}) %all-to-all-start.7) | async-done | bytes 344096 | tf_op jit(solution)/shard_map/all_to_all | solution.py:70
  116.7 11.5 %all-to-all-start.2 = ((bf16[8,21,3584]{2,1,0:T(8,128)(2,1)}), bf16[8,21,3584]{2,1,0:T(8,128)(2,1)S(1)}, u32[]{:S(2)}, u32[]{:S(2)}) async-start(bf16[8,21,3584]{2,1,0:T(8,128)(2,1)} %convolution_convert_fusion), calls=%async_computation.2 | async-start | bytes 2752512 | tf_op jit(solution)/shard_map/all_to_all | solution.py:69
  128.2 0.1 reshape.128
  128.3 0.1 reshape.129
  128.4 21.2 %all-to-all-done.2 = bf16[8,21,3584]{2,1,0:T(8,128)(2,1)S(1)} async-done(((bf16[8,21,3584]{2,1,0:T(8,128)(2,1)}), bf16[8,21,3584]{2,1,0:T(8,128)(2,1)S(1)}, u32[]{:S(2)}, u32[]{:S(2)}) %all-to-all-start.2) | async-done | bytes 1204256 | tf_op jit(solution)/shard_map/all_to_all | solution.py:69
  149.6 0.4 reshape.121
  150.0 5.9 %multiply_convert_fusion = (bf16[168,1024]{1,0:T(8,128)(2,1)}, bf16[168,1024]{1,0:T(8,128)(2,1)S(1)}) fusion(f32[168,1024]{1,0:T(8,128)S(1)} %reshape.129, f32[168]{0:T(256)S(1)} %reshape.128, bf16[168,3584]{1,0:T(8,128)(2,1)S(1)} %reshape.121, bf16[1,3584,1024]{2,1,0:T(8,128)(2,1)} %param.11), kind=kOutput, calls=%fused_computation.26 | convolution fusion | flops 1235189760 | bytes 9921184 | tf_op jit(solution)/shard_map/dot_general | solution.py:80
  156.0 0.7 all-gather.3.cloned.1.call-update
  156.7 0.1 reshape.122
  156.9 44.0 %all_to_all.59 = bf16[8,21,1024]{2,1,0:T(8,128)(2,1)S(1)} all-to-all(bf16[8,21,1024]{2,1,0:T(8,128)(2,1)S(1)} %reshape.122), channel_id=1, replica_groups=mesh['rep'=8,'node'=16,'local'=8] {'local'}, dimensions={0} | all-to-all | bytes 688128 | tf_op jit(solution)/shard_map/all_to_all | solution.py:91
  200.9 1.2 multiply_reduce_fusion
  202.1 0.1 fusion.24
  202.2 0.7 copy.82
  202.9 3.7 all-to-all-start.10
  206.6 5.7 fusion.4
  212.3 1.5 reshape.125
  213.7 0.3 all-to-all-done.10
  214.0 9.3 %all-to-all-start.8 = ((bf16[8,21,3584]{2,1,0:T(8,128)(2,1)}), bf16[8,21,3584]{2,1,0:T(8,128)(2,1)S(1)}, u32[]{:S(2)}, u32[]{:S(2)}) async-start(bf16[8,21,3584]{2,1,0:T(8,128)(2,1)} %reshape.125), calls=%async_computation.8 | async-start | bytes 2752512 | tf_op jit(solution)/shard_map/all_to_all | solution.py:98
  223.4 0.5 fusion.10
  223.8 0.7 reshape.123
  224.5 56.5 %all-to-all-done.8 = bf16[8,21,3584]{2,1,0:T(8,128)(2,1)S(1)} async-done(((bf16[8,21,3584]{2,1,0:T(8,128)(2,1)}), bf16[8,21,3584]{2,1,0:T(8,128)(2,1)S(1)}, u32[]{:S(2)}, u32[]{:S(2)}) %all-to-all-start.8) | async-done | bytes 1204256 | tf_op jit(solution)/shard_map/all_to_all | solution.py:98
  281.0 10.3 %all-to-all-start.4 = ((bf16[16,4,1024]{2,1,0:T(4,128)(2,1)}), bf16[16,4,1024]{2,1,0:T(4,128)(2,1)S(1)}, u32[]{:S(2)}, u32[]{:S(2)}) async-start(bf16[16,4,1024]{2,1,0:T(4,128)(2,1)} %reshape.123), calls=%async_computation.4 | async-start | bytes 262144 | tf_op jit(solution)/shard_map/all_to_all | solution.py:116
  291.4 0.4 fusion.7
  291.8 0.9 reshape.126
  292.7 7.9 %all-to-all-done.4 = bf16[16,4,1024]{2,1,0:T(4,128)(2,1)S(1)} async-done(((bf16[16,4,1024]{2,1,0:T(4,128)(2,1)}), bf16[16,4,1024]{2,1,0:T(4,128)(2,1)S(1)}, u32[]{:S(2)}, u32[]{:S(2)}) %all-to-all-start.4) | async-done | bytes 131104 | tf_op jit(solution)/shard_map/all_to_all | solution.py:116
  300.5 3.5 all-to-all-start.9
  304.0 0.1 copy.73
  304.1 0.2 convolution_bitcast_fusion.6
  304.3 0.1 copy.75
  304.4 0.2 fusion.13
  304.6 0.7 copy.90
  305.3 0.8 fusion.11
  306.1 13.9 %all-to-all-done.9 = bf16[16,4,3584]{2,1,0:T(4,128)(2,1)S(1)} async-done(((bf16[16,4,3584]{2,1,0:T(4,128)(2,1)}), bf16[16,4,3584]{2,1,0:T(4,128)(2,1)S(1)}, u32[]{:S(2)}, u32[]{:S(2)}) %all-to-all-start.9) | async-done | bytes 458784 | tf_op jit(solution)/shard_map/all_to_all | solution.py:123
  320.0 0.9 fusion.8
  320.8 28.9 %all-gather.5.cloned.1.call-done = bf16[1344,1024]{1,0:T(8,128)(2,1)} async-done(((bf16[168,1024]{1,0:T(8,128)(2,1)}), bf16[1344,1024]{1,0:T(8,128)(2,1)}) %all-gather.5.cloned.1.call-update) | async-done | bytes 2752528 | tf_op jit(solution)/shard_map/all_gather | solution.py:154
  349.7 203.6 %all-gather.3.cloned.1.call-done = bf16[1344,3584]{1,0:T(8,128)(2,1)} async-done(((bf16[168,3584]{1,0:T(8,128)(2,1)}), bf16[1344,3584]{1,0:T(8,128)(2,1)}) %all-gather.3.cloned.1.call-update) | async-done | bytes 9633808 | tf_op jit(solution)/shard_map/all_gather | solution.py:150
  553.4 5.3 convolution_bitcast_fusion.2
  (23 shorter events, 0.5 us)
Async XLA Ops:
  7.2 60.2 %copy-start = (bf16[16,3584]{1,0:T(8,128)(2,1)S(1)}, bf16[16,3584]{1,0:T(8,128)(2,1)}, u32[]{:S(2)}) copy-start(bf16[16,3584]{1,0:T(8,128)(2,1)} %param.6) | copy-start | bytes 344068
  10.7 24.9 %all-to-all-start = ((bf16[16,4,8]{2,1,0:T(4,128)(2,1)}), bf16[16,4,8]{2,1,0:T(4,128)(2,1)S(1)}, u32[]{:S(2)}, u32[]{:S(2)}) async-start(bf16[16,4,8]{2,1,0:T(4,128)(2,1)} %copy.63), calls=%async_computation | async-start | bytes 32768 | tf_op jit(solution)/shard_map/all_to_all | solution.py:49
  36.6 25.7 %all-to-all-start.5 = ((bf16[8,1,21]{2,1,0:T(2,128)(2,1)}), bf16[8,1,21]{2,1,0:T(2,128)(2,1)S(1)}, u32[]{:S(2)}, u32[]{:S(2)}) async-start(bf16[8,1,21]{2,1,0:T(2,128)(2,1)} %copy.69), calls=%async_computation.5 | async-start | bytes 8192 | tf_op jit(solution)/shard_map/all_to_all | solution.py:71
  62.3 14.3 %all-to-all-start.6 = ((bf16[16,4,1024]{2,1,0:T(4,128)(2,1)}), bf16[16,4,1024]{2,1,0:T(4,128)(2,1)S(1)}, u32[]{:S(2)}, u32[]{:S(2)}) async-start(bf16[16,4,1024]{2,1,0:T(4,128)(2,1)} %copy.70), calls=%async_computation.6 | async-start | bytes 262144 | tf_op jit(solution)/shard_map/all_to_all | solution.py:48
  76.6 19.0 %all-to-all-start.1 = ((bf16[16,4,3584]{2,1,0:T(4,128)(2,1)}), bf16[16,4,3584]{2,1,0:T(4,128)(2,1)S(1)}, u32[]{:S(2)}, u32[]{:S(2)}) async-start(bf16[16,4,3584]{2,1,0:T(4,128)(2,1)} %copy.66), calls=%async_computation.1 | async-start | bytes 917504 | tf_op jit(solution)/shard_map/all_to_all | solution.py:47
  95.7 21.0 %all-to-all-start.7 = ((bf16[8,21,1024]{2,1,0:T(8,128)(2,1)}), bf16[8,21,1024]{2,1,0:T(8,128)(2,1)S(1)}, u32[]{:S(2)}, u32[]{:S(2)}) async-start(bf16[8,21,1024]{2,1,0:T(8,128)(2,1)} %convolution_convert_fusion.2), calls=%async_computation.7 | async-start | bytes 786432 | tf_op jit(solution)/shard_map/all_to_all | solution.py:70
  116.7 33.0 %all-to-all-start.2 = ((bf16[8,21,3584]{2,1,0:T(8,128)(2,1)}), bf16[8,21,3584]{2,1,0:T(8,128)(2,1)S(1)}, u32[]{:S(2)}, u32[]{:S(2)}) async-start(bf16[8,21,3584]{2,1,0:T(8,128)(2,1)} %convolution_convert_fusion), calls=%async_computation.2 | async-start | bytes 2752512 | tf_op jit(solution)/shard_map/all_to_all | solution.py:69
  128.1 221.6 %all-gather.5.cloned.1.call-start = ((), (), s32[]{:S(2)}) async-start(), calls=%async_computation.12 | async-start | bytes 3096576 | tf_op jit(solution)/shard_map/all_gather | solution.py:154
  150.0 5.9 %copy-start.1 = (bf16[168,3584]{1,0:T(8,128)(2,1)}, bf16[168,3584]{1,0:T(8,128)(2,1)S(1)}, u32[]{:S(2)}) copy-start(bf16[168,3584]{1,0:T(8,128)(2,1)S(1)} %reshape.121) | copy-start | bytes 3612676
  156.0 50.6 %copy-start.2 = (bf16[168,1024]{1,0:T(8,128)(2,1)S(1)}, bf16[168,1024]{1,0:T(8,128)(2,1)}, u32[]{:S(2)}) copy-start(bf16[168,1024]{1,0:T(8,128)(2,1)} %get-tuple-element.4) | copy-start | bytes 1032196
  156.0 397.4 %all-gather.3.cloned.1.call-start = ((), (), s32[]{:S(2)}) async-start(), calls=%async_computation.11 | async-start | bytes 10838016 | tf_op jit(solution)/shard_map/all_gather | solution.py:150
  202.9 11.1 %all-to-all-start.10 = ((bf16[16,4,8]{2,1,0:T(4,128)(2,1)}), bf16[16,4,8]{2,1,0:T(4,128)(2,1)S(1)}, u32[]{:S(2)}, u32[]{:S(2)}) async-start(bf16[16,4,8]{2,1,0:T(4,128)(2,1)} %bitcast.26), calls=%async_computation.10 | async-start | bytes 32768 | tf_op jit(solution)/shard_map/all_to_all | solution.py:130
  214.0 67.0 %all-to-all-start.8 = ((bf16[8,21,3584]{2,1,0:T(8,128)(2,1)}), bf16[8,21,3584]{2,1,0:T(8,128)(2,1)S(1)}, u32[]{:S(2)}, u32[]{:S(2)}) async-start(bf16[8,21,3584]{2,1,0:T(8,128)(2,1)} %reshape.125), calls=%async_computation.8 | async-start | bytes 2752512 | tf_op jit(solution)/shard_map/all_to_all | solution.py:98
  281.0 19.5 %all-to-all-start.4 = ((bf16[16,4,1024]{2,1,0:T(4,128)(2,1)}), bf16[16,4,1024]{2,1,0:T(4,128)(2,1)S(1)}, u32[]{:S(2)}, u32[]{:S(2)}) async-start(bf16[16,4,1024]{2,1,0:T(4,128)(2,1)} %reshape.123), calls=%async_computation.4 | async-start | bytes 262144 | tf_op jit(solution)/shard_map/all_to_all | solution.py:116
  300.5 19.4 %all-to-all-start.9 = ((bf16[16,4,3584]{2,1,0:T(4,128)(2,1)}), bf16[16,4,3584]{2,1,0:T(4,128)(2,1)S(1)}, u32[]{:S(2)}, u32[]{:S(2)}) async-start(bf16[16,4,3584]{2,1,0:T(4,128)(2,1)} %reshape.126), calls=%async_computation.9 | async-start | bytes 917504 | tf_op jit(solution)/shard_map/all_to_all | solution.py:123
Sparse Core Ops, SparseCore 0:
  156.1 193.5 all-gather.4
  352.4 200.9 all-gather.2
where the time goes:
time: 567 us; the launch traced here: 565 us
  waiting for transfers between devices  391 us (69%)
  starting transfers between devices  79.9 us (14%)
  blocking collectives  44 us (8%)
  matrix products  24.2 us (4%)
  between operations  14.2 us (3%)
  local copies, waits for them, and re-layouts  9.14 us (2%)
    all_gather x1, waiting for transfers between devices, on_device(): lax.all_gather(exp_x, 'rep', axis=0, tiled=True)  204 us
    all_to_all x1, waiting for transfers between devices, on_device(): lax.all_to_all(grad_in.reshape(local_count, cap_local, feature_width), 'l...  56.5 us
    all_to_all x1, blocking collectives, on_device(): lax.all_to_all(activated.reshape(local_count, cap_local, hidden), 'local'...  44 us
    all_gather x1, waiting for transfers between devices, on_device(): lax.all_gather(grad_pre, 'rep', axis=0, tiled=True)  28.9 us
    all_to_all x1, waiting for transfers between devices, on_device(): lax.all_to_all(slot_x, 'local', split_axis=0, concat_axis=0, tiled=True)  21.2 us
    all_to_all x1, starting transfers between devices, on_device(): lax.all_to_all(send_gate, 'node', split_axis=0, concat_axis=0, tiled=True)  17.4 us
    all_to_all x1, waiting for transfers between devices, on_device(): lax.all_to_all(slot_dy, 'local', split_axis=0, concat_axis=0, tiled=True)  15.9 us
    all_to_all x1, waiting for transfers between devices, on_device(): lax.all_to_all(send_x, 'node', split_axis=0, concat_axis=0, tiled=True)  14.5 us
  transfers between devices with their start and end apart: 12, of which 12 were waited for; matrix products, arithmetic and copies ran while one was open for 4% of the time, Pallas kernels for 0%

commit v1 on v0

v1 whole, which is shorter than its diff:
```python
import jax
import jax.numpy as jnp
from jax import lax
from jax.sharding import Mesh, PartitionSpec as P

ALL = ("rep", "node", "x", "half")


def partner_pairs(reps):
    ring = 2 * reps
    step = reps // 2
    pairs = []
    for z in range(ring):
        other = z + step if (z // step) % 2 == 1 else z - step
        other %= ring
        pairs.append(((z % reps) * 2 + z // reps, (other % reps) * 2 + other // reps))
    return pairs


def on_device(activations, cotangent, gates, experts, groups, weights):
    reps = lax.axis_size("rep")
    nodes = lax.axis_size("node")
    xs = lax.axis_size("x")
    locals_ = xs * lax.axis_size("half")
    tokens, width = activations.shape
    hidden = weights.shape[2]
    slots = experts.shape[1]
    named = groups.shape[1]
    per_group = slots // named
    block = nodes // named
    blocks = tokens // block
    rows_one = nodes * blocks
    cap = max(rows_one // 3, (per_group * rows_one + locals_ - 1) // locals_)
    total = nodes * locals_
    bf = jnp.bfloat16
    f32 = jnp.float32
    pairs = partner_pairs(reps)
    rep_at = lax.axis_index("rep")
    node_at = lax.axis_index("node")
    x_at = lax.axis_index("x")
    half_at = lax.axis_index("half")

    expert_full = jnp.repeat(groups, per_group, axis=1) * locals_ + experts
    gate_wide = jnp.sum(
        jnp.where(
            expert_full[:, :, None] == jnp.arange(total, dtype=jnp.int32)[None, None, :],
            gates.astype(f32)[:, :, None],
            0.0,
        ),
        axis=1,
    ).astype(bf)
    own = jnp.concatenate([activations, cotangent, gate_wide], axis=1)
    wide = own.shape[1]
    other = lax.ppermute(own, ("rep", "half"), pairs)
    both = jnp.concatenate([own, other], axis=0)

    places = 2 * rows_one
    place_index = jnp.arange(places, dtype=jnp.int32)
    place_expert = (
        (place_index // (2 * blocks))[:, None]
        == (jnp.arange(total, dtype=jnp.int32) // locals_)[None, :]
    ).astype(bf)
    named_both = (both[:, width + hidden :] != 0).astype(bf)
    hit = lax.dot_general(
        place_expert, named_both, (((1,), (1,)), ((), ())), preferred_element_type=f32
    )
    placing = (
        (hit > 0)
        & (
            (place_index % (2 * blocks))[:, None]
            == (jnp.arange(2 * tokens, dtype=jnp.int32) // block)[None, :]
        )
    ).astype(bf)
    send_rows = jnp.dot(placing, both, preferred_element_type=f32).astype(bf)
    rows = lax.all_to_all(
        send_rows.reshape(nodes, 2 * blocks, wide), "node", 0, 0, tiled=True
    ).reshape(places, wide)

    cap2 = 2 * cap
    taken = xs * cap2
    slot_index = jnp.arange(taken, dtype=jnp.int32)
    slot_expert = (
        (node_at * locals_ + (slot_index // cap2) * 2 + half_at)[:, None]
        == jnp.arange(total, dtype=jnp.int32)[None, :]
    ).astype(bf)
    named_rows = (rows[:, width + hidden :] != 0).astype(bf)
    live = lax.dot_general(
        slot_expert, named_rows, (((1,), (1,)), ((), ())), preferred_element_type=f32
    )
    before = (place_index[:, None] < place_index[None, :]).astype(bf)
    rank = jnp.dot(live.astype(bf), before, preferred_element_type=f32)
    picker = (
        (live > 0) & (rank == (slot_index % cap2).astype(f32)[:, None])
    ).astype(bf)
    send_slots = jnp.dot(picker, rows, preferred_element_type=f32).astype(bf)
    inside = lax.all_to_all(
        send_slots.reshape(xs, cap2, wide), "x", 0, 0, tiled=True
    ).reshape(taken, wide)

    exp_x = inside[:, :width]
    exp_dy = inside[:, width : width + hidden].astype(f32)
    mine = jnp.arange(total, dtype=jnp.int32) == node_at * locals_ + x_at * 2 + half_at
    gate = jnp.sum(
        jnp.where(mine[None, :], inside[:, width + hidden :].astype(f32), 0.0), axis=1, keepdims=True
    )
    weight = weights[0]
    pre = jnp.dot(exp_x, weight, preferred_element_type=f32)
    sig = jax.nn.sigmoid(pre)
    act = (pre * sig).astype(bf).astype(f32)
    slope = sig * (1.0 + pre * (1.0 - sig))
    grad_pre = (gate * exp_dy * slope).astype(bf)
    grad_in = lax.dot_general(
        grad_pre, weight, (((1,), (1,)), ((), ())), preferred_element_type=f32
    ).astype(bf)
    grad_gate = jnp.sum(exp_dy * act, axis=1, keepdims=True)
    back = jnp.concatenate(
        [
            grad_in,
            (gate * act).astype(bf),
            jnp.where(mine[None, :], grad_gate, 0.0).astype(bf),
        ],
        axis=1,
    )

    share = width // reps
    gathered = lax.all_gather(grad_pre, "rep", axis=0, tiled=True)
    x_cols = jnp.zeros((reps * taken, share), bf)
    for k in range(reps):
        piece = lax.dynamic_slice_in_dim(exp_x, (rep_at + k) % reps * share, share, 1)
        if k:
            piece = lax.ppermute(piece, "rep", [(i, (i + k) % reps) for i in range(reps)])
        x_cols = lax.dynamic_update_slice_in_dim(
            x_cols, piece, (rep_at + reps - k) % reps * taken, 0
        )
    grad_share = lax.dot_general(
        x_cols, gathered, (((0,), (0,)), ((), ())), preferred_element_type=f32
    )

    back_slots = lax.all_to_all(
        back.reshape(xs, cap2, wide), "x", 0, 0, tiled=True
    ).reshape(taken, wide)
    back_rows = lax.dot_general(
        picker, back_slots, (((0,), (0,)), ((), ())), preferred_element_type=f32
    ).astype(bf)
    home_rows = lax.all_to_all(
        back_rows.reshape(nodes, 2 * blocks, wide), "node", 0, 0, tiled=True
    ).reshape(places, wide)
    home = lax.dot_general(
        placing, home_rows, (((0,), (0,)), ((), ())), preferred_element_type=f32
    )
    returned = lax.ppermute(home[tokens:].astype(bf), ("rep", "half"), pairs)
    result = home[:tokens] + returned.astype(f32)
    grad_activations = result[:, :width].astype(bf)
    output = result[:, width : width + hidden].astype(bf)
    gate_back = result[:, width + hidden :]
    grad_gates = jnp.sum(
        jnp.where(
            expert_full[:, :, None] == jnp.arange(total, dtype=jnp.int32)[None, None, :],
            gate_back[:, None, :],
            0.0,
        ),
        axis=2,
    ).astype(bf)
    return (output, grad_activations, grad_gates, grad_share[None])


def solution(mesh):
    reps, nodes, locals_ = (mesh.shape[name] for name in ("rep", "node", "local"))
    fine = Mesh(mesh.devices.reshape(reps, nodes, locals_ // 2, 2), ALL)
    rows = P(ALL, None)
    return jax.shard_map(
        on_device,
        mesh=fine,
        in_specs=(rows, rows, rows, rows, rows, P(("node", "x", "half"), None, None)),
        out_specs=(rows, rows, rows, P(("node", "x", "half"), "rep", None)),
        check_vma=False,
    )
```

time: 567 us -> 288 us (0.51)
  waiting for transfers between devices: 391 us -> 137 us
  blocking collectives: 44 us -> 0 us
  starting transfers between devices: 79.9 us -> 94.4 us
    all_gather x2 -> x1, waiting for transfers between devices: 233 us -> 0.01 us  [on_device(): gathered = lax.all_gather(grad_pre, 'rep', axis=0, tiled=True)]
    all_to_all x10 -> x4, waiting for transfers between devices: 157 us -> 76.9 us  [the longest x1 31.2 us: on_device(): lax.all_to_all(send_rows.reshape(nodes, 2 * blocks, wide), 'node', 0, 0,...]
    ppermute x0 -> x9, starting transfers between devices: none -> 73.4 us  [the longest x7 27.8 us: on_device(): lax.ppermute(piece, 'rep', [(i, (i + k) % reps) for i in range(reps)])]
    ppermute x0 -> x9, waiting for transfers between devices: none -> 59.5 us  [the longest x7 27 us: on_device(): lax.ppermute(piece, 'rep', [(i, (i + k) % reps) for i in range(reps)])]
    all_to_all x10 -> x4, starting transfers between devices: 79.8 us -> 21 us  [the longest x1 8.67 us: on_device(): lax.all_to_all(send_rows.reshape(nodes, 2 * blocks, wide), 'node', 0, 0,...]
    all_to_all x1 -> x0, blocking collectives: 44 us -> none  [on_device(): lax.all_to_all(activated.reshape(local_count, cap_local, hidden), 'local'...]
    dot_general x17 -> x10, matrix products: 24.2 us -> 23.1 us  [the longest x1 5.79 us: on_device(): pre = jnp.dot(exp_x, weight, preferred_element_type=f32)]
  transfers between devices with their start and end apart: 12 -> 14, of which waited for: 12 -> 9; matrix products, arithmetic and copies ran while one was open for 4% -> 3% of each run, Pallas kernels for 0% -> 0%
where the time goes in v1:
time: 288 us; the launch traced here: 283 us
  waiting for transfers between devices  137 us (48%)
  starting transfers between devices  94.4 us (33%)
  matrix products  23.1 us (8%)
  between operations  14.4 us (5%)
  local copies, waits for them, and re-layouts  11.2 us (4%)
  other arithmetic  3.33 us (1%)
    all_to_all x1, waiting for transfers between devices, on_device(): lax.all_to_all(send_rows.reshape(nodes, 2 * blocks, wide), 'node', 0, 0,...  31.2 us
    ppermute x7, starting transfers between devices, on_device(): lax.ppermute(piece, 'rep', [(i, (i + k) % reps) for i in range(reps)])  27.8 us
    ppermute x7, waiting for transfers between devices, on_device(): lax.ppermute(piece, 'rep', [(i, (i + k) % reps) for i in range(reps)])  27 us
    ppermute x1, starting transfers between devices, on_device(): returned = lax.ppermute(home[tokens:].astype(bf), ('rep', 'half'), pairs)  26.8 us
    all_to_all x1, waiting for transfers between devices, on_device(): lax.all_to_all(send_slots.reshape(xs, cap2, wide), 'x', 0, 0, tiled=True)  23.4 us
    all_to_all x1, waiting for transfers between devices, on_device(): lax.all_to_all(back.reshape(xs, cap2, wide), 'x', 0, 0, tiled=True)  22.3 us
    ppermute x1, waiting for transfers between devices, on_device(): returned = lax.ppermute(home[tokens:].astype(bf), ('rep', 'half'), pairs)  20.3 us
    ppermute x1, starting transfers between devices, on_device(): other = lax.ppermute(own, ('rep', 'half'), pairs)  18.7 us
  transfers between devices with their start and end apart: 14, of which 9 were waited for; matrix products, arithmetic and copies ran while one was open for 3% of the time, Pallas kernels for 0%

profile of v1, /device:TPU:1, one launch (start us, length us, event | category | flops | bytes accessed | tf_op | source)
XLA Modules:
  0.0 283.5 jit_solution(17143962402926148010)
XLA Ops:
  7.2 0.8 copy.15
  7.9 0.7 broadcast_multiply_fusion
  8.6 0.7 add.206
  9.3 0.1 copy.14
  9.4 0.1 select_reduce_fusion.2
  9.5 0.9 pad_maximum_fusion.1
  10.4 18.7 %collective-permute-start = (bf16[16,4736]{1,0:T(8,128)(2,1)S(1)}, bf16[16,4736]{1,0:T(8,128)(2,1)S(1)}, u32[]{:S(2)}, u32[]{:S(2)}) collective-permute-start(bf16[16,4736]{1,0:T(8,128)(2,1)S(1)} %pad_maximum_fusion.1), channel_id=1, source_target_pairs={{0,513},{128,641},{256,769},{384,897},{512,1},{640,129},{768,257},... | collective-permute-start | bytes 454664 | tf_op jit(solution)/shard_map/ppermute | solution.py:54
  29.2 12.3 %collective-permute-done = bf16[16,4736]{1,0:T(8,128)(2,1)S(1)} collective-permute-done((bf16[16,4736]{1,0:T(8,128)(2,1)S(1)}, bf16[16,4736]{1,0:T(8,128)(2,1)S(1)}, u32[]{:S(2)}, u32[]{:S(2)}) %collective-permute-start) | collective-permute-done | bytes 151584 | tf_op jit(solution)/shard_map/ppermute | solution.py:54
  41.5 0.2 fusion.12
  41.7 2.5 fusion.5
  44.2 8.7 %all-to-all-start = ((bf16[16,8,4736]{2,1,0:T(8,128)(2,1)}), bf16[16,8,4736]{2,1,0:T(8,128)(2,1)S(1)}, u32[]{:S(2)}, u32[]{:S(2)}) async-start(bf16[16,8,4736]{2,1,0:T(8,128)(2,1)} %fusion.5), calls=%async_computation | async-start | bytes 2424832 | tf_op jit(solution)/shard_map/all_to_all | solution.py:75
  52.9 31.2 %all-to-all-done = bf16[16,8,4736]{2,1,0:T(8,128)(2,1)S(1)} async-done(((bf16[16,8,4736]{2,1,0:T(8,128)(2,1)}), bf16[16,8,4736]{2,1,0:T(8,128)(2,1)S(1)}, u32[]{:S(2)}, u32[]{:S(2)}) %all-to-all-start) | async-done | bytes 1212448 | tf_op jit(solution)/shard_map/all_to_all | solution.py:75
  84.1 0.2 fusion.24
  84.3 0.2 fusion.11
  84.5 0.6 convolution_convert_fusion
  85.1 1.7 reshape.117
  86.8 4.0 %all-to-all-start.1 = ((bf16[4,42,4736]{2,1,0:T(8,128)(2,1)}), bf16[4,42,4736]{2,1,0:T(8,128)(2,1)S(1)}, u32[]{:S(2)}, u32[]{:S(2)}) async-start(bf16[4,42,4736]{2,1,0:T(8,128)(2,1)} %reshape.117), calls=%async_computation.1 | async-start | bytes 3637248 | tf_op jit(solution)/shard_map/all_to_all | solution.py:96
  90.8 23.4 %all-to-all-done.1 = bf16[4,42,4736]{2,1,0:T(8,128)(2,1)S(1)} async-done(((bf16[4,42,4736]{2,1,0:T(8,128)(2,1)}), bf16[4,42,4736]{2,1,0:T(8,128)(2,1)S(1)}, u32[]{:S(2)}, u32[]{:S(2)}) %all-to-all-start.1) | async-done | bytes 1591328 | tf_op jit(solution)/shard_map/all_to_all | solution.py:96
  114.2 0.5 reshape.118
  114.7 0.0 copy-start
  114.7 0.1 select_reduce_fusion
  114.8 5.8 %fusion.15 = (bf16[168,1024]{1,0:T(8,128)(2,1)}, bf16[168,1024]{1,0:T(8,128)(2,1)S(1)}, f32[168,1024]{1,0:T(8,128)S(1)}) fusion(f32[168]{0:T(256)S(1)} %select_reduce_fusion, bf16[1,3584,1024]{2,1,0:T(8,128)(2,1)} %param.11, bf16[168,4736]{1,0:T(8,128)(2,1)S(1)} %reshape.118), kind=kOutput, calls=%fused_computation.23 | convolution fusion | flops 1234501632 | bytes 9921536 | tf_op jit(solution)/shard_map/dot_general | solution.py:107
  120.6 0.4 fusion.14
  120.9 0.0 copy-start.1
  121.0 0.1 select_convert_fusion
  121.1 0.0 copy-start.2
  121.1 5.7 %fusion.6 = bf16[168,3584]{1,0:T(8,128)(2,1)S(1)} fusion(bf16[168,1024]{1,0:T(8,128)(2,1)S(1)} %get-tuple-element.12, bf16[1,3584,1024]{2,1,0:T(8,128)(2,1)} %param.11), kind=kOutput, calls=%fused_computation.9 | convolution fusion | flops 1233727488 | bytes 8888320 | tf_op jit(solution)/shard_map/dot_general | solution.py:112
  126.8 0.0 copy-done.1
  126.8 0.1 pad_maximum_fusion
  126.9 1.7 reshape.119
  128.6 3.6 %all-to-all-start.2 = ((bf16[4,42,4736]{2,1,0:T(8,128)(2,1)}), bf16[4,42,4736]{2,1,0:T(8,128)(2,1)S(1)}, u32[]{:S(2)}, u32[]{:S(2)}) async-start(bf16[4,42,4736]{2,1,0:T(8,128)(2,1)} %reshape.119), calls=%async_computation.2 | async-start | bytes 3637248 | tf_op jit(solution)/shard_map/all_to_all | solution.py:139
  132.2 0.0 all-gather.2.cloned.1.call-start
  132.2 0.7 all-gather.2.cloned.1.call-update
  132.9 22.3 %all-to-all-done.2 = bf16[4,42,4736]{2,1,0:T(8,128)(2,1)S(1)} async-done(((bf16[4,42,4736]{2,1,0:T(8,128)(2,1)}), bf16[4,42,4736]{2,1,0:T(8,128)(2,1)S(1)}, u32[]{:S(2)}, u32[]{:S(2)}) %all-to-all-start.2) | async-done | bytes 1591328 | tf_op jit(solution)/shard_map/all_to_all | solution.py:139
  155.2 1.6 reshape.120
  156.8 3.0 %fusion.4 = bf16[16,8,4736]{2,1,0:T(8,128)(2,1)} fusion(pred[168,128]{1,0:T(8,128)(4,1)S(1)} %fusion.11, bf16[168,4736]{1,0:T(8,128)(2,1)} %reshape.120), kind=kOutput, calls=%fused_computation.7 | convolution fusion | flops 204292096 | bytes 2825216 | tf_op jit(solution)/shard_map/dot_general | solution.py:142
  159.8 4.7 %all-to-all-start.3 = ((bf16[16,8,4736]{2,1,0:T(8,128)(2,1)}), bf16[16,8,4736]{2,1,0:T(8,128)(2,1)S(1)}, u32[]{:S(2)}, u32[]{:S(2)}) async-start(bf16[16,8,4736]{2,1,0:T(8,128)(2,1)} %fusion.4), calls=%async_computation.3 | async-start | bytes 2424832 | tf_op jit(solution)/shard_map/all_to_all | solution.py:145
  164.6 0.0 slice-start
  164.6 0.1 broadcast_in_dim.82
  164.7 1.2 slice-done
  165.9 1.5 constant_dynamic-slice_fusion
  167.3 1.9 collective-permute-start.2
  169.3 5.9 %collective-permute-start.3 = (bf16[168,448]{1,0:T(8,128)(2,1)}, bf16[168,448]{1,0:T(8,128)(2,1)S(1)}, u32[]{:S(2)}, u32[]{:S(2)}) collective-permute-start(bf16[168,448]{1,0:T(8,128)(2,1)} %get-tuple-element.19), channel_id=1, source_target_pairs={{0,256},{128,384},{256,512},{384,640},{512,768},{640,896},{768,0},... | collective-permute-start | bytes 451592 | tf_op jit(solution)/shard_map/ppermute | solution.py:131
  175.2 1.9 collective-permute-start.4
  177.2 6.3 %collective-permute-start.5 = (bf16[168,448]{1,0:T(8,128)(2,1)}, bf16[168,448]{1,0:T(8,128)(2,1)S(1)}, u32[]{:S(2)}, u32[]{:S(2)}) collective-permute-start(bf16[168,448]{1,0:T(8,128)(2,1)} %get-tuple-element.17), channel_id=1, source_target_pairs={{0,512},{128,640},{256,768},{384,896},{512,0},{640,128},{768,256},... | collective-permute-start | bytes 451592 | tf_op jit(solution)/shard_map/ppermute | solution.py:131
  183.4 3.8 %collective-permute-start.6 = (bf16[168,448]{1,0:T(8,128)(2,1)}, bf16[168,448]{1,0:T(8,128)(2,1)S(1)}, u32[]{:S(2)}, u32[]{:S(2)}) collective-permute-start(bf16[168,448]{1,0:T(8,128)(2,1)} %get-tuple-element.16), channel_id=1, source_target_pairs={{0,640},{128,768},{256,896},{384,0},{512,128},{640,256},{768,384},... | collective-permute-start | bytes 451592 | tf_op jit(solution)/shard_map/ppermute | solution.py:131
  187.3 0.0 collective-permute-done.2
  187.3 6.1 %collective-permute-start.7 = (bf16[168,448]{1,0:T(8,128)(2,1)S(1)}, bf16[168,448]{1,0:T(8,128)(2,1)S(1)}, u32[]{:S(2)}, u32[]{:S(2)}) collective-permute-start(bf16[168,448]{1,0:T(8,128)(2,1)S(1)} %get-tuple-element.15), channel_id=1, source_target_pairs={{0,768},{128,896},{256,0},{384,128},{512,256},{640,384},{768,512},... | collective-permute-start | bytes 451592 | tf_op jit(solution)/shard_map/ppermute | solution.py:131
  193.4 15.3 %collective-permute-done.3 = bf16[168,448]{1,0:T(8,128)(2,1)S(1)} collective-permute-done((bf16[168,448]{1,0:T(8,128)(2,1)}, bf16[168,448]{1,0:T(8,128)(2,1)S(1)}, u32[]{:S(2)}, u32[]{:S(2)}) %collective-permute-start.3) | collective-permute-done | bytes 150560 | tf_op jit(solution)/shard_map/ppermute | solution.py:131
  208.7 1.9 collective-permute-start.8
  210.7 10.6 %collective-permute-done.4 = bf16[168,448]{1,0:T(8,128)(2,1)S(1)} collective-permute-done((bf16[168,448]{1,0:T(8,128)(2,1)}, bf16[168,448]{1,0:T(8,128)(2,1)S(1)}, u32[]{:S(2)}, u32[]{:S(2)}) %collective-permute-start.4) | collective-permute-done | bytes 150560 | tf_op jit(solution)/shard_map/ppermute | solution.py:131
  221.3 0.2 collective-permute-done.5
  221.5 0.9 collective-permute-done.6
  222.4 0.0 all-to-all-done.3
  222.4 0.3 fusion.9
  222.7 26.8 %collective-permute-start.1 = (bf16[16,4736]{1,0:T(8,128)(2,1)S(1)}, bf16[16,4736]{1,0:T(8,128)(2,1)S(1)}, u32[]{:S(2)}, u32[]{:S(2)}) collective-permute-start(bf16[16,4736]{1,0:T(8,128)(2,1)S(1)} %slice.63), channel_id=1, source_target_pairs={{0,513},{128,641},{256,769},{384,897},{512,1},{640,129},{768,257},... | collective-permute-start | bytes 454664 | tf_op jit(solution)/shard_map/ppermute | solution.py:151
  249.6 0.0 collective-permute-done.7
  249.6 0.0 collective-permute-done.8
  249.6 20.3 %collective-permute-done.1 = bf16[16,4736]{1,0:T(8,128)(2,1)S(1)} collective-permute-done((bf16[16,4736]{1,0:T(8,128)(2,1)S(1)}, bf16[16,4736]{1,0:T(8,128)(2,1)S(1)}, u32[]{:S(2)}, u32[]{:S(2)}) %collective-permute-start.1) | collective-permute-done | bytes 151584 | tf_op jit(solution)/shard_map/ppermute | solution.py:151
  269.9 0.6 slice.49
  270.6 0.7 slice.50
  271.2 0.2 select_reduce_fusion.1
  271.4 0.7 copy.16
  272.0 4.6 %convolution_bitcast_fusion = f32[1,448,1024]{2,1,0:T(8,128)} fusion(bf16[1344,448]{1,0:T(8,128)(2,1)S(1)} %constant_dynamic-update-slice_fusion.6, bf16[1344,1024]{1,0:T(8,128)(2,1)} %all-gather.2.cloned.1.call-done), kind=kOutput, calls=%fused_computation.11 | convolution fusion | flops 1233125376 | bytes 5791744 | tf_op jit(solution)/shard_map/dot_general | solution.py:135
  (19 shorter events, 0.2 us)
Async XLA Ops:
  10.4 31.1 %collective-permute-start = (bf16[16,4736]{1,0:T(8,128)(2,1)S(1)}, bf16[16,4736]{1,0:T(8,128)(2,1)S(1)}, u32[]{:S(2)}, u32[]{:S(2)}) collective-permute-start(bf16[16,4736]{1,0:T(8,128)(2,1)S(1)} %pad_maximum_fusion.1), channel_id=1, source_target_pairs={{0,513},{128,641},{256,769},{384,897},{512,1},{640,129},{768,257},... | collective-permute-start | bytes 454664 | tf_op jit(solution)/shard_map/ppermute | solution.py:54
  44.2 39.9 %all-to-all-start = ((bf16[16,8,4736]{2,1,0:T(8,128)(2,1)}), bf16[16,8,4736]{2,1,0:T(8,128)(2,1)S(1)}, u32[]{:S(2)}, u32[]{:S(2)}) async-start(bf16[16,8,4736]{2,1,0:T(8,128)(2,1)} %fusion.5), calls=%async_computation | async-start | bytes 2424832 | tf_op jit(solution)/shard_map/all_to_all | solution.py:75
  86.8 27.4 %all-to-all-start.1 = ((bf16[4,42,4736]{2,1,0:T(8,128)(2,1)}), bf16[4,42,4736]{2,1,0:T(8,128)(2,1)S(1)}, u32[]{:S(2)}, u32[]{:S(2)}) async-start(bf16[4,42,4736]{2,1,0:T(8,128)(2,1)} %reshape.117), calls=%async_computation.1 | async-start | bytes 3637248 | tf_op jit(solution)/shard_map/all_to_all | solution.py:96
  114.7 49.9 %copy-start = (bf16[168,4736]{1,0:T(8,128)(2,1)}, bf16[168,4736]{1,0:T(8,128)(2,1)S(1)}, u32[]{:S(2)}) copy-start(bf16[168,4736]{1,0:T(8,128)(2,1)S(1)} %reshape.118) | copy-start | bytes 4773892
  120.9 5.8 %copy-start.1 = (bf16[168,1024]{1,0:T(8,128)(2,1)}, bf16[168,1024]{1,0:T(8,128)(2,1)S(1)}, u32[]{:S(2)}) copy-start(bf16[168,1024]{1,0:T(8,128)(2,1)S(1)} %get-tuple-element.12) | copy-start | bytes 1032196
  121.1 5.7 %copy-start.2 = (bf16[168,1024]{1,0:T(8,128)(2,1)S(1)}, bf16[168,1024]{1,0:T(8,128)(2,1)}, u32[]{:S(2)}) copy-start(bf16[168,1024]{1,0:T(8,128)(2,1)} %get-tuple-element.10) | copy-start | bytes 1032196
  128.6 26.6 %all-to-all-start.2 = ((bf16[4,42,4736]{2,1,0:T(8,128)(2,1)}), bf16[4,42,4736]{2,1,0:T(8,128)(2,1)S(1)}, u32[]{:S(2)}, u32[]{:S(2)}) async-start(bf16[4,42,4736]{2,1,0:T(8,128)(2,1)} %reshape.119), calls=%async_computation.2 | async-start | bytes 3637248 | tf_op jit(solution)/shard_map/all_to_all | solution.py:139
  132.2 139.8 %all-gather.2.cloned.1.call-start = ((), (), s32[]{:S(2)}) async-start(), calls=%async_computation.4 | async-start | bytes 3096576 | tf_op jit(solution)/shard_map/all_gather | solution.py:126
  159.8 62.5 %all-to-all-start.3 = ((bf16[16,8,4736]{2,1,0:T(8,128)(2,1)}), bf16[16,8,4736]{2,1,0:T(8,128)(2,1)S(1)}, u32[]{:S(2)}, u32[]{:S(2)}) async-start(bf16[16,8,4736]{2,1,0:T(8,128)(2,1)} %fusion.4), calls=%async_computation.3 | async-start | bytes 2424832 | tf_op jit(solution)/shard_map/all_to_all | solution.py:145
  164.6 1.3 slice-start
  167.3 19.9 %collective-permute-start.2 = (bf16[168,448]{1,0:T(8,128)(2,1)S(1)}, bf16[168,448]{1,0:T(8,128)(2,1)S(1)}, u32[]{:S(2)}, u32[]{:S(2)}) collective-permute-start(bf16[168,448]{1,0:T(8,128)(2,1)S(1)} %get-tuple-element.20), channel_id=1, source_target_pairs={{0,128},{128,256},{256,384},{384,512},{512,640},{640,768},{768,896... | collective-permute-start | bytes 451592 | tf_op jit(solution)/shard_map/ppermute | solution.py:131
  169.3 39.5 %collective-permute-start.3 = (bf16[168,448]{1,0:T(8,128)(2,1)}, bf16[168,448]{1,0:T(8,128)(2,1)S(1)}, u32[]{:S(2)}, u32[]{:S(2)}) collective-permute-start(bf16[168,448]{1,0:T(8,128)(2,1)} %get-tuple-element.19), channel_id=1, source_target_pairs={{0,256},{128,384},{256,512},{384,640},{512,768},{640,896},{768,0},... | collective-permute-start | bytes 451592 | tf_op jit(solution)/shard_map/ppermute | solution.py:131
  175.2 46.0 %collective-permute-start.4 = (bf16[168,448]{1,0:T(8,128)(2,1)}, bf16[168,448]{1,0:T(8,128)(2,1)S(1)}, u32[]{:S(2)}, u32[]{:S(2)}) collective-permute-start(bf16[168,448]{1,0:T(8,128)(2,1)} %get-tuple-element.18), channel_id=1, source_target_pairs={{0,384},{128,512},{256,640},{384,768},{512,896},{640,0},{768,128},... | collective-permute-start | bytes 451592 | tf_op jit(solution)/shard_map/ppermute | solution.py:131
  177.2 44.3 %collective-permute-start.5 = (bf16[168,448]{1,0:T(8,128)(2,1)}, bf16[168,448]{1,0:T(8,128)(2,1)S(1)}, u32[]{:S(2)}, u32[]{:S(2)}) collective-permute-start(bf16[168,448]{1,0:T(8,128)(2,1)} %get-tuple-element.17), channel_id=1, source_target_pairs={{0,512},{128,640},{256,768},{384,896},{512,0},{640,128},{768,256},... | collective-permute-start | bytes 451592 | tf_op jit(solution)/shard_map/ppermute | solution.py:131
  183.4 38.9 %collective-permute-start.6 = (bf16[168,448]{1,0:T(8,128)(2,1)}, bf16[168,448]{1,0:T(8,128)(2,1)S(1)}, u32[]{:S(2)}, u32[]{:S(2)}) collective-permute-start(bf16[168,448]{1,0:T(8,128)(2,1)} %get-tuple-element.16), channel_id=1, source_target_pairs={{0,640},{128,768},{256,896},{384,0},{512,128},{640,256},{768,384},... | collective-permute-start | bytes 451592 | tf_op jit(solution)/shard_map/ppermute | solution.py:131
  187.3 62.3 %collective-permute-start.7 = (bf16[168,448]{1,0:T(8,128)(2,1)S(1)}, bf16[168,448]{1,0:T(8,128)(2,1)S(1)}, u32[]{:S(2)}, u32[]{:S(2)}) collective-permute-start(bf16[168,448]{1,0:T(8,128)(2,1)S(1)} %get-tuple-element.15), channel_id=1, source_target_pairs={{0,768},{128,896},{256,0},{384,128},{512,256},{640,384},{768,512},... | collective-permute-start | bytes 451592 | tf_op jit(solution)/shard_map/ppermute | solution.py:131
  208.7 40.9 %collective-permute-start.8 = (bf16[168,448]{1,0:T(8,128)(2,1)S(1)}, bf16[168,448]{1,0:T(8,128)(2,1)S(1)}, u32[]{:S(2)}, u32[]{:S(2)}) collective-permute-start(bf16[168,448]{1,0:T(8,128)(2,1)S(1)} %get-tuple-element.14), channel_id=1, source_target_pairs={{0,896},{128,0},{256,128},{384,256},{512,384},{640,512},{768,640},... | collective-permute-start | bytes 451592 | tf_op jit(solution)/shard_map/ppermute | solution.py:131
  222.7 47.2 %collective-permute-start.1 = (bf16[16,4736]{1,0:T(8,128)(2,1)S(1)}, bf16[16,4736]{1,0:T(8,128)(2,1)S(1)}, u32[]{:S(2)}, u32[]{:S(2)}) collective-permute-start(bf16[16,4736]{1,0:T(8,128)(2,1)S(1)} %slice.63), channel_id=1, source_target_pairs={{0,513},{128,641},{256,769},{384,897},{512,1},{640,129},{768,257},... | collective-permute-start | bytes 454664 | tf_op jit(solution)/shard_map/ppermute | solution.py:151
Sparse Core Ops, SparseCore 0:
  135.7 107.8 all-gather.1

commit v2 on v1

--- a/solution.py
+++ b/solution.py
@@ -15,6 +15,10 @@
         other %= ring
         pairs.append(((z % reps) * 2 + z // reps, (other % reps) * 2 + other // reps))
     return pairs
+
+
+def ring(size, step):
+    return [(i, (i + step) % size) for i in range(size)]
 
 
 def on_device(activations, cotangent, gates, experts, groups, weights):
@@ -77,25 +81,44 @@
     ).reshape(places, wide)
 
     cap2 = 2 * cap
+    before = (place_index[:, None] < place_index[None, :]).astype(bf)
+    slot_at = jnp.arange(cap2, dtype=jnp.int32).astype(f32)
+
+    def pickers(named_here):
+        result = []
+        for j in range(xs):
+            mine_local = jnp.arange(named_here.shape[-1]) == (x_at + j) % xs * 2 + half_at
+            live = jnp.sum(jnp.where(mine_local, named_here, 0.0), axis=-1)
+            rank = jnp.dot(live.astype(bf), before, preferred_element_type=f32)
+            result.append(
+                ((live[..., None, :] > 0) & (rank[..., None, :] == slot_at[:, None])).astype(bf)
+            )
+        return result
+
+    group_gates = lax.dynamic_slice_in_dim(rows, width + hidden + node_at * locals_, locals_, 1)
+    picker = pickers((group_gates != 0).astype(f32))
+    sent = [jnp.dot(p, rows, preferred_element_type=f32).astype(bf) for p in picker]
+    inside = jnp.concatenate(
+        [sent[0]] + [lax.ppermute(sent[j], "x", ring(xs, j)) for j in range(1, xs)], axis=0
+    )
     taken = xs * cap2
-    slot_index = jnp.arange(taken, dtype=jnp.int32)
-    slot_expert = (
-        (node_at * locals_ + (slot_index // cap2) * 2 + half_at)[:, None]
-        == jnp.arange(total, dtype=jnp.int32)[None, :]
-    ).astype(bf)
-    named_rows = (rows[:, width + hidden :] != 0).astype(bf)
-    live = lax.dot_general(
-        slot_expert, named_rows, (((1,), (1,)), ((), ())), preferred_element_type=f32
-    )
-    before = (place_index[:, None] < place_index[None, :]).astype(bf)
-    rank = jnp.dot(live.astype(bf), before, preferred_element_type=f32)
-    picker = (
-        (live > 0) & (rank == (slot_index % cap2).astype(f32)[:, None])
-    ).astype(bf)
-    send_slots = jnp.dot(picker, rows, preferred_element_type=f32).astype(bf)
-    inside = lax.all_to_all(
-        send_slots.reshape(xs, cap2, wide), "x", 0, 0, tiled=True
-    ).reshape(taken, wide)
+
+    share = width // reps
+    spare = -(share + locals_) % 128
+    cols = jnp.stack(
+        [
+            jnp.concatenate(
+                [
+                    rows[:, k * share : (k + 1) * share],
+                    group_gates,
+                    jnp.zeros((places, spare), bf),
+                ],
+                axis=1,
+            )
+            for k in range(reps)
+        ]
+    )
+    cols = lax.all_to_all(cols, "rep", 0, 0, tiled=True)
 
     exp_x = inside[:, :width]
     exp_dy = inside[:, width : width + hidden].astype(f32)
@@ -122,29 +145,41 @@
         axis=1,
     )
 
-    share = width // reps
     gathered = lax.all_gather(grad_pre, "rep", axis=0, tiled=True)
-    x_cols = jnp.zeros((reps * taken, share), bf)
-    for k in range(reps):
-        piece = lax.dynamic_slice_in_dim(exp_x, (rep_at + k) % reps * share, share, 1)
-        if k:
-            piece = lax.ppermute(piece, "rep", [(i, (i + k) % reps) for i in range(reps)])
-        x_cols = lax.dynamic_update_slice_in_dim(
-            x_cols, piece, (rep_at + reps - k) % reps * taken, 0
-        )
-    grad_share = lax.dot_general(
-        x_cols, gathered, (((0,), (0,)), ((), ())), preferred_element_type=f32
-    )
-
-    back_slots = lax.all_to_all(
-        back.reshape(xs, cap2, wide), "x", 0, 0, tiled=True
-    ).reshape(taken, wide)
+
+    back_slots = jnp.concatenate(
+        [back[:cap2]]
+        + [
+            lax.ppermute(back[j * cap2 : (j + 1) * cap2], "x", ring(xs, -j))
+            for j in range(1, xs)
+        ],
+        axis=0,
+    )
     back_rows = lax.dot_general(
-        picker, back_slots, (((0,), (0,)), ((), ())), preferred_element_type=f32
-    ).astype(bf)
+        jnp.concatenate(picker, axis=0),
+        back_slots,
+        (((0,), (0,)), ((), ())),
+        preferred_element_type=f32,
+    ).astype(bf)
+    back_rows, cols = lax.optimization_barrier((back_rows, cols))
     home_rows = lax.all_to_all(
         back_rows.reshape(nodes, 2 * blocks, wide), "node", 0, 0, tiled=True
     ).reshape(places, wide)
+
+    share_sent = [
+        jnp.einsum(
+            "pcr,prd->pcd", p, cols[:, :, :share], preferred_element_type=f32
+        ).astype(bf)
+        for p in pickers((cols[:, :, share : share + locals_] != 0).astype(f32))
+    ]
+    share_rows = [share_sent[0]] + [
+        lax.ppermute(share_sent[j], "x", ring(xs, j)) for j in range(1, xs)
+    ]
+    home_rows, share_rows = lax.optimization_barrier((home_rows, share_rows))
+    x_cols = jnp.stack(share_rows, axis=1).reshape(reps * taken, share)
+    grad_share = lax.dot_general(
+        x_cols, gathered, (((0,), (0,)), ((), ())), preferred_element_type=f32
+    )
     home = lax.dot_general(
         placing, home_rows, (((0,), (0,)), ((), ())), preferred_element_type=f32
     )

time: 288 us -> 243 us (0.84)
  the two profiles are of different devices: /device:TPU:1 before, /device:TPU:131 now
where the time goes in v2:
time: 243 us; the launch traced here: 242 us
  waiting for transfers between devices  107 us (44%)
  starting transfers between devices  75.7 us (31%)
  matrix products  26.8 us (11%)
  between operations  14.3 us (6%)
  other arithmetic  11.8 us (5%)
  local copies, waits for them, and re-layouts  6.39 us (3%)
    all_to_all x1, waiting for transfers between devices, on_device(): lax.all_to_all(send_rows.reshape(nodes, 2 * blocks, wide), 'node', 0, 0,...  31.1 us
    all_to_all x1, waiting for transfers between devices, on_device(): cols = lax.all_to_all(cols, 'rep', 0, 0, tiled=True)  25 us
    ppermute x3, waiting for transfers between devices, on_device(): lax.ppermute(back[j * cap2:(j + 1) * cap2], 'x', ring(xs, -j))  18.7 us
    ppermute x1, starting transfers between devices, on_device(): other = lax.ppermute(own, ('rep', 'half'), pairs)  16.1 us
    ppermute x3, waiting for transfers between devices, on_device(): lax.ppermute(share_sent[j], 'x', ring(xs, j))  14.4 us
    ppermute x1, waiting for transfers between devices, on_device(): other = lax.ppermute(own, ('rep', 'half'), pairs)  10.9 us
    ppermute x1, starting transfers between devices, on_device(): returned = lax.ppermute(home[tokens:].astype(bf), ('rep', 'half'), pairs)  10.8 us
    ppermute x3, starting transfers between devices, on_device(): lax.ppermute(back[j * cap2:(j + 1) * cap2], 'x', ring(xs, -j))  10.2 us
  transfers between devices with their start and end apart: 15, of which 12 were waited for; matrix products, arithmetic and copies ran while one was open for 15% of the time, Pallas kernels for 0%

profile of v2, /device:TPU:131, one launch (start us, length us, event | category | flops | bytes accessed | tf_op | source)
XLA Modules:
  0.0 241.7 jit_solution(4436199606432545214)
XLA Ops:
  7.2 0.8 copy.26
  7.9 0.7 broadcast_multiply_fusion
  8.6 0.7 add.92
  9.5 0.9 pad_maximum_fusion.17
  10.4 16.1 %collective-permute-start = (bf16[16,4736]{1,0:T(8,128)(2,1)S(1)}, bf16[16,4736]{1,0:T(8,128)(2,1)S(1)}, u32[]{:S(2)}, u32[]{:S(2)}) collective-permute-start(bf16[16,4736]{1,0:T(8,128)(2,1)S(1)} %pad_maximum_fusion.17), channel_id=1, source_target_pairs={{0,513},{128,641},{256,769},{384,897},{512,1},{640,129},{768,257},... | collective-permute-start | bytes 454664 | tf_op jit(solution)/shard_map/ppermute | solution.py:58
  26.6 10.9 %collective-permute-done = bf16[16,4736]{1,0:T(8,128)(2,1)S(1)} collective-permute-done((bf16[16,4736]{1,0:T(8,128)(2,1)S(1)}, bf16[16,4736]{1,0:T(8,128)(2,1)S(1)}, u32[]{:S(2)}, u32[]{:S(2)}) %collective-permute-start) | collective-permute-done | bytes 151584 | tf_op jit(solution)/shard_map/ppermute | solution.py:58
  37.5 0.2 fusion.16
  37.7 2.5 %fusion.4 = bf16[16,8,4736]{2,1,0:T(8,128)(2,1)} fusion(pred[128,32]{0,1:T(32,128)(4,1)S(1)} %fusion.16, bf16[16,4736]{1,0:T(8,128)(2,1)S(1)} %collective-permute-done, bf16[16,128]{1,0:T(8,128)(2,1)S(1)} %select_reduce_fusion.2, bf16[16,1024]{1,0:T(8,128)(2,1)} %param.7, bf16[16,3584]{1,0:T(8,128)(2,1)} %param.6), kind=kOutput, calls=%fused_computation.6 | convolution fusion | flops 40615936 | bytes 1519616 | tf_op jit(solution)/shard_map/dot_general | solution.py:78
  40.2 7.6 %all-to-all-start = ((bf16[16,8,4736]{2,1,0:T(8,128)(2,1)}), bf16[16,8,4736]{2,1,0:T(8,128)(2,1)S(1)}, u32[]{:S(2)}, u32[]{:S(2)}) async-start(bf16[16,8,4736]{2,1,0:T(8,128)(2,1)} %fusion.4), calls=%async_computation | async-start | bytes 2424832 | tf_op jit(solution)/shard_map/all_to_all | solution.py:79
  47.9 31.1 %all-to-all-done = bf16[16,8,4736]{2,1,0:T(8,128)(2,1)S(1)} async-done(((bf16[16,8,4736]{2,1,0:T(8,128)(2,1)}), bf16[16,8,4736]{2,1,0:T(8,128)(2,1)S(1)}, u32[]{:S(2)}, u32[]{:S(2)}) %all-to-all-start) | async-done | bytes 1212448 | tf_op jit(solution)/shard_map/all_to_all | solution.py:79
  79.7 0.3 fusion.131
  80.0 0.4 convolution_convert_fusion.2
  80.4 2.2 collective-permute-start.3
  82.5 0.4 convolution_convert_fusion.3
  82.9 4.0 %collective-permute-start.2 = (bf16[42,4736]{1,0:T(8,128)(2,1)S(1)}, bf16[42,4736]{1,0:T(8,128)(2,1)}, u32[]{:S(2)}, u32[]{:S(2)}) collective-permute-start(bf16[42,4736]{1,0:T(8,128)(2,1)S(1)} %convolution_convert_fusion.3), channel_id=1, source_target_pairs={{0,4},{2,6},{4,0},{6,2},{1,5},{3,7},{5,1},{7,3},{8,12},{10,14},{12... | collective-permute-start | bytes 1193480 | tf_op jit(solution)/shard_map/ppermute | solution.py:102
  87.0 1.1 convolution_convert_fusion.4
  88.1 3.4 %collective-permute-start.1 = (bf16[42,4736]{1,0:T(8,128)(2,1)}, bf16[42,4736]{1,0:T(8,128)(2,1)}, u32[]{:S(2)}, u32[]{:S(2)}) collective-permute-start(bf16[42,4736]{1,0:T(8,128)(2,1)} %convolution_convert_fusion.4), channel_id=1, source_target_pairs={{0,2},{2,4},{4,6},{6,0},{1,3},{3,5},{5,7},{7,1},{8,10},{10,12},{12... | collective-permute-start | bytes 1193480 | tf_op jit(solution)/shard_map/ppermute | solution.py:102
  91.7 0.1 copy.40
  92.7 0.8 fusion.42
  93.5 0.8 fusion.45
  94.2 0.8 fusion.48
  95.0 0.8 fusion.51
  95.8 0.8 fusion.54
  96.6 0.8 fusion.57
  97.4 0.8 fusion.60
  98.2 0.8 fusion.63
  98.9 8.1 %all-to-all-start.1 = ((bf16[8,128,512]{1,2,0:T(8,128)(2,1)}), bf16[8,128,512]{1,2,0:T(8,128)(2,1)S(1)}, u32[]{:S(2)}, u32[]{:S(2)}) async-start(bf16[8,128,512]{1,2,0:T(8,128)(2,1)} %fusion.63), calls=%async_computation.1 | async-start | bytes 2097152 | tf_op jit(solution)/shard_map/all_to_all | solution.py:121
  107.2 0.4 convolution_convert_fusion.5
  107.6 0.6 collective-permute-done.1
  108.2 0.9 select_reduce_fusion
  109.1 5.9 %fusion.18 = (bf16[168,1024]{1,0:T(8,128)(2,1)}, bf16[168,1024]{1,0:T(8,128)(2,1)S(1)}, bf16[168,1024]{1,0:T(8,128)(2,1)S(1)}, bf16[168,1024]{1,0:T(8,128)(2,1)S(1)}) fusion(f32[168]{0:T(256)S(1)} %select_reduce_fusion, bf16[42,4736]{1,0:T(8,128)(2,1)} %collective-permute-done.3, bf16[42,4736]{1,0:T(8,128)(2,1)} %collective-permute-done.2, ...), kind=kOutput, calls=%fused_computation.40 | convolution fusion | flops 1242071040 | bytes 10308256 | tf_op jit(solution)/shard_map/dot_general | solution.py:130
  115.0 0.2 fusion.20
  115.3 5.8 %fusion.5 = bf16[168,3584]{1,0:T(8,128)(2,1)S(1)} fusion(bf16[168,1024]{1,0:T(8,128)(2,1)} %get-tuple-element.32, bf16[1,3584,1024]{2,1,0:T(8,128)(2,1)} %param.11), kind=kOutput, calls=%fused_computation.11 | convolution fusion | flops 1233727488 | bytes 8888320 | tf_op jit(solution)/shard_map/dot_general | solution.py:135
  121.2 0.3 fusion.130
  121.5 3.3 %collective-permute-start.6 = (bf16[42,4736]{1,0:T(8,128)(2,1)S(1)}, bf16[42,4736]{1,0:T(8,128)(2,1)S(1)}, u32[]{:S(2)}, u32[]{:S(2)}) collective-permute-start(bf16[42,4736]{1,0:T(8,128)(2,1)S(1)} %get-tuple-element.37), channel_id=1, source_target_pairs={{0,2},{2,4},{4,6},{6,0},{1,3},{3,5},{5,7},{7,1},{8,10},{10,12},{12... | collective-permute-start | bytes 1193480 | tf_op jit(solution)/shard_map/ppermute | solution.py:153
  124.8 5.0 %collective-permute-start.5 = (bf16[42,4736]{1,0:T(8,128)(2,1)S(1)}, bf16[42,4736]{1,0:T(8,128)(2,1)S(1)}, u32[]{:S(2)}, u32[]{:S(2)}) collective-permute-start(bf16[42,4736]{1,0:T(8,128)(2,1)S(1)} %get-tuple-element.38), channel_id=1, source_target_pairs={{0,4},{2,6},{4,0},{6,2},{1,5},{3,7},{5,1},{7,3},{8,12},{10,14},{12... | collective-permute-start | bytes 1193480 | tf_op jit(solution)/shard_map/ppermute | solution.py:153
  129.7 1.9 collective-permute-start.4
  131.8 4.8 %collective-permute-done.6 = bf16[42,4736]{1,0:T(8,128)(2,1)S(1)} collective-permute-done((bf16[42,4736]{1,0:T(8,128)(2,1)S(1)}, bf16[42,4736]{1,0:T(8,128)(2,1)S(1)}, u32[]{:S(2)}, u32[]{:S(2)}) %collective-permute-start.6) | collective-permute-done | bytes 397856 | tf_op jit(solution)/shard_map/ppermute | solution.py:153
  136.6 3.1 %collective-permute-done.5 = bf16[42,4736]{1,0:T(8,128)(2,1)S(1)} collective-permute-done((bf16[42,4736]{1,0:T(8,128)(2,1)S(1)}, bf16[42,4736]{1,0:T(8,128)(2,1)S(1)}, u32[]{:S(2)}, u32[]{:S(2)}) %collective-permute-start.5) | collective-permute-done | bytes 397856 | tf_op jit(solution)/shard_map/ppermute | solution.py:153
  139.7 10.7 %collective-permute-done.4 = bf16[42,4736]{1,0:T(8,128)(2,1)S(1)} collective-permute-done((bf16[42,4736]{1,0:T(8,128)(2,1)S(1)}, bf16[42,4736]{1,0:T(8,128)(2,1)S(1)}, u32[]{:S(2)}, u32[]{:S(2)}) %collective-permute-start.4) | collective-permute-done | bytes 397856 | tf_op jit(solution)/shard_map/ppermute | solution.py:153
  150.5 1.8 convolution_convert_fusion
  152.2 25.0 %all-to-all-done.1 = bf16[8,128,512]{1,2,0:T(8,128)(2,1)S(1)} async-done(((bf16[8,128,512]{1,2,0:T(8,128)(2,1)}), bf16[8,128,512]{1,2,0:T(8,128)(2,1)S(1)}, u32[]{:S(2)}, u32[]{:S(2)}) %all-to-all-start.1) | async-done | bytes 1048608 | tf_op jit(solution)/shard_map/all_to_all | solution.py:121
  177.2 4.1 %all-to-all-start.2 = ((bf16[16,8,4736]{2,1,0:T(8,128)(2,1)}), bf16[16,8,4736]{2,1,0:T(8,128)(2,1)S(1)}, u32[]{:S(2)}, u32[]{:S(2)}) async-start(bf16[16,8,4736]{2,1,0:T(8,128)(2,1)} %bitcast.20), calls=%async_computation.2 | async-start | bytes 2424832 | tf_op jit(solution)/shard_map/all_to_all | solution.py:165
  181.6 0.5 convolution_convert_fusion.8
  182.1 1.9 collective-permute-start.7
  184.2 0.5 convolution_convert_fusion.7
  184.7 3.6 %collective-permute-start.8 = (bf16[8,42,448]{2,1,0:T(8,128)(2,1)S(1)}, bf16[8,42,448]{2,1,0:T(8,128)(2,1)S(1)}, u32[]{:S(2)}, u32[]{:S(2)}) collective-permute-start(bf16[8,42,448]{2,1,0:T(8,128)(2,1)S(1)} %convolution_convert_fusion.7), channel_id=1, source_target_pairs={{0,4},{2,6},{4,0},{6,2},{1,5},{3,7},{5,1},{7,3},{8,12},{10,14},{12... | collective-permute-start | bytes 903176 | tf_op jit(solution)/shard_map/ppermute | solution.py:176
  188.5 0.5 convolution_convert_fusion.6
  189.0 3.6 %collective-permute-start.9 = (bf16[8,42,448]{2,1,0:T(8,128)(2,1)S(1)}, bf16[8,42,448]{2,1,0:T(8,128)(2,1)}, u32[]{:S(2)}, u32[]{:S(2)}) collective-permute-start(bf16[8,42,448]{2,1,0:T(8,128)(2,1)S(1)} %convolution_convert_fusion.6), channel_id=1, source_target_pairs={{0,6},{2,0},{4,2},{6,4},{1,7},{3,1},{5,3},{7,5},{8,14},{10,8},{12,... | collective-permute-start | bytes 903176 | tf_op jit(solution)/shard_map/ppermute | solution.py:176
  192.7 0.5 convolution_convert_fusion.9
  193.2 1.4 collective-permute-done.7
  194.6 3.9 %collective-permute-done.8 = bf16[8,42,448]{2,1,0:T(8,128)(2,1)S(1)} collective-permute-done((bf16[8,42,448]{2,1,0:T(8,128)(2,1)S(1)}, bf16[8,42,448]{2,1,0:T(8,128)(2,1)S(1)}, u32[]{:S(2)}, u32[]{:S(2)}) %collective-permute-start.8) | collective-permute-done | bytes 301088 | tf_op jit(solution)/shard_map/ppermute | solution.py:176
  198.5 9.1 %collective-permute-done.9 = bf16[8,42,448]{2,1,0:T(8,128)(2,1)} collective-permute-done((bf16[8,42,448]{2,1,0:T(8,128)(2,1)S(1)}, bf16[8,42,448]{2,1,0:T(8,128)(2,1)}, u32[]{:S(2)}, u32[]{:S(2)}) %collective-permute-start.9) | collective-permute-done | bytes 301088 | tf_op jit(solution)/shard_map/ppermute | solution.py:176
  207.6 4.9 %all-to-all-done.2 = bf16[16,8,4736]{2,1,0:T(8,128)(2,1)S(1)} async-done(((bf16[16,8,4736]{2,1,0:T(8,128)(2,1)}), bf16[16,8,4736]{2,1,0:T(8,128)(2,1)S(1)}, u32[]{:S(2)}, u32[]{:S(2)}) %all-to-all-start.2) | async-done | bytes 1212448 | tf_op jit(solution)/shard_map/all_to_all | solution.py:165
  212.6 0.3 fusion.132
  212.9 10.8 %collective-permute-start.10 = (bf16[16,4736]{1,0:T(8,128)(2,1)S(1)}, bf16[16,4736]{1,0:T(8,128)(2,1)S(1)}, u32[]{:S(2)}, u32[]{:S(2)}) collective-permute-start(bf16[16,4736]{1,0:T(8,128)(2,1)S(1)} %slice.126), channel_id=1, source_target_pairs={{0,513},{128,641},{256,769},{384,897},{512,1},{640,129},{768,257},... | collective-permute-start | bytes 454664 | tf_op jit(solution)/shard_map/ppermute | solution.py:186
  223.7 1.3 pad_maximum_fusion.1
  225.1 1.5 reshape.135
  226.7 5.0 %convolution_bitcast_fusion = f32[1,448,1024]{2,1,0:T(8,128)} fusion(bf16[1344,448]{1,0:T(8,128)(2,1)} %reshape.135, bf16[1344,1024]{1,0:T(8,128)(2,1)} %all-gather.2.cloned.1.call-done), kind=kOutput, calls=%fused_computation.21 | convolution fusion | flops 1233125376 | bytes 5791744 | tf_op jit(solution)/shard_map/dot_general | solution.py:180
  231.7 1.0 collective-permute-done.10
  232.7 0.6 slice.112
  233.3 0.7 slice.113
  234.0 0.2 select_reduce_fusion.1
  234.2 0.7 copy.37
  (50 shorter events, 3.2 us)
Async XLA Ops:
  10.4 27.0 %collective-permute-start = (bf16[16,4736]{1,0:T(8,128)(2,1)S(1)}, bf16[16,4736]{1,0:T(8,128)(2,1)S(1)}, u32[]{:S(2)}, u32[]{:S(2)}) collective-permute-start(bf16[16,4736]{1,0:T(8,128)(2,1)S(1)} %pad_maximum_fusion.17), channel_id=1, source_target_pairs={{0,513},{128,641},{256,769},{384,897},{512,1},{640,129},{768,257},... | collective-permute-start | bytes 454664 | tf_op jit(solution)/shard_map/ppermute | solution.py:58
  40.2 38.9 %all-to-all-start = ((bf16[16,8,4736]{2,1,0:T(8,128)(2,1)}), bf16[16,8,4736]{2,1,0:T(8,128)(2,1)S(1)}, u32[]{:S(2)}, u32[]{:S(2)}) async-start(bf16[16,8,4736]{2,1,0:T(8,128)(2,1)} %fusion.4), calls=%async_computation | async-start | bytes 2424832 | tf_op jit(solution)/shard_map/all_to_all | solution.py:79
  80.4 27.2 %collective-permute-start.3 = (bf16[42,4736]{1,0:T(8,128)(2,1)S(1)}, bf16[42,4736]{1,0:T(8,128)(2,1)}, u32[]{:S(2)}, u32[]{:S(2)}) collective-permute-start(bf16[42,4736]{1,0:T(8,128)(2,1)S(1)} %convolution_convert_fusion.2), channel_id=1, source_target_pairs={{0,6},{2,0},{4,2},{6,4},{1,7},{3,1},{5,3},{7,5},{8,14},{10,8},{12,... | collective-permute-start | bytes 1193480 | tf_op jit(solution)/shard_map/ppermute | solution.py:102
  82.9 24.6 %collective-permute-start.2 = (bf16[42,4736]{1,0:T(8,128)(2,1)S(1)}, bf16[42,4736]{1,0:T(8,128)(2,1)}, u32[]{:S(2)}, u32[]{:S(2)}) collective-permute-start(bf16[42,4736]{1,0:T(8,128)(2,1)S(1)} %convolution_convert_fusion.3), channel_id=1, source_target_pairs={{0,4},{2,6},{4,0},{6,2},{1,5},{3,7},{5,1},{7,3},{8,12},{10,14},{12... | collective-permute-start | bytes 1193480 | tf_op jit(solution)/shard_map/ppermute | solution.py:102
  88.1 20.1 %collective-permute-start.1 = (bf16[42,4736]{1,0:T(8,128)(2,1)}, bf16[42,4736]{1,0:T(8,128)(2,1)}, u32[]{:S(2)}, u32[]{:S(2)}) collective-permute-start(bf16[42,4736]{1,0:T(8,128)(2,1)} %convolution_convert_fusion.4), channel_id=1, source_target_pairs={{0,2},{2,4},{4,6},{6,0},{1,3},{3,5},{5,7},{7,1},{8,10},{10,12},{12... | collective-permute-start | bytes 1193480 | tf_op jit(solution)/shard_map/ppermute | solution.py:102
  98.9 78.3 %all-to-all-start.1 = ((bf16[8,128,512]{1,2,0:T(8,128)(2,1)}), bf16[8,128,512]{1,2,0:T(8,128)(2,1)S(1)}, u32[]{:S(2)}, u32[]{:S(2)}) async-start(bf16[8,128,512]{1,2,0:T(8,128)(2,1)} %fusion.63), calls=%async_computation.1 | async-start | bytes 2097152 | tf_op jit(solution)/shard_map/all_to_all | solution.py:121
  107.0 119.6 %all-gather.2.cloned.1.call-start = ((), (), s32[]{:S(2)}) async-start(), calls=%async_computation.3 | async-start | bytes 3096576 | tf_op jit(solution)/shard_map/all_gather | solution.py:148
  121.5 15.1 %collective-permute-start.6 = (bf16[42,4736]{1,0:T(8,128)(2,1)S(1)}, bf16[42,4736]{1,0:T(8,128)(2,1)S(1)}, u32[]{:S(2)}, u32[]{:S(2)}) collective-permute-start(bf16[42,4736]{1,0:T(8,128)(2,1)S(1)} %get-tuple-element.37), channel_id=1, source_target_pairs={{0,2},{2,4},{4,6},{6,0},{1,3},{3,5},{5,7},{7,1},{8,10},{10,12},{12... | collective-permute-start | bytes 1193480 | tf_op jit(solution)/shard_map/ppermute | solution.py:153
  124.8 15.0 %collective-permute-start.5 = (bf16[42,4736]{1,0:T(8,128)(2,1)S(1)}, bf16[42,4736]{1,0:T(8,128)(2,1)S(1)}, u32[]{:S(2)}, u32[]{:S(2)}) collective-permute-start(bf16[42,4736]{1,0:T(8,128)(2,1)S(1)} %get-tuple-element.38), channel_id=1, source_target_pairs={{0,4},{2,6},{4,0},{6,2},{1,5},{3,7},{5,1},{7,3},{8,12},{10,14},{12... | collective-permute-start | bytes 1193480 | tf_op jit(solution)/shard_map/ppermute | solution.py:153
  129.7 20.7 %collective-permute-start.4 = (bf16[42,4736]{1,0:T(8,128)(2,1)S(1)}, bf16[42,4736]{1,0:T(8,128)(2,1)S(1)}, u32[]{:S(2)}, u32[]{:S(2)}) collective-permute-start(bf16[42,4736]{1,0:T(8,128)(2,1)S(1)} %get-tuple-element.39), channel_id=1, source_target_pairs={{0,6},{2,0},{4,2},{6,4},{1,7},{3,1},{5,3},{7,5},{8,14},{10,8},{12,... | collective-permute-start | bytes 1193480 | tf_op jit(solution)/shard_map/ppermute | solution.py:153
  177.2 35.3 %all-to-all-start.2 = ((bf16[16,8,4736]{2,1,0:T(8,128)(2,1)}), bf16[16,8,4736]{2,1,0:T(8,128)(2,1)S(1)}, u32[]{:S(2)}, u32[]{:S(2)}) async-start(bf16[16,8,4736]{2,1,0:T(8,128)(2,1)} %bitcast.20), calls=%async_computation.2 | async-start | bytes 2424832 | tf_op jit(solution)/shard_map/all_to_all | solution.py:165
  182.1 12.5 %collective-permute-start.7 = (bf16[8,42,448]{2,1,0:T(8,128)(2,1)S(1)}, bf16[8,42,448]{2,1,0:T(8,128)(2,1)S(1)}, u32[]{:S(2)}, u32[]{:S(2)}) collective-permute-start(bf16[8,42,448]{2,1,0:T(8,128)(2,1)S(1)} %convolution_convert_fusion.8), channel_id=1, source_target_pairs={{0,2},{2,4},{4,6},{6,0},{1,3},{3,5},{5,7},{7,1},{8,10},{10,12},{12... | collective-permute-start | bytes 903176 | tf_op jit(solution)/shard_map/ppermute | solution.py:176
  184.7 13.8 %collective-permute-start.8 = (bf16[8,42,448]{2,1,0:T(8,128)(2,1)S(1)}, bf16[8,42,448]{2,1,0:T(8,128)(2,1)S(1)}, u32[]{:S(2)}, u32[]{:S(2)}) collective-permute-start(bf16[8,42,448]{2,1,0:T(8,128)(2,1)S(1)} %convolution_convert_fusion.7), channel_id=1, source_target_pairs={{0,4},{2,6},{4,0},{6,2},{1,5},{3,7},{5,1},{7,3},{8,12},{10,14},{12... | collective-permute-start | bytes 903176 | tf_op jit(solution)/shard_map/ppermute | solution.py:176
  189.0 18.7 %collective-permute-start.9 = (bf16[8,42,448]{2,1,0:T(8,128)(2,1)S(1)}, bf16[8,42,448]{2,1,0:T(8,128)(2,1)}, u32[]{:S(2)}, u32[]{:S(2)}) collective-permute-start(bf16[8,42,448]{2,1,0:T(8,128)(2,1)S(1)} %convolution_convert_fusion.6), channel_id=1, source_target_pairs={{0,6},{2,0},{4,2},{6,4},{1,7},{3,1},{5,3},{7,5},{8,14},{10,8},{12,... | collective-permute-start | bytes 903176 | tf_op jit(solution)/shard_map/ppermute | solution.py:176
  212.9 19.8 %collective-permute-start.10 = (bf16[16,4736]{1,0:T(8,128)(2,1)S(1)}, bf16[16,4736]{1,0:T(8,128)(2,1)S(1)}, u32[]{:S(2)}, u32[]{:S(2)}) collective-permute-start(bf16[16,4736]{1,0:T(8,128)(2,1)S(1)} %slice.126), channel_id=1, source_target_pairs={{0,513},{128,641},{256,769},{384,897},{512,1},{640,129},{768,257},... | collective-permute-start | bytes 454664 | tf_op jit(solution)/shard_map/ppermute | solution.py:186
Sparse Core Ops, SparseCore 0:
  115.1 91.9 all-gather.1

commit v3 on v2

--- a/solution.py
+++ b/solution.py
@@ -53,9 +53,11 @@
         ),
         axis=1,
     ).astype(bf)
-    own = jnp.concatenate([activations, cotangent, gate_wide], axis=1)
+    own = jnp.concatenate([cotangent, activations, gate_wide], axis=1)
     wide = own.shape[1]
     other = lax.ppermute(own, ("rep", "half"), pairs)
+    own, other = lax.optimization_barrier((own, other))
+    along_z = lax.all_gather(own[:, hidden:], ("rep", "half"), axis=0, tiled=True)
     both = jnp.concatenate([own, other], axis=0)
 
     places = 2 * rows_one
@@ -84,44 +86,84 @@
     before = (place_index[:, None] < place_index[None, :]).astype(bf)
     slot_at = jnp.arange(cap2, dtype=jnp.int32).astype(f32)
 
-    def pickers(named_here):
+    def pickers(gates_here):
+        named_here = (gates_here != 0).astype(f32)
         result = []
         for j in range(xs):
-            mine_local = jnp.arange(named_here.shape[-1]) == (x_at + j) % xs * 2 + half_at
-            live = jnp.sum(jnp.where(mine_local, named_here, 0.0), axis=-1)
+            mine_local = jnp.arange(locals_) == (x_at + j) % xs * 2 + half_at
+            live = jnp.sum(jnp.where(mine_local[:, None], named_here, 0.0), axis=-2)
             rank = jnp.dot(live.astype(bf), before, preferred_element_type=f32)
             result.append(
                 ((live[..., None, :] > 0) & (rank[..., None, :] == slot_at[:, None])).astype(bf)
             )
         return result
 
-    group_gates = lax.dynamic_slice_in_dim(rows, width + hidden + node_at * locals_, locals_, 1)
-    picker = pickers((group_gates != 0).astype(f32))
-    sent = [jnp.dot(p, rows, preferred_element_type=f32).astype(bf) for p in picker]
+    share = width // reps
+    group_expert = (
+        (node_at * locals_ + jnp.arange(locals_, dtype=jnp.int32))[:, None]
+        == jnp.arange(total, dtype=jnp.int32)[None, :]
+    ).astype(bf)
+    group_gates = lax.dot_general(
+        group_expert,
+        rows[:, width + hidden :],
+        (((1,), (1,)), ((), ())),
+        preferred_element_type=f32,
+    ).astype(bf)
+    ring_rows = reps * 2 * blocks
+    row_index = jnp.arange(nodes * ring_rows, dtype=jnp.int32)
+    token_index = jnp.arange(reps * 2 * tokens, dtype=jnp.int32)
+    token_rep = token_index // (2 * tokens)
+    token_block = token_index % tokens // block
+    token_place = jnp.where(
+        token_index // tokens % 2 == half_at,
+        token_rep * 2 * blocks + token_block,
+        (token_rep + reps // 2) % reps * 2 * blocks + blocks + token_block,
+    )
+    expert_index = jnp.arange(total, dtype=jnp.int32)
+    row_expert = (row_index // ring_rows)[:, None] == (expert_index // locals_)[None, :]
+    ring_gates = along_z[:, width:]
+    row_hit = lax.dot_general(
+        row_expert.astype(bf),
+        (ring_gates != 0).astype(bf),
+        (((1,), (1,)), ((), ())),
+        preferred_element_type=f32,
+    )
+    ring_placing = (
+        (row_hit > 0) & ((row_index % ring_rows)[:, None] == token_place[None, :])
+    ).astype(bf)
+    spare = -share % 128
+    fold = ((expert_index % locals_)[:, None] == jnp.arange(spare)[None, :]).astype(bf)
+    row_gates = jnp.where(
+        row_expert, jnp.dot(ring_placing, ring_gates, preferred_element_type=f32), 0.0
+    ).astype(bf)
+    cols = jnp.concatenate(
+        [
+            jnp.dot(
+                ring_placing,
+                lax.dynamic_slice_in_dim(along_z, rep_at * share, share, 1),
+                preferred_element_type=f32,
+            ),
+            jnp.dot(row_gates, fold, preferred_element_type=f32),
+        ],
+        axis=1,
+    ).astype(bf)
+
+    picker = pickers(group_gates)
+    sent = [
+        jnp.dot(p, rows, preferred_element_type=f32).astype(bf) for p in picker[1:]
+    ]
+    moved = [lax.ppermute(sent[j - 1], "x", ring(xs, j)) for j in range(1, xs)]
+    kept, cols = lax.optimization_barrier((picker[0], cols))
     inside = jnp.concatenate(
-        [sent[0]] + [lax.ppermute(sent[j], "x", ring(xs, j)) for j in range(1, xs)], axis=0
+        [jnp.dot(kept, rows, preferred_element_type=f32).astype(bf)] + moved, axis=0
     )
     taken = xs * cap2
-
-    share = width // reps
-    spare = -(share + locals_) % 128
-    cols = jnp.stack(
-        [
-            jnp.concatenate(
-                [
-                    rows[:, k * share : (k + 1) * share],
-                    group_gates,
-                    jnp.zeros((places, spare), bf),
-                ],
-                axis=1,
-            )
-            for k in range(reps)
-        ]
-    )
-    cols = lax.all_to_all(cols, "rep", 0, 0, tiled=True)
-
-    exp_x = inside[:, :width]
-    exp_dy = inside[:, width : width + hidden].astype(f32)
+    cols = lax.all_to_all(
+        cols.reshape(nodes, ring_rows, share + spare), "node", 0, 0, tiled=True
+    )
+
+    exp_x = inside[:, hidden : hidden + width]
+    exp_dy = inside[:, :hidden].astype(f32)
     mine = jnp.arange(total, dtype=jnp.int32) == node_at * locals_ + x_at * 2 + half_at
     gate = jnp.sum(
         jnp.where(mine[None, :], inside[:, width + hidden :].astype(f32), 0.0), axis=1, keepdims=True
@@ -138,8 +180,8 @@
     grad_gate = jnp.sum(exp_dy * act, axis=1, keepdims=True)
     back = jnp.concatenate(
         [
+            (gate * act).astype(bf),
             grad_in,
-            (gate * act).astype(bf),
             jnp.where(mine[None, :], grad_gate, 0.0).astype(bf),
         ],
         axis=1,
@@ -166,17 +208,26 @@
         back_rows.reshape(nodes, 2 * blocks, wide), "node", 0, 0, tiled=True
     ).reshape(places, wide)
 
+    cols = (
+        cols.reshape(nodes, reps, 2 * blocks, share + spare)
+        .transpose(1, 0, 2, 3)
+        .reshape(reps, places, share + spare)
+    )
+    gate_lane = (
+        share + jnp.arange(locals_, dtype=jnp.int32)[:, None]
+        == jnp.arange(share + spare, dtype=jnp.int32)[None, :]
+    ).astype(bf)
+    all_gates = jnp.einsum("lc,prc->plr", gate_lane, cols, preferred_element_type=f32)
     share_sent = [
-        jnp.einsum(
-            "pcr,prd->pcd", p, cols[:, :, :share], preferred_element_type=f32
-        ).astype(bf)
-        for p in pickers((cols[:, :, share : share + locals_] != 0).astype(f32))
+        jnp.einsum("pcr,prd->pcd", p, cols, preferred_element_type=f32).astype(bf)
+        for p in pickers(all_gates)
     ]
     share_rows = [share_sent[0]] + [
         lax.ppermute(share_sent[j], "x", ring(xs, j)) for j in range(1, xs)
     ]
-    home_rows, share_rows = lax.optimization_barrier((home_rows, share_rows))
-    x_cols = jnp.stack(share_rows, axis=1).reshape(reps * taken, share)
+    home_rows, share_rows, gathered = lax.optimization_barrier((home_rows, share_rows, gathered))
+    x_cols = jnp.stack(share_rows, axis=1).reshape(reps * taken, cols.shape[2])
+    x_cols = x_cols[:, :share]
     grad_share = lax.dot_general(
         x_cols, gathered, (((0,), (0,)), ((), ())), preferred_element_type=f32
     )
@@ -185,8 +236,8 @@
     )
     returned = lax.ppermute(home[tokens:].astype(bf), ("rep", "half"), pairs)
     result = home[:tokens] + returned.astype(f32)
-    grad_activations = result[:, :width].astype(bf)
-    output = result[:, width : width + hidden].astype(bf)
+    grad_activations = result[:, hidden : hidden + width].astype(bf)
+    output = result[:, :hidden].astype(bf)
     gate_back = result[:, width + hidden :]
     grad_gates = jnp.sum(
         jnp.where(

time: 243 us -> 440 us (1.81)
  the two profiles are of different devices: /device:TPU:131 before, /device:TPU:1 now
where the time goes in v3:
time: 440 us; the launch traced here: 439 us
  waiting for transfers between devices  281 us (64%)
  starting transfers between devices  96 us (22%)
  matrix products  31.3 us (7%)
  between operations  14.6 us (3%)
  other arithmetic  8.3 us (2%)
  local copies, waits for them, and re-layouts  7.11 us (2%)
    all_gather x1, waiting for transfers between devices, on_device(): lax.all_gather(own[:, hidden:], ('rep', 'half'), axis=0, tiled=True)  197 us
    all_to_all x1, waiting for transfers between devices, on_device(): lax.all_to_all(send_rows.reshape(nodes, 2 * blocks, wide), 'node', 0, 0,...  30.7 us
    all_to_all x1, starting transfers between devices, on_device(): lax.all_to_all(cols.reshape(nodes, ring_rows, share + spare), 'node', 0,...  26.1 us
    ppermute x1, starting transfers between devices, on_device(): other = lax.ppermute(own, ('rep', 'half'), pairs)  18.7 us
    ppermute x3, waiting for transfers between devices, on_device(): lax.ppermute(back[j * cap2:(j + 1) * cap2], 'x', ring(xs, -j))  16.2 us
    ppermute x1, waiting for transfers between devices, on_device(): other = lax.ppermute(own, ('rep', 'half'), pairs)  12.3 us
    ppermute x3, starting transfers between devices, on_device(): lax.ppermute(back[j * cap2:(j + 1) * cap2], 'x', ring(xs, -j))  12.2 us
    ppermute x3, starting transfers between devices, on_device(): lax.ppermute(share_sent[j], 'x', ring(xs, j))  11.6 us
  transfers between devices with their start and end apart: 16, of which 12 were waited for; matrix products, arithmetic and copies ran while one was open for 5% of the time, Pallas kernels for 0%

profile of v3, /device:TPU:1, one launch (start us, length us, event | category | flops | bytes accessed | tf_op | source)
XLA Modules:
  0.0 438.6 jit_solution(1126397782667273084)
XLA Ops:
  7.2 0.8 copy.23
  7.9 0.7 broadcast_multiply_fusion
  8.6 0.7 add.198
  9.5 0.9 pad_maximum_fusion.5
  10.4 18.7 %collective-permute-start = (bf16[16,4736]{1,0:T(8,128)(2,1)S(1)}, bf16[16,4736]{1,0:T(8,128)(2,1)S(1)}, u32[]{:S(2)}, u32[]{:S(2)}) collective-permute-start(bf16[16,4736]{1,0:T(8,128)(2,1)S(1)} %pad_maximum_fusion.5), channel_id=1, source_target_pairs={{0,513},{128,641},{256,769},{384,897},{512,1},{640,129},{768,257},... | collective-permute-start | bytes 454664 | tf_op jit(solution)/shard_map/ppermute | solution.py:58
  29.2 12.3 %collective-permute-done = bf16[16,4736]{1,0:T(8,128)(2,1)S(1)} collective-permute-done((bf16[16,4736]{1,0:T(8,128)(2,1)S(1)}, bf16[16,4736]{1,0:T(8,128)(2,1)S(1)}, u32[]{:S(2)}, u32[]{:S(2)}) %collective-permute-start) | collective-permute-done | bytes 151584 | tf_op jit(solution)/shard_map/ppermute | solution.py:58
  41.5 0.2 fusion.25
  41.7 1.6 fusion.4
  43.3 8.7 %all-to-all-start = ((bf16[16,8,4736]{2,1,0:T(8,128)(2,1)}), bf16[16,8,4736]{2,1,0:T(8,128)(2,1)S(1)}, u32[]{:S(2)}, u32[]{:S(2)}) async-start(bf16[16,8,4736]{2,1,0:T(8,128)(2,1)} %fusion.4), calls=%async_computation | async-start | bytes 2424832 | tf_op jit(solution)/shard_map/all_to_all | solution.py:81
  52.0 0.6 slice.56
  52.9 30.7 %all-to-all-done = bf16[16,8,4736]{2,1,0:T(8,128)(2,1)S(1)} async-done(((bf16[16,8,4736]{2,1,0:T(8,128)(2,1)}), bf16[16,8,4736]{2,1,0:T(8,128)(2,1)S(1)}, u32[]{:S(2)}, u32[]{:S(2)}) %all-to-all-start) | async-done | bytes 1212448 | tf_op jit(solution)/shard_map/all_to_all | solution.py:81
  83.6 0.2 select_reduce_fusion.6
  83.9 1.1 convolution_convert_fusion.2
  85.1 4.4 collective-permute-start.3
  89.6 1.1 convolution_convert_fusion.3
  90.7 2.4 collective-permute-start.2
  93.3 1.1 convolution_convert_fusion.4
  94.4 2.5 collective-permute-start.1
  97.1 0.7 fusion.97
  97.8 197.4 %all-gather.3.cloned.1.call-done = bf16[256,3712]{1,0:T(8,128)(2,1)} async-done(((bf16[16,3712]{1,0:T(8,128)(2,1)}), bf16[256,3712]{1,0:T(8,128)(2,1)}) %all-gather.3.cloned.1.call-update) | async-done | bytes 1900560 | tf_op jit(solution)/shard_map/all_gather | solution.py:60
  295.2 1.9 fusion.19
  297.1 1.4 fusion.20
  298.4 1.6 convolution_convert_fusion.6
  300.1 0.3 convolution_convert_fusion.5
  300.4 1.4 pad_maximum_fusion
  301.9 0.8 select_reduce_fusion
  302.7 5.5 %fusion.35 = (bf16[168,1024]{1,0:T(8,128)(2,1)S(1)}, bf16[168,1024]{1,0:T(8,128)(2,1)S(1)}, bf16[168,1024]{1,0:T(8,128)(2,1)}, bf16[168,1024]{1,0:T(8,128)(2,1)S(1)}) fusion(f32[168]{0:T(256)S(1)} %select_reduce_fusion, bf16[42,4736]{1,0:T(8,128)(2,1)S(1)} %collective-permute-done.3, bf16[42,4736]{1,0:T(8,128)(2,1)S(1)} %collective-permute-done.2, ...), kind=kOutput, calls=%fused_computation.61 | convolution fusion | flops 1237254144 | bytes 11683328 | tf_op jit(solution)/shard_map/dot_general | solution.py:172
  308.2 5.8 %fusion.5 = bf16[168,3584]{1,0:T(8,128)(2,1)S(1)} fusion(bf16[168,1024]{1,0:T(8,128)(2,1)S(1)} %get-tuple-element.44, bf16[1,3584,1024]{2,1,0:T(8,128)(2,1)} %param.11), kind=kOutput, calls=%fused_computation.11 | convolution fusion | flops 1233727488 | bytes 8888320 | tf_op jit(solution)/shard_map/dot_general | solution.py:177
  314.3 1.3 copy.24
  315.6 26.1 %all-to-all-start.1 = ((bf16[16,64,512]{2,1,0:T(8,128)(2,1)}), bf16[16,64,512]{2,1,0:T(8,128)(2,1)S(1)}, u32[]{:S(2)}, u32[]{:S(2)}) async-start(bf16[16,64,512]{2,1,0:T(8,128)(2,1)} %bitcast.12), calls=%async_computation.1 | async-start | bytes 2097152 | tf_op jit(solution)/shard_map/all_to_all | solution.py:161
  341.9 0.3 fusion.151
  342.2 6.0 %collective-permute-start.6 = (bf16[42,4736]{1,0:T(8,128)(2,1)S(1)}, bf16[42,4736]{1,0:T(8,128)(2,1)S(1)}, u32[]{:S(2)}, u32[]{:S(2)}) collective-permute-start(bf16[42,4736]{1,0:T(8,128)(2,1)S(1)} %get-tuple-element.47), channel_id=1, source_target_pairs={{0,2},{2,4},{4,6},{6,0},{1,3},{3,5},{5,7},{7,1},{8,10},{10,12},{12... | collective-permute-start | bytes 1193480 | tf_op jit(solution)/shard_map/ppermute | solution.py:195
  348.2 1.9 collective-permute-start.5
  350.1 4.3 collective-permute-start.4
  354.4 3.5 collective-permute-done.6
  357.9 10.7 %collective-permute-done.5 = bf16[42,4736]{1,0:T(8,128)(2,1)S(1)} collective-permute-done((bf16[42,4736]{1,0:T(8,128)(2,1)S(1)}, bf16[42,4736]{1,0:T(8,128)(2,1)S(1)}, u32[]{:S(2)}, u32[]{:S(2)}) %collective-permute-start.5) | collective-permute-done | bytes 397856 | tf_op jit(solution)/shard_map/ppermute | solution.py:195
  368.7 2.0 collective-permute-done.4
  370.7 1.8 convolution_convert_fusion
  372.5 7.5 %all-to-all-start.2 = ((bf16[16,8,4736]{2,1,0:T(8,128)(2,1)}), bf16[16,8,4736]{2,1,0:T(8,128)(2,1)S(1)}, u32[]{:S(2)}, u32[]{:S(2)}) async-start(bf16[16,8,4736]{2,1,0:T(8,128)(2,1)} %bitcast.13), calls=%async_computation.2 | async-start | bytes 2424832 | tf_op jit(solution)/shard_map/all_to_all | solution.py:207
  379.9 0.4 fusion.24
  380.6 0.3 convolution_convert_fusion.9
  380.9 4.8 %collective-permute-start.7 = (bf16[8,42,512]{2,1,0:T(8,128)(2,1)S(1)}, bf16[8,42,512]{2,1,0:T(8,128)(2,1)S(1)}, u32[]{:S(2)}, u32[]{:S(2)}) collective-permute-start(bf16[8,42,512]{2,1,0:T(8,128)(2,1)S(1)} %convolution_convert_fusion.9), channel_id=1, source_target_pairs={{0,2},{2,4},{4,6},{6,0},{1,3},{3,5},{5,7},{7,1},{8,10},{10,12},{12... | collective-permute-start | bytes 1032200 | tf_op jit(solution)/shard_map/ppermute | solution.py:226
  385.9 0.3 convolution_convert_fusion.8
  386.3 2.7 collective-permute-start.8
  389.2 0.3 convolution_convert_fusion.7
  389.5 4.0 collective-permute-start.9
  393.7 0.3 convolution_convert_fusion.10
  394.0 0.8 collective-permute-done.7
  394.8 9.3 %collective-permute-done.8 = bf16[8,42,512]{2,1,0:T(8,128)(2,1)S(1)} collective-permute-done((bf16[8,42,512]{2,1,0:T(8,128)(2,1)S(1)}, bf16[8,42,512]{2,1,0:T(8,128)(2,1)S(1)}, u32[]{:S(2)}, u32[]{:S(2)}) %collective-permute-start.8) | collective-permute-done | bytes 344096 | tf_op jit(solution)/shard_map/ppermute | solution.py:226
  404.2 0.8 copy-done.3
  404.9 1.0 collective-permute-done.9
  406.0 5.6 %all-to-all-done.2 = bf16[16,8,4736]{2,1,0:T(8,128)(2,1)S(1)} async-done(((bf16[16,8,4736]{2,1,0:T(8,128)(2,1)}), bf16[16,8,4736]{2,1,0:T(8,128)(2,1)S(1)}, u32[]{:S(2)}, u32[]{:S(2)}) %all-to-all-start.2) | async-done | bytes 1212448 | tf_op jit(solution)/shard_map/all_to_all | solution.py:207
  411.5 0.7 all-gather.5.cloned.1.call-done
  412.3 0.3 fusion.152
  412.6 0.7 slice.104
  413.2 1.9 collective-permute-start.10
  415.2 1.2 pad_maximum_fusion.2
  416.5 0.4 reshape.267
  416.9 4.6 %convolution_bitcast_fusion = f32[1,448,1024]{2,1,0:T(8,128)} fusion(bf16[1344,1024]{1,0:T(8,128)(2,1)} %all-gather.5.cloned.1.call-done, bf16[1344,512]{1,0:T(8,128)(2,1)S(1)} %reshape.267), kind=kOutput, calls=%fused_computation.22 | convolution fusion | flops 1233125376 | bytes 5963776 | tf_op jit(solution)/shard_map/dot_general | solution.py:231
  421.6 7.2 %collective-permute-done.10 = bf16[16,4736]{1,0:T(8,128)(2,1)} collective-permute-done((bf16[16,4736]{1,0:T(8,128)(2,1)}, bf16[16,4736]{1,0:T(8,128)(2,1)}, u32[]{:S(2)}, u32[]{:S(2)}) %collective-permute-start.10) | collective-permute-done | bytes 151584 | tf_op jit(solution)/shard_map/ppermute | solution.py:237
  428.7 0.9 fusion.150
  429.7 0.6 slice.81
  430.3 0.7 slice.82
  431.1 0.7 copy.27
  (84 shorter events, 2.4 us)
Async XLA Ops:
  9.4 33.9 %copy-start.6 = (s32[16,8]{1,0:T(8,128)}, s32[16,8]{1,0:T(8,128)S(1)}, u32[]{:S(2)}) copy-start(s32[16,8]{1,0:T(8,128)S(1)} %copy.22) | copy-start | bytes 1540
  10.4 31.1 %collective-permute-start = (bf16[16,4736]{1,0:T(8,128)(2,1)S(1)}, bf16[16,4736]{1,0:T(8,128)(2,1)S(1)}, u32[]{:S(2)}, u32[]{:S(2)}) collective-permute-start(bf16[16,4736]{1,0:T(8,128)(2,1)S(1)} %pad_maximum_fusion.5), channel_id=1, source_target_pairs={{0,513},{128,641},{256,769},{384,897},{512,1},{640,129},{768,257},... | collective-permute-start | bytes 454664 | tf_op jit(solution)/shard_map/ppermute | solution.py:58
  41.7 1.6 copy-start.8
  43.3 40.3 %all-to-all-start = ((bf16[16,8,4736]{2,1,0:T(8,128)(2,1)}), bf16[16,8,4736]{2,1,0:T(8,128)(2,1)S(1)}, u32[]{:S(2)}, u32[]{:S(2)}) async-start(bf16[16,8,4736]{2,1,0:T(8,128)(2,1)} %fusion.4), calls=%async_computation | async-start | bytes 2424832 | tf_op jit(solution)/shard_map/all_to_all | solution.py:81
  52.0 243.2 %all-gather.3.cloned.1.call-start = ((), (), s32[]{:S(2)}) async-start(), calls=%async_computation.3 | async-start | bytes 2019328 | tf_op jit(solution)/shard_map/all_gather | solution.py:60
  52.7 359.6 %all-gather.5.cloned.1.call-start = ((), (), s32[]{:S(2)}) async-start(), calls=%async_computation.4 | async-start | bytes 3096576 | tf_op jit(solution)/shard_map/all_gather | solution.py:190
  52.8 249.0 %copy-start.17 = (pred[128]{0:T(512)(128)(4,1)}, pred[128]{0:T(512)(128)(4,1)S(1)}, u32[]{:S(2)}) copy-start(pred[128]{0:T(512)(128)(4,1)S(1)} %iota_compare_fusion.15) | copy-start | bytes 388
  52.9 37.8 %copy-start.11 = (pred[8]{0:T(512)(128)(4,1)}, pred[8]{0:T(512)(128)(4,1)S(1)}, u32[]{:S(2)}) copy-start(pred[8]{0:T(512)(128)(4,1)S(1)} %get-tuple-element.61) | copy-start | bytes 28
  52.9 37.8 %copy-start.13 = (pred[8]{0:T(512)(128)(4,1)}, pred[8]{0:T(512)(128)(4,1)S(1)}, u32[]{:S(2)}) copy-start(pred[8]{0:T(512)(128)(4,1)S(1)} %get-tuple-element.58) | copy-start | bytes 28
  52.9 37.8 %copy-start.15 = (pred[8]{0:T(512)(128)(4,1)}, pred[8]{0:T(512)(128)(4,1)S(1)}, u32[]{:S(2)}) copy-start(pred[8]{0:T(512)(128)(4,1)S(1)} %get-tuple-element.59) | copy-start | bytes 28
  85.1 215.3 %collective-permute-start.3 = (bf16[42,4736]{1,0:T(8,128)(2,1)}, bf16[42,4736]{1,0:T(8,128)(2,1)S(1)}, u32[]{:S(2)}, u32[]{:S(2)}) collective-permute-start(bf16[42,4736]{1,0:T(8,128)(2,1)} %convolution_convert_fusion.2), channel_id=1, source_target_pairs={{0,6},{2,0},{4,2},{6,4},{1,7},{3,1},{5,3},{7,5},{8,14},{10,8},{12,... | collective-permute-start | bytes 1193480 | tf_op jit(solution)/shard_map/ppermute | solution.py:155
  90.7 209.7 %collective-permute-start.2 = (bf16[42,4736]{1,0:T(8,128)(2,1)}, bf16[42,4736]{1,0:T(8,128)(2,1)S(1)}, u32[]{:S(2)}, u32[]{:S(2)}) collective-permute-start(bf16[42,4736]{1,0:T(8,128)(2,1)} %convolution_convert_fusion.3), channel_id=1, source_target_pairs={{0,4},{2,6},{4,0},{6,2},{1,5},{3,7},{5,1},{7,3},{8,12},{10,14},{12... | collective-permute-start | bytes 1193480 | tf_op jit(solution)/shard_map/ppermute | solution.py:155
  94.4 206.0 %collective-permute-start.1 = (bf16[42,4736]{1,0:T(8,128)(2,1)}, bf16[42,4736]{1,0:T(8,128)(2,1)}, u32[]{:S(2)}, u32[]{:S(2)}) collective-permute-start(bf16[42,4736]{1,0:T(8,128)(2,1)} %convolution_convert_fusion.4), channel_id=1, source_target_pairs={{0,2},{2,4},{4,6},{6,0},{1,3},{3,5},{5,7},{7,1},{8,10},{10,12},{12... | collective-permute-start | bytes 1193480 | tf_op jit(solution)/shard_map/ppermute | solution.py:155
  308.2 5.8 %copy-start = (bf16[168,1024]{1,0:T(8,128)(2,1)}, bf16[168,1024]{1,0:T(8,128)(2,1)S(1)}, u32[]{:S(2)}) copy-start(bf16[168,1024]{1,0:T(8,128)(2,1)S(1)} %get-tuple-element.44) | copy-start | bytes 1032196
  308.2 6.0 %copy-start.18 = (pred[128]{0:T(512)(128)(4,1)S(1)}, pred[128]{0:T(512)(128)(4,1)}, u32[]{:S(2)}) copy-start(pred[128]{0:T(512)(128)(4,1)} %copy-done.17) | copy-start | bytes 388
  315.6 26.1 %copy-start.5 = (bf16[168,1024]{1,0:T(8,128)(2,1)S(1)}, bf16[168,1024]{1,0:T(8,128)(2,1)}, u32[]{:S(2)}) copy-start(bf16[168,1024]{1,0:T(8,128)(2,1)} %get-tuple-element.50) | copy-start | bytes 1032196
  315.6 56.8 %all-to-all-start.1 = ((bf16[16,64,512]{2,1,0:T(8,128)(2,1)}), bf16[16,64,512]{2,1,0:T(8,128)(2,1)S(1)}, u32[]{:S(2)}, u32[]{:S(2)}) async-start(bf16[16,64,512]{2,1,0:T(8,128)(2,1)} %bitcast.12), calls=%async_computation.1 | async-start | bytes 2097152 | tf_op jit(solution)/shard_map/all_to_all | solution.py:161
  341.9 28.8 %copy-start.10 = (bf16[42,128]{1,0:T(8,128)(2,1)S(1)}, bf16[42,128]{1,0:T(8,128)(2,1)}, u32[]{:S(2)}) copy-start(bf16[42,128]{1,0:T(8,128)(2,1)} %get-tuple-element.54) | copy-start | bytes 32260
  342.2 15.7 %collective-permute-start.6 = (bf16[42,4736]{1,0:T(8,128)(2,1)S(1)}, bf16[42,4736]{1,0:T(8,128)(2,1)S(1)}, u32[]{:S(2)}, u32[]{:S(2)}) collective-permute-start(bf16[42,4736]{1,0:T(8,128)(2,1)S(1)} %get-tuple-element.47), channel_id=1, source_target_pairs={{0,2},{2,4},{4,6},{6,0},{1,3},{3,5},{5,7},{7,1},{8,10},{10,12},{12... | collective-permute-start | bytes 1193480 | tf_op jit(solution)/shard_map/ppermute | solution.py:195
  348.2 20.5 %collective-permute-start.5 = (bf16[42,4736]{1,0:T(8,128)(2,1)S(1)}, bf16[42,4736]{1,0:T(8,128)(2,1)S(1)}, u32[]{:S(2)}, u32[]{:S(2)}) collective-permute-start(bf16[42,4736]{1,0:T(8,128)(2,1)S(1)} %get-tuple-element.48), channel_id=1, source_target_pairs={{0,4},{2,6},{4,0},{6,2},{1,5},{3,7},{5,1},{7,3},{8,12},{10,14},{12... | collective-permute-start | bytes 1193480 | tf_op jit(solution)/shard_map/ppermute | solution.py:195
  350.1 20.6 %collective-permute-start.4 = (bf16[42,4736]{1,0:T(8,128)(2,1)S(1)}, bf16[42,4736]{1,0:T(8,128)(2,1)S(1)}, u32[]{:S(2)}, u32[]{:S(2)}) collective-permute-start(bf16[42,4736]{1,0:T(8,128)(2,1)S(1)} %get-tuple-element.49), channel_id=1, source_target_pairs={{0,6},{2,0},{4,2},{6,4},{1,7},{3,1},{5,3},{7,5},{8,14},{10,8},{12,... | collective-permute-start | bytes 1193480 | tf_op jit(solution)/shard_map/ppermute | solution.py:195
  372.5 7.8 %copy-start.12 = (pred[8]{0:T(512)(128)(4,1)S(1)}, pred[8]{0:T(512)(128)(4,1)}, u32[]{:S(2)}) copy-start(pred[8]{0:T(512)(128)(4,1)} %copy-done.11) | copy-start | bytes 28
  372.5 7.9 %copy-start.14 = (pred[8]{0:T(512)(128)(4,1)S(1)}, pred[8]{0:T(512)(128)(4,1)}, u32[]{:S(2)}) copy-start(pred[8]{0:T(512)(128)(4,1)} %copy-done.13) | copy-start | bytes 28
  372.5 7.9 %copy-start.16 = (pred[8]{0:T(512)(128)(4,1)S(1)}, pred[8]{0:T(512)(128)(4,1)}, u32[]{:S(2)}) copy-start(pred[8]{0:T(512)(128)(4,1)} %copy-done.15) | copy-start | bytes 28
  372.5 39.1 %all-to-all-start.2 = ((bf16[16,8,4736]{2,1,0:T(8,128)(2,1)}), bf16[16,8,4736]{2,1,0:T(8,128)(2,1)S(1)}, u32[]{:S(2)}, u32[]{:S(2)}) async-start(bf16[16,8,4736]{2,1,0:T(8,128)(2,1)} %bitcast.13), calls=%async_computation.2 | async-start | bytes 2424832 | tf_op jit(solution)/shard_map/all_to_all | solution.py:207
  380.9 13.9 %collective-permute-start.7 = (bf16[8,42,512]{2,1,0:T(8,128)(2,1)S(1)}, bf16[8,42,512]{2,1,0:T(8,128)(2,1)S(1)}, u32[]{:S(2)}, u32[]{:S(2)}) collective-permute-start(bf16[8,42,512]{2,1,0:T(8,128)(2,1)S(1)} %convolution_convert_fusion.9), channel_id=1, source_target_pairs={{0,2},{2,4},{4,6},{6,0},{1,3},{3,5},{5,7},{7,1},{8,10},{10,12},{12... | collective-permute-start | bytes 1032200 | tf_op jit(solution)/shard_map/ppermute | solution.py:226
  386.3 26.0 %copy-start.9 = (pred[128,32]{0,1:T(32,128)(4,1)S(1)}, pred[128,32]{0,1:T(32,128)(4,1)}, u32[]{:S(2)}) copy-start(pred[128,32]{0,1:T(32,128)(4,1)} %copy-done.8) | copy-start | bytes 12292
  386.3 17.9 %collective-permute-start.8 = (bf16[8,42,512]{2,1,0:T(8,128)(2,1)S(1)}, bf16[8,42,512]{2,1,0:T(8,128)(2,1)S(1)}, u32[]{:S(2)}, u32[]{:S(2)}) collective-permute-start(bf16[8,42,512]{2,1,0:T(8,128)(2,1)S(1)} %convolution_convert_fusion.8), channel_id=1, source_target_pairs={{0,4},{2,6},{4,0},{6,2},{1,5},{3,7},{5,1},{7,3},{8,12},{10,14},{12... | collective-permute-start | bytes 1032200 | tf_op jit(solution)/shard_map/ppermute | solution.py:226
  389.5 16.5 %collective-permute-start.9 = (bf16[8,42,512]{2,1,0:T(8,128)(2,1)S(1)}, bf16[8,42,512]{2,1,0:T(8,128)(2,1)}, u32[]{:S(2)}, u32[]{:S(2)}) collective-permute-start(bf16[8,42,512]{2,1,0:T(8,128)(2,1)S(1)} %convolution_convert_fusion.7), channel_id=1, source_target_pairs={{0,6},{2,0},{4,2},{6,4},{1,7},{3,1},{5,3},{7,5},{8,14},{10,8},{12,... | collective-permute-start | bytes 1032200 | tf_op jit(solution)/shard_map/ppermute | solution.py:226
  394.8 9.3 %copy-start.1 = (bf16[8,42,512]{2,1,0:T(8,128)(2,1)}, bf16[8,42,512]{2,1,0:T(8,128)(2,1)S(1)}, u32[]{:S(2)}) copy-start(bf16[8,42,512]{2,1,0:T(8,128)(2,1)S(1)} %collective-permute-done.7) | copy-start | bytes 1032196
  404.2 0.8 copy-start.3
  406.0 9.2 %copy-start.2 = (bf16[8,42,512]{2,1,0:T(8,128)(2,1)S(1)}, bf16[8,42,512]{2,1,0:T(8,128)(2,1)}, u32[]{:S(2)}) copy-start(bf16[8,42,512]{2,1,0:T(8,128)(2,1)} %copy-done.1) | copy-start | bytes 1032196
  406.0 9.2 %copy-start.4 = (bf16[8,42,512]{2,1,0:T(8,128)(2,1)S(1)}, bf16[8,42,512]{2,1,0:T(8,128)(2,1)}, u32[]{:S(2)}) copy-start(bf16[8,42,512]{2,1,0:T(8,128)(2,1)} %copy-done.3) | copy-start | bytes 1032196
  413.2 15.5 %collective-permute-start.10 = (bf16[16,4736]{1,0:T(8,128)(2,1)}, bf16[16,4736]{1,0:T(8,128)(2,1)}, u32[]{:S(2)}, u32[]{:S(2)}) collective-permute-start(bf16[16,4736]{1,0:T(8,128)(2,1)} %slice.104), channel_id=1, source_target_pairs={{0,513},{128,641},{256,769},{384,897},{512,1},{640,129},{768,257},... | collective-permute-start | bytes 454664 | tf_op jit(solution)/shard_map/ppermute | solution.py:237
  416.9 14.0 %copy-start.7 = (s32[16,8]{1,0:T(8,128)S(1)}, s32[16,8]{1,0:T(8,128)}, u32[]{:S(2)}) copy-start(s32[16,8]{1,0:T(8,128)} %copy-done.6) | copy-start | bytes 1540
Sparse Core Ops, SparseCore 0:
  55.5 239.6 all-gather.2
  314.2 98.0 all-gather.4

commit v4 on v3

--- a/solution.py
+++ b/solution.py
@@ -1,6 +1,10 @@
+import functools
+
 import jax
 import jax.numpy as jnp
 from jax import lax
+from jax.experimental import pallas as pl
+from jax.experimental.pallas import tpu as pltpu
 from jax.sharding import Mesh, PartitionSpec as P
 
 ALL = ("rep", "node", "x", "half")
@@ -19,6 +23,91 @@
 
 def ring(size, step):
     return [(i, (i + step) % size) for i in range(size)]
+
+
+def expert_kernel(hidden, width, chunk, mine_ref, *refs):
+    count = (len(refs) - 5) // 2
+    slabs, weight_ref = refs[:count], refs[count]
+    backs, grad_ref = refs[count + 1 : 2 * count + 1], refs[2 * count + 1]
+    held, total, sems = refs[2 * count + 2 :]
+    rows = slabs[0].shape[0]
+    chunks = width // chunk
+    f32 = jnp.float32
+    bf = jnp.bfloat16
+    copies = [
+        pltpu.make_async_copy(
+            weight_ref.at[0, pl.ds(k * chunk, chunk), :],
+            held.at[pl.ds(k * chunk, chunk), :],
+            sems.at[k],
+        )
+        for k in range(chunks)
+    ]
+    for copy in copies:
+        copy.start()
+
+    def gather(start, size):
+        return jnp.concatenate([slab[:, start : start + size] for slab in slabs], axis=0)
+
+    for k in range(chunks):
+        copies[k].wait()
+        part = jnp.dot(
+            gather(hidden + k * chunk, chunk),
+            held[k * chunk : (k + 1) * chunk, :],
+            preferred_element_type=f32,
+        )
+        if k:
+            total[...] += part
+        else:
+            total[...] = part
+    mine = mine_ref[...]
+    gate = jnp.sum(
+        gather(hidden + width, mine.shape[1]).astype(f32) * mine, axis=1, keepdims=True
+    )
+    pre = total[...]
+    dy = gather(0, hidden).astype(f32)
+    sig = jax.nn.sigmoid(pre)
+    act = (pre * sig).astype(bf).astype(f32)
+    grad_pre = (gate * dy * (sig * (1.0 + pre * (1.0 - sig)))).astype(bf)
+    grad_ref[...] = grad_pre
+    grad_gate = (jnp.sum(dy * act, axis=1, keepdims=True) * mine).astype(bf)
+    scaled = (gate * act).astype(bf)
+    for j, back in enumerate(backs):
+        back[:, :hidden] = scaled[j * rows : (j + 1) * rows]
+        back[:, hidden + width :] = grad_gate[j * rows : (j + 1) * rows]
+    for k in range(chunks):
+        part = lax.dot_general(
+            grad_pre,
+            held[k * chunk : (k + 1) * chunk, :],
+            (((1,), (1,)), ((), ())),
+            preferred_element_type=f32,
+        ).astype(bf)
+        for j, back in enumerate(backs):
+            back[:, hidden + k * chunk : hidden + (k + 1) * chunk] = part[
+                j * rows : (j + 1) * rows
+            ]
+
+
+def expert(slabs, weights, mine):
+    rows, wide = slabs[0].shape
+    width, hidden = weights.shape[1:]
+    chunk = 512 if width % 512 == 0 else width
+    count = len(slabs)
+    vmem = pl.BlockSpec(memory_space=pltpu.VMEM)
+    result = pl.pallas_call(
+        functools.partial(expert_kernel, hidden, width, chunk),
+        out_shape=[jax.ShapeDtypeStruct((rows, wide), jnp.bfloat16)] * count
+        + [jax.ShapeDtypeStruct((count * rows, hidden), jnp.bfloat16)],
+        in_specs=[vmem] * (count + 1) + [pl.BlockSpec(memory_space=pl.ANY)],
+        out_specs=[vmem] * (count + 1),
+        scratch_shapes=[
+            pltpu.VMEM((width, hidden), jnp.bfloat16),
+            pltpu.VMEM((count * rows, hidden), jnp.float32),
+            pltpu.SemaphoreType.DMA((width // chunk,)),
+        ],
+        compiler_params=pltpu.CompilerParams(vmem_limit_bytes=32 * 1024 * 1024),
+        cost_estimate=pl.CostEstimate(flops=0, bytes_accessed=1024, transcendentals=0),
+    )(mine, *slabs, weights)
+    return result[:count], result[count]
 
 
 def on_device(activations, cotangent, gates, experts, groups, weights):
@@ -57,7 +146,7 @@
     wide = own.shape[1]
     other = lax.ppermute(own, ("rep", "half"), pairs)
     own, other = lax.optimization_barrier((own, other))
-    along_z = lax.all_gather(own[:, hidden:], ("rep", "half"), axis=0, tiled=True)
+    along_z = lax.all_gather(own[:, hidden:], ("half", "rep"), axis=0, tiled=True)
     both = jnp.concatenate([own, other], axis=0)
 
     places = 2 * rows_one
@@ -82,7 +171,7 @@
         send_rows.reshape(nodes, 2 * blocks, wide), "node", 0, 0, tiled=True
     ).reshape(places, wide)
 
-    cap2 = 2 * cap
+    cap2 = -(-2 * cap // 16) * 16
     before = (place_index[:, None] < place_index[None, :]).astype(bf)
     slot_at = jnp.arange(cap2, dtype=jnp.int32).astype(f32)
 
@@ -112,10 +201,10 @@
     ring_rows = reps * 2 * blocks
     row_index = jnp.arange(nodes * ring_rows, dtype=jnp.int32)
     token_index = jnp.arange(reps * 2 * tokens, dtype=jnp.int32)
-    token_rep = token_index // (2 * tokens)
+    token_rep = token_index // tokens % reps
     token_block = token_index % tokens // block
     token_place = jnp.where(
-        token_index // tokens % 2 == half_at,
+        token_index // (tokens * reps) == half_at,
         token_rep * 2 * blocks + token_block,
         (token_rep + reps // 2) % reps * 2 * blocks + blocks + token_block,
     )
@@ -154,45 +243,23 @@
     ]
     moved = [lax.ppermute(sent[j - 1], "x", ring(xs, j)) for j in range(1, xs)]
     kept, cols = lax.optimization_barrier((picker[0], cols))
-    inside = jnp.concatenate(
-        [jnp.dot(kept, rows, preferred_element_type=f32).astype(bf)] + moved, axis=0
-    )
+    slabs = [jnp.dot(kept, rows, preferred_element_type=f32).astype(bf)] + moved
     taken = xs * cap2
     cols = lax.all_to_all(
         cols.reshape(nodes, ring_rows, share + spare), "node", 0, 0, tiled=True
     )
 
-    exp_x = inside[:, hidden : hidden + width]
-    exp_dy = inside[:, :hidden].astype(f32)
     mine = jnp.arange(total, dtype=jnp.int32) == node_at * locals_ + x_at * 2 + half_at
-    gate = jnp.sum(
-        jnp.where(mine[None, :], inside[:, width + hidden :].astype(f32), 0.0), axis=1, keepdims=True
-    )
-    weight = weights[0]
-    pre = jnp.dot(exp_x, weight, preferred_element_type=f32)
-    sig = jax.nn.sigmoid(pre)
-    act = (pre * sig).astype(bf).astype(f32)
-    slope = sig * (1.0 + pre * (1.0 - sig))
-    grad_pre = (gate * exp_dy * slope).astype(bf)
-    grad_in = lax.dot_general(
-        grad_pre, weight, (((1,), (1,)), ((), ())), preferred_element_type=f32
-    ).astype(bf)
-    grad_gate = jnp.sum(exp_dy * act, axis=1, keepdims=True)
-    back = jnp.concatenate(
-        [
-            (gate * act).astype(bf),
-            grad_in,
-            jnp.where(mine[None, :], grad_gate, 0.0).astype(bf),
-        ],
-        axis=1,
-    )
+    back, grad_pre = expert(slabs, weights, mine.astype(f32)[None, :])
 
     gathered = lax.all_gather(grad_pre, "rep", axis=0, tiled=True)
 
+    last = xs - 1
+    back_last, cols = lax.optimization_barrier((back[last], cols))
     back_slots = jnp.concatenate(
-        [back[:cap2]]
+        [back[0]]
         + [
-            lax.ppermute(back[j * cap2 : (j + 1) * cap2], "x", ring(xs, -j))
+            lax.ppermute(back_last if j == last else back[j], "x", ring(xs, -j))
             for j in range(1, xs)
         ],
         axis=0,
@@ -203,7 +270,6 @@
         (((0,), (0,)), ((), ())),
         preferred_element_type=f32,
     ).astype(bf)
-    back_rows, cols = lax.optimization_barrier((back_rows, cols))
     home_rows = lax.all_to_all(
         back_rows.reshape(nodes, 2 * blocks, wide), "node", 0, 0, tiled=True
     ).reshape(places, wide)
@@ -225,7 +291,6 @@
     share_rows = [share_sent[0]] + [
         lax.ppermute(share_sent[j], "x", ring(xs, j)) for j in range(1, xs)
     ]
-    home_rows, share_rows, gathered = lax.optimization_barrier((home_rows, share_rows, gathered))
     x_cols = jnp.stack(share_rows, axis=1).reshape(reps * taken, cols.shape[2])
     x_cols = x_cols[:, :share]
     grad_share = lax.dot_general(
@@ -235,6 +300,7 @@
         placing, home_rows, (((0,), (0,)), ((), ())), preferred_element_type=f32
     )
     returned = lax.ppermute(home[tokens:].astype(bf), ("rep", "half"), pairs)
+    returned, grad_share = lax.optimization_barrier((returned, grad_share))
     result = home[:tokens] + returned.astype(f32)
     grad_activations = result[:, hidden : hidden + width].astype(bf)
     output = result[:, :hidden].astype(bf)

time: 440 us -> 261 us (0.59)
  waiting for transfers between devices: 281 us -> 117 us
  starting transfers between devices: 96 us -> 80.5 us
  matrix products: 31.3 us -> 25.9 us
  Pallas kernels: 0 us -> 5.25 us
    all_gather x1, waiting for transfers between devices: 197 us -> 24.1 us  [on_device(): lax.all_gather(own[:, hidden:], ('half', 'rep'), axis=0, tiled=True)]
    all_to_all x1, waiting for transfers between devices: 0.01 us -> 12.4 us  [on_device(): lax.all_to_all(cols.reshape(nodes, ring_rows, share + spare), 'node', 0,...]
    all_gather x1, waiting for transfers between devices: 0.72 us -> 12.3 us  [on_device(): gathered = lax.all_gather(grad_pre, 'rep', axis=0, tiled=True)]
    dot_general x3 -> x1, matrix products: 11.6 us -> 0.31 us  [on_device(): slabs = [jnp.dot(kept, rows, preferred_element_type=f32).astype(bf)] + moved]
    all_to_all x1, starting transfers between devices: 26.1 us -> 16.5 us  [on_device(): lax.all_to_all(cols.reshape(nodes, ring_rows, share + spare), 'node', 0,...]
    ppermute x1, waiting for transfers between devices: 7.17 us -> 0.01 us  [on_device(): returned = lax.ppermute(home[tokens:].astype(bf), ('rep', 'half'), pairs)]
    ppermute x3, waiting for transfers between devices: 16.2 us -> 10.5 us  [on_device(): lax.ppermute(back_last if j == last else back[j], 'x', ring(xs, -j))]
    pallas_call x0 -> x1, Pallas kernels: none -> 5.25 us  [expert(): pl.pallas_call(functools.partial(expert_kernel, hidden, width, chunk), ou...]
  transfers between devices with their start and end apart: 16 -> 16, of which waited for: 12 -> 10; matrix products, arithmetic and copies ran while one was open for 5% -> 12% of each run, Pallas kernels for 0% -> 2%
where the time goes in v4:
time: 261 us; the launch traced here: 259 us
  waiting for transfers between devices  117 us (45%)
  starting transfers between devices  80.5 us (31%)
  matrix products  25.9 us (10%)
  between operations  14.6 us (6%)
  local copies, waits for them, and re-layouts  8.98 us (3%)
  other arithmetic  6.21 us (2%)
  Pallas kernels  5.25 us (2%)
    all_to_all x1, waiting for transfers between devices, on_device(): lax.all_to_all(send_rows.reshape(nodes, 2 * blocks, wide), 'node', 0, 0,...  29.2 us
    all_gather x1, waiting for transfers between devices, on_device(): lax.all_gather(own[:, hidden:], ('half', 'rep'), axis=0, tiled=True)  24.1 us
    ppermute x1, starting transfers between devices, on_device(): other = lax.ppermute(own, ('rep', 'half'), pairs)  18.7 us
    all_to_all x1, starting transfers between devices, on_device(): lax.all_to_all(cols.reshape(nodes, ring_rows, share + spare), 'node', 0,...  16.5 us
    ppermute x3, waiting for transfers between devices, on_device(): lax.ppermute(share_sent[j], 'x', ring(xs, j))  14.7 us
    all_to_all x1, waiting for transfers between devices, on_device(): lax.all_to_all(cols.reshape(nodes, ring_rows, share + spare), 'node', 0,...  12.4 us
    all_gather x1, waiting for transfers between devices, on_device(): gathered = lax.all_gather(grad_pre, 'rep', axis=0, tiled=True)  12.3 us
    ppermute x1, waiting for transfers between devices, on_device(): other = lax.ppermute(own, ('rep', 'half'), pairs)  12.3 us
  transfers between devices with their start and end apart: 16, of which 10 were waited for; matrix products, arithmetic and copies ran while one was open for 12% of the time, Pallas kernels for 2%

profile of v4, /device:TPU:1, one launch (start us, length us, event | category | flops | bytes accessed | tf_op | source)
XLA Modules:
  0.0 258.5 jit_solution(16983012127800812835)
XLA Ops:
  7.2 0.8 copy.23
  7.9 0.7 broadcast_multiply_fusion
  8.6 0.7 add.194
  9.5 0.9 pad_maximum_fusion.2
  10.4 18.7 %collective-permute-start = (bf16[16,4736]{1,0:T(8,128)(2,1)S(1)}, bf16[16,4736]{1,0:T(8,128)(2,1)S(1)}, u32[]{:S(2)}, u32[]{:S(2)}) collective-permute-start(bf16[16,4736]{1,0:T(8,128)(2,1)S(1)} %pad_maximum_fusion.2), channel_id=1, source_target_pairs={{0,513},{128,641},{256,769},{384,897},{512,1},{640,129},{768,257},... | collective-permute-start | bytes 454664 | tf_op jit(solution)/shard_map/ppermute | solution.py:147
  29.2 12.3 %collective-permute-done = bf16[16,4736]{1,0:T(8,128)(2,1)S(1)} collective-permute-done((bf16[16,4736]{1,0:T(8,128)(2,1)S(1)}, bf16[16,4736]{1,0:T(8,128)(2,1)S(1)}, u32[]{:S(2)}, u32[]{:S(2)}) %collective-permute-start) | collective-permute-done | bytes 151584 | tf_op jit(solution)/shard_map/ppermute | solution.py:147
  41.5 0.2 fusion.22
  41.7 1.6 fusion
  43.3 8.7 %all-to-all-start = ((bf16[16,8,4736]{2,1,0:T(8,128)(2,1)}), bf16[16,8,4736]{2,1,0:T(8,128)(2,1)S(1)}, u32[]{:S(2)}, u32[]{:S(2)}) async-start(bf16[16,8,4736]{2,1,0:T(8,128)(2,1)} %fusion), calls=%async_computation | async-start | bytes 2424832 | tf_op jit(solution)/shard_map/all_to_all | solution.py:170
  52.0 0.7 slice.35
  52.8 0.6 compare_select_fusion.4
  53.4 0.6 fusion.105
  54.0 29.2 %all-to-all-done = bf16[16,8,4736]{2,1,0:T(8,128)(2,1)S(1)} async-done(((bf16[16,8,4736]{2,1,0:T(8,128)(2,1)}), bf16[16,8,4736]{2,1,0:T(8,128)(2,1)S(1)}, u32[]{:S(2)}, u32[]{:S(2)}) %all-to-all-start) | async-done | bytes 1212448 | tf_op jit(solution)/shard_map/all_to_all | solution.py:170
  83.2 0.2 select_reduce_fusion.2
  83.4 0.1 convolution_bitcast_fusion.2
  83.5 0.4 convolution_convert_fusion.4
  83.9 3.1 %collective-permute-start.1 = (bf16[48,4736]{1,0:T(8,128)(2,1)S(1)}, bf16[48,4736]{1,0:T(8,128)(2,1)S(1)}, u32[]{:S(2)}, u32[]{:S(2)}) collective-permute-start(bf16[48,4736]{1,0:T(8,128)(2,1)S(1)} %convolution_convert_fusion.4), channel_id=1, source_target_pairs={{0,2},{2,4},{4,6},{6,0},{1,3},{3,5},{5,7},{7,1},{8,10},{10,12},{12... | collective-permute-start | bytes 1363976 | tf_op jit(solution)/shard_map/ppermute | solution.py:244
  87.0 0.1 convolution_bitcast_fusion.1
  87.2 0.4 convolution_convert_fusion.3
  87.6 4.4 %collective-permute-start.2 = (bf16[48,4736]{1,0:T(8,128)(2,1)S(1)}, bf16[48,4736]{1,0:T(8,128)(2,1)S(1)}, u32[]{:S(2)}, u32[]{:S(2)}) collective-permute-start(bf16[48,4736]{1,0:T(8,128)(2,1)S(1)} %convolution_convert_fusion.3), channel_id=1, source_target_pairs={{0,4},{2,6},{4,0},{6,2},{1,5},{3,7},{5,1},{7,3},{8,12},{10,14},{12... | collective-permute-start | bytes 1363976 | tf_op jit(solution)/shard_map/ppermute | solution.py:244
  91.9 0.1 convolution_bitcast_fusion
  92.1 1.1 convolution_convert_fusion.2
  93.2 3.0 %collective-permute-start.3 = (bf16[48,4736]{1,0:T(8,128)(2,1)}, bf16[48,4736]{1,0:T(8,128)(2,1)S(1)}, u32[]{:S(2)}, u32[]{:S(2)}) collective-permute-start(bf16[48,4736]{1,0:T(8,128)(2,1)} %convolution_convert_fusion.2), channel_id=1, source_target_pairs={{0,6},{2,0},{4,2},{6,4},{1,7},{3,1},{5,3},{7,5},{8,14},{10,8},{12,... | collective-permute-start | bytes 1363976 | tf_op jit(solution)/shard_map/ppermute | solution.py:244
  96.5 24.1 %all-gather.3.cloned.1.call-done = bf16[256,3712]{1,0:T(8,128)(2,1)} async-done(((bf16[16,3712]{1,0:T(8,128)(2,1)}), bf16[256,3712]{1,0:T(8,128)(2,1)}) %all-gather.3.cloned.1.call-update) | async-done | bytes 1900560 | tf_op jit(solution)/shard_map/all_gather | solution.py:149
  120.6 2.5 fusion.16
  123.1 2.2 fusion.17
  125.3 1.6 convolution_convert_fusion.6
  126.9 1.9 pad_maximum_fusion.1
  128.9 2.3 copy.24
  131.1 16.5 %all-to-all-start.1 = ((bf16[16,64,512]{2,1,0:T(8,128)(2,1)}), bf16[16,64,512]{2,1,0:T(8,128)(2,1)}, u32[]{:S(2)}, u32[]{:S(2)}) async-start(bf16[16,64,512]{2,1,0:T(8,128)(2,1)} %bitcast.85), calls=%async_computation.1 | async-start | bytes 2097152 | tf_op jit(solution)/shard_map/all_to_all | solution.py:248
  147.7 0.3 convolution_convert_fusion.5.refs_0_
  148.1 3.1 %copy-done = bf16[1,3584,1024]{2,1,0:T(8,128)(2,1)S(1)} copy-done((bf16[1,3584,1024]{2,1,0:T(8,128)(2,1)S(1)}, bf16[1,3584,1024]{2,1,0:T(8,128)(2,1)}, u32[]{:S(2)}) %copy-start) | copy-done | bytes 7340056
  151.1 5.3 %shard_map.93 = (bf16[48,4736]{1,0:T(8,128)(2,1)S(1)}, bf16[48,4736]{1,0:T(8,128)(2,1)S(1)}, bf16[48,4736]{1,0:T(8,128)(2,1)S(1)}, bf16[48,4736]{1,0:T(8,128)(2,1)S(1)}, bf16[192,1024]{1,0:T(8,128)(2,1)}) custom-call(f32[1,128]{1,0:T(1,128)S(1)} %compare_convert_fusion.mine_ref, bf16[48,4736]{1,0:T(8,128)(2,1)S(1)} %convolution_convert_fusion.5.refs_0_, ...), custom_call_target="tpu_custom_call" | custom-call | bytes 1024 | tf_op jit(solution)/shard_map/pallas_call | solution.py:96
  156.5 4.3 %collective-permute-start.5 = (bf16[48,4736]{1,0:T(8,128)(2,1)S(1)}, bf16[48,4736]{1,0:T(8,128)(2,1)S(1)}, u32[]{:S(2)}, u32[]{:S(2)}) collective-permute-start(bf16[48,4736]{1,0:T(8,128)(2,1)S(1)} %get-tuple-element.22), channel_id=1, source_target_pairs={{0,4},{2,6},{4,0},{6,2},{1,5},{3,7},{5,1},{7,3},{8,12},{10,14},{12... | collective-permute-start | bytes 1363976 | tf_op jit(solution)/shard_map/ppermute | solution.py:262
  160.7 2.6 %collective-permute-start.4 = (bf16[48,4736]{1,0:T(8,128)(2,1)S(1)}, bf16[48,4736]{1,0:T(8,128)(2,1)S(1)}, u32[]{:S(2)}, u32[]{:S(2)}) collective-permute-start(bf16[48,4736]{1,0:T(8,128)(2,1)S(1)} %get-tuple-element.21), channel_id=1, source_target_pairs={{0,6},{2,0},{4,2},{6,4},{1,7},{3,1},{5,3},{7,5},{8,14},{10,8},{12,... | collective-permute-start | bytes 1363976 | tf_op jit(solution)/shard_map/ppermute | solution.py:262
  163.4 12.4 %all-to-all-done.1 = bf16[16,64,512]{2,1,0:T(8,128)(2,1)} async-done(((bf16[16,64,512]{2,1,0:T(8,128)(2,1)}), bf16[16,64,512]{2,1,0:T(8,128)(2,1)}, u32[]{:S(2)}, u32[]{:S(2)}) %all-to-all-start.1) | async-done | bytes 1048608 | tf_op jit(solution)/shard_map/all_to_all | solution.py:248
  175.7 2.6 collective-permute-start.6
  178.3 1.6 fusion.21
  180.0 0.1 fusion.64
  180.2 1.3 collective-permute-done.4
  181.4 9.2 %collective-permute-done.6 = bf16[48,4736]{1,0:T(8,128)(2,1)S(1)} collective-permute-done((bf16[48,4736]{1,0:T(8,128)(2,1)S(1)}, bf16[48,4736]{1,0:T(8,128)(2,1)S(1)}, u32[]{:S(2)}, u32[]{:S(2)}) %collective-permute-start.6) | collective-permute-done | bytes 454688 | tf_op jit(solution)/shard_map/ppermute | solution.py:262
  190.6 1.5 fusion.1
  192.2 4.1 %all-to-all-start.2 = ((bf16[16,8,4736]{2,1,0:T(8,128)(2,1)}), bf16[16,8,4736]{2,1,0:T(8,128)(2,1)S(1)}, u32[]{:S(2)}, u32[]{:S(2)}) async-start(bf16[16,8,4736]{2,1,0:T(8,128)(2,1)} %fusion.1), calls=%async_computation.2 | async-start | bytes 2424832 | tf_op jit(solution)/shard_map/all_to_all | solution.py:273
  196.3 1.6 convolution_convert_fusion.7
  197.9 2.9 %collective-permute-start.10 = (bf16[8,48,512]{2,1,0:T(8,128)(2,1)S(1)}, bf16[8,48,512]{2,1,0:T(8,128)(2,1)S(1)}, u32[]{:S(2)}, u32[]{:S(2)}) collective-permute-start(bf16[8,48,512]{2,1,0:T(8,128)(2,1)S(1)} %convolution_convert_fusion.7), channel_id=1, source_target_pairs={{0,6},{2,0},{4,2},{6,4},{1,7},{3,1},{5,3},{7,5},{8,14},{10,8},{12,... | collective-permute-start | bytes 1179656 | tf_op jit(solution)/shard_map/ppermute | solution.py:292
  201.0 1.6 convolution_convert_fusion.8
  202.5 2.1 collective-permute-start.9
  204.7 0.1 fusion.66
  204.8 1.6 convolution_convert_fusion.9
  206.4 2.7 %collective-permute-start.8 = (bf16[8,48,512]{2,1,0:T(8,128)(2,1)S(1)}, bf16[8,48,512]{2,1,0:T(8,128)(2,1)S(1)}, u32[]{:S(2)}, u32[]{:S(2)}) collective-permute-start(bf16[8,48,512]{2,1,0:T(8,128)(2,1)S(1)} %convolution_convert_fusion.9), channel_id=1, source_target_pairs={{0,2},{2,4},{4,6},{6,0},{1,3},{3,5},{5,7},{7,1},{8,10},{10,12},{12... | collective-permute-start | bytes 1179656 | tf_op jit(solution)/shard_map/ppermute | solution.py:292
  209.1 0.1 fusion.67
  209.2 1.6 fusion.14
  210.8 5.6 %collective-permute-done.9 = bf16[8,48,512]{2,1,0:T(8,128)(2,1)S(1)} collective-permute-done((bf16[8,48,512]{2,1,0:T(8,128)(2,1)S(1)}, bf16[8,48,512]{2,1,0:T(8,128)(2,1)S(1)}, u32[]{:S(2)}, u32[]{:S(2)}) %collective-permute-start.9) | collective-permute-done | bytes 393248 | tf_op jit(solution)/shard_map/ppermute | solution.py:292
  216.4 9.1 %collective-permute-done.8 = bf16[8,48,512]{2,1,0:T(8,128)(2,1)S(1)} collective-permute-done((bf16[8,48,512]{2,1,0:T(8,128)(2,1)S(1)}, bf16[8,48,512]{2,1,0:T(8,128)(2,1)S(1)}, u32[]{:S(2)}, u32[]{:S(2)}) %collective-permute-start.8) | collective-permute-done | bytes 393248 | tf_op jit(solution)/shard_map/ppermute | solution.py:292
  225.5 0.2 pad_maximum_fusion
  225.8 1.8 all-to-all-done.2
  227.6 0.3 fusion.11
  227.9 4.6 %collective-permute-start.7 = (bf16[16,4736]{1,0:T(8,128)(2,1)S(1)}, bf16[16,4736]{1,0:T(8,128)(2,1)S(1)}, u32[]{:S(2)}, u32[]{:S(2)}) collective-permute-start(bf16[16,4736]{1,0:T(8,128)(2,1)S(1)} %slice.69), channel_id=1, source_target_pairs={{0,513},{128,641},{256,769},{384,897},{512,1},{640,129},{768,257},... | collective-permute-start | bytes 454664 | tf_op jit(solution)/shard_map/ppermute | solution.py:302
  232.5 12.3 %all-gather.5.cloned.1.call-done = bf16[1536,1024]{1,0:T(8,128)(2,1)} async-done(((bf16[192,1024]{1,0:T(8,128)(2,1)}), bf16[1536,1024]{1,0:T(8,128)(2,1)}) %all-gather.5.cloned.1.call-update) | async-done | bytes 3145744 | tf_op jit(solution)/shard_map/all_gather | solution.py:255
  244.8 4.7 %fusion.9 = f32[448,1024]{1,0:T(8,128)} fusion(bf16[1536,1024]{1,0:T(8,128)(2,1)} %all-gather.5.cloned.1.call-done, bf16[1536,512]{1,0:T(8,128)(2,1)S(1)} %bitcast.86), kind=kOutput, calls=%fused_computation.15 | convolution fusion | flops 1409286144 | bytes 6553600 | tf_op jit(solution)/shard_map/dot_general | solution.py:296
  249.6 0.6 slice.49
  250.2 0.7 slice.50
  250.8 0.2 select_reduce_fusion
  251.0 0.7 copy.27
  (60 shorter events, 1.1 us)
Async XLA Ops:
  10.4 31.1 %collective-permute-start = (bf16[16,4736]{1,0:T(8,128)(2,1)S(1)}, bf16[16,4736]{1,0:T(8,128)(2,1)S(1)}, u32[]{:S(2)}, u32[]{:S(2)}) collective-permute-start(bf16[16,4736]{1,0:T(8,128)(2,1)S(1)} %pad_maximum_fusion.2), channel_id=1, source_target_pairs={{0,513},{128,641},{256,769},{384,897},{512,1},{640,129},{768,257},... | collective-permute-start | bytes 454664 | tf_op jit(solution)/shard_map/ppermute | solution.py:147
  29.2 14.1 %copy-start.9 = (s32[128]{0:T(128)}, s32[128]{0:T(128)S(1)}, u32[]{:S(2)}) copy-start(s32[128]{0:T(128)S(1)} %get-tuple-element.48) | copy-start | bytes 1540
  29.2 14.1 %copy-start.10 = (s32[128]{0:T(128)}, s32[128]{0:T(128)S(1)}, u32[]{:S(2)}) copy-start(s32[128]{0:T(128)S(1)} %get-tuple-element.49) | copy-start | bytes 1540
  43.3 39.9 %all-to-all-start = ((bf16[16,8,4736]{2,1,0:T(8,128)(2,1)}), bf16[16,8,4736]{2,1,0:T(8,128)(2,1)S(1)}, u32[]{:S(2)}, u32[]{:S(2)}) async-start(bf16[16,8,4736]{2,1,0:T(8,128)(2,1)} %fusion), calls=%async_computation | async-start | bytes 2424832 | tf_op jit(solution)/shard_map/all_to_all | solution.py:170
  52.0 68.6 %all-gather.3.cloned.1.call-start = ((), (), s32[]{:S(2)}) async-start(), calls=%async_computation.3 | async-start | bytes 2019328 | tf_op jit(solution)/shard_map/all_gather | solution.py:149
  53.4 34.2 %copy-start.1 = (pred[8]{0:T(512)(128)(4,1)}, pred[8]{0:T(512)(128)(4,1)S(1)}, u32[]{:S(2)}) copy-start(pred[8]{0:T(512)(128)(4,1)S(1)} %get-tuple-element.50) | copy-start | bytes 28
  53.4 34.2 %copy-start.3 = (pred[8]{0:T(512)(128)(4,1)}, pred[8]{0:T(512)(128)(4,1)S(1)}, u32[]{:S(2)}) copy-start(pred[8]{0:T(512)(128)(4,1)S(1)} %get-tuple-element.51) | copy-start | bytes 28
  53.4 30.1 %copy-start.7 = (pred[8]{0:T(512)(128)(4,1)}, pred[8]{0:T(512)(128)(4,1)S(1)}, u32[]{:S(2)}) copy-start(pred[8]{0:T(512)(128)(4,1)S(1)} %get-tuple-element.53) | copy-start | bytes 28
  53.4 34.1 %copy-start.5 = (pred[8]{0:T(512)(128)(4,1)}, pred[8]{0:T(512)(128)(4,1)S(1)}, u32[]{:S(2)}) copy-start(pred[8]{0:T(512)(128)(4,1)S(1)} %get-tuple-element.52) | copy-start | bytes 28
  83.9 64.1 %collective-permute-start.1 = (bf16[48,4736]{1,0:T(8,128)(2,1)S(1)}, bf16[48,4736]{1,0:T(8,128)(2,1)S(1)}, u32[]{:S(2)}, u32[]{:S(2)}) collective-permute-start(bf16[48,4736]{1,0:T(8,128)(2,1)S(1)} %convolution_convert_fusion.4), channel_id=1, source_target_pairs={{0,2},{2,4},{4,6},{6,0},{1,3},{3,5},{5,7},{7,1},{8,10},{10,12},{12... | collective-permute-start | bytes 1363976 | tf_op jit(solution)/shard_map/ppermute | solution.py:244
  87.6 60.5 %collective-permute-start.2 = (bf16[48,4736]{1,0:T(8,128)(2,1)S(1)}, bf16[48,4736]{1,0:T(8,128)(2,1)S(1)}, u32[]{:S(2)}, u32[]{:S(2)}) collective-permute-start(bf16[48,4736]{1,0:T(8,128)(2,1)S(1)} %convolution_convert_fusion.3), channel_id=1, source_target_pairs={{0,4},{2,6},{4,0},{6,2},{1,5},{3,7},{5,1},{7,3},{8,12},{10,14},{12... | collective-permute-start | bytes 1363976 | tf_op jit(solution)/shard_map/ppermute | solution.py:244
  93.2 54.8 %collective-permute-start.3 = (bf16[48,4736]{1,0:T(8,128)(2,1)}, bf16[48,4736]{1,0:T(8,128)(2,1)S(1)}, u32[]{:S(2)}, u32[]{:S(2)}) collective-permute-start(bf16[48,4736]{1,0:T(8,128)(2,1)} %convolution_convert_fusion.2), channel_id=1, source_target_pairs={{0,6},{2,0},{4,2},{6,4},{1,7},{3,1},{5,3},{7,5},{8,14},{10,8},{12,... | collective-permute-start | bytes 1363976 | tf_op jit(solution)/shard_map/ppermute | solution.py:244
  131.1 44.6 %all-to-all-start.1 = ((bf16[16,64,512]{2,1,0:T(8,128)(2,1)}), bf16[16,64,512]{2,1,0:T(8,128)(2,1)}, u32[]{:S(2)}, u32[]{:S(2)}) async-start(bf16[16,64,512]{2,1,0:T(8,128)(2,1)} %bitcast.85), calls=%async_computation.1 | async-start | bytes 2097152 | tf_op jit(solution)/shard_map/all_to_all | solution.py:248
  147.7 97.1 %all-gather.5.cloned.1.call-start = ((), (), s32[]{:S(2)}) async-start(), calls=%async_computation.4 | async-start | bytes 3538944 | tf_op jit(solution)/shard_map/all_gather | solution.py:255
  148.1 3.1 %copy-start = (bf16[1,3584,1024]{2,1,0:T(8,128)(2,1)S(1)}, bf16[1,3584,1024]{2,1,0:T(8,128)(2,1)}, u32[]{:S(2)}) copy-start(bf16[1,3584,1024]{2,1,0:T(8,128)(2,1)} %refs_4_.1) | copy-start | bytes 22020100
  156.4 23.5 %copy-start.2 = (pred[8]{0:T(512)(128)(4,1)S(1)}, pred[8]{0:T(512)(128)(4,1)}, u32[]{:S(2)}) copy-start(pred[8]{0:T(512)(128)(4,1)} %copy-done.1) | copy-start | bytes 28
  156.4 23.5 %copy-start.4 = (pred[8]{0:T(512)(128)(4,1)S(1)}, pred[8]{0:T(512)(128)(4,1)}, u32[]{:S(2)}) copy-start(pred[8]{0:T(512)(128)(4,1)} %copy-done.3) | copy-start | bytes 28
  156.4 23.5 %copy-start.6 = (pred[8]{0:T(512)(128)(4,1)S(1)}, pred[8]{0:T(512)(128)(4,1)}, u32[]{:S(2)}) copy-start(pred[8]{0:T(512)(128)(4,1)} %copy-done.5) | copy-start | bytes 28
  156.4 23.5 %copy-start.8 = (pred[8]{0:T(512)(128)(4,1)S(1)}, pred[8]{0:T(512)(128)(4,1)}, u32[]{:S(2)}) copy-start(pred[8]{0:T(512)(128)(4,1)} %copy-done.7) | copy-start | bytes 28
  156.5 23.7 %collective-permute-start.5 = (bf16[48,4736]{1,0:T(8,128)(2,1)S(1)}, bf16[48,4736]{1,0:T(8,128)(2,1)S(1)}, u32[]{:S(2)}, u32[]{:S(2)}) collective-permute-start(bf16[48,4736]{1,0:T(8,128)(2,1)S(1)} %get-tuple-element.22), channel_id=1, source_target_pairs={{0,4},{2,6},{4,0},{6,2},{1,5},{3,7},{5,1},{7,3},{8,12},{10,14},{12... | collective-permute-start | bytes 1363976 | tf_op jit(solution)/shard_map/ppermute | solution.py:262
  160.7 20.7 %collective-permute-start.4 = (bf16[48,4736]{1,0:T(8,128)(2,1)S(1)}, bf16[48,4736]{1,0:T(8,128)(2,1)S(1)}, u32[]{:S(2)}, u32[]{:S(2)}) collective-permute-start(bf16[48,4736]{1,0:T(8,128)(2,1)S(1)} %get-tuple-element.21), channel_id=1, source_target_pairs={{0,6},{2,0},{4,2},{6,4},{1,7},{3,1},{5,3},{7,5},{8,14},{10,8},{12,... | collective-permute-start | bytes 1363976 | tf_op jit(solution)/shard_map/ppermute | solution.py:262
  175.7 14.9 %collective-permute-start.6 = (bf16[48,4736]{1,0:T(8,128)(2,1)S(1)}, bf16[48,4736]{1,0:T(8,128)(2,1)S(1)}, u32[]{:S(2)}, u32[]{:S(2)}) collective-permute-start(bf16[48,4736]{1,0:T(8,128)(2,1)S(1)} %get-tuple-element.25), channel_id=1, source_target_pairs={{0,2},{2,4},{4,6},{6,0},{1,3},{3,5},{5,7},{7,1},{8,10},{10,12},{12... | collective-permute-start | bytes 1363976 | tf_op jit(solution)/shard_map/ppermute | solution.py:262
  192.2 35.4 %all-to-all-start.2 = ((bf16[16,8,4736]{2,1,0:T(8,128)(2,1)}), bf16[16,8,4736]{2,1,0:T(8,128)(2,1)S(1)}, u32[]{:S(2)}, u32[]{:S(2)}) async-start(bf16[16,8,4736]{2,1,0:T(8,128)(2,1)} %fusion.1), calls=%async_computation.2 | async-start | bytes 2424832 | tf_op jit(solution)/shard_map/all_to_all | solution.py:273
  197.9 12.9 %collective-permute-start.10 = (bf16[8,48,512]{2,1,0:T(8,128)(2,1)S(1)}, bf16[8,48,512]{2,1,0:T(8,128)(2,1)S(1)}, u32[]{:S(2)}, u32[]{:S(2)}) collective-permute-start(bf16[8,48,512]{2,1,0:T(8,128)(2,1)S(1)} %convolution_convert_fusion.7), channel_id=1, source_target_pairs={{0,6},{2,0},{4,2},{6,4},{1,7},{3,1},{5,3},{7,5},{8,14},{10,8},{12,... | collective-permute-start | bytes 1179656 | tf_op jit(solution)/shard_map/ppermute | solution.py:292
  202.5 13.9 %collective-permute-start.9 = (bf16[8,48,512]{2,1,0:T(8,128)(2,1)S(1)}, bf16[8,48,512]{2,1,0:T(8,128)(2,1)S(1)}, u32[]{:S(2)}, u32[]{:S(2)}) collective-permute-start(bf16[8,48,512]{2,1,0:T(8,128)(2,1)S(1)} %convolution_convert_fusion.8), channel_id=1, source_target_pairs={{0,4},{2,6},{4,0},{6,2},{1,5},{3,7},{5,1},{7,3},{8,12},{10,14},{12... | collective-permute-start | bytes 1179656 | tf_op jit(solution)/shard_map/ppermute | solution.py:292
  206.4 19.1 %collective-permute-start.8 = (bf16[8,48,512]{2,1,0:T(8,128)(2,1)S(1)}, bf16[8,48,512]{2,1,0:T(8,128)(2,1)S(1)}, u32[]{:S(2)}, u32[]{:S(2)}) collective-permute-start(bf16[8,48,512]{2,1,0:T(8,128)(2,1)S(1)} %convolution_convert_fusion.9), channel_id=1, source_target_pairs={{0,2},{2,4},{4,6},{6,0},{1,3},{3,5},{5,7},{7,1},{8,10},{10,12},{12... | collective-permute-start | bytes 1179656 | tf_op jit(solution)/shard_map/ppermute | solution.py:292
  227.9 21.6 %collective-permute-start.7 = (bf16[16,4736]{1,0:T(8,128)(2,1)S(1)}, bf16[16,4736]{1,0:T(8,128)(2,1)S(1)}, u32[]{:S(2)}, u32[]{:S(2)}) collective-permute-start(bf16[16,4736]{1,0:T(8,128)(2,1)S(1)} %slice.69), channel_id=1, source_target_pairs={{0,513},{128,641},{256,769},{384,897},{512,1},{640,129},{768,257},... | collective-permute-start | bytes 454664 | tf_op jit(solution)/shard_map/ppermute | solution.py:302
Sparse Core Ops, SparseCore 0:
  55.5 65.1 all-gather.2
  156.6 88.1 all-gather.4

commit v5 on v4

--- a/solution.py
+++ b/solution.py
@@ -110,6 +110,97 @@
     return result[:count], result[count]
 
 
+def window_kernel(width, starts_ref, rows_ref, *refs):
+    outs, sems = refs[:-1], refs[-1]
+    window = outs[0].shape[1] - rows_ref.shape[1] + width
+    first = rows_ref.shape[1] - width
+    copies = []
+    for k, out in enumerate(outs):
+        start = pl.multiple_of(starts_ref[k], 128)
+        copies.append(
+            pltpu.make_async_copy(
+                rows_ref.at[:, pl.ds(start, window)], out.at[:, :window], sems.at[2 * k]
+            )
+        )
+        copies.append(
+            pltpu.make_async_copy(
+                rows_ref.at[:, pl.ds(width, first)], out.at[:, window:], sems.at[2 * k + 1]
+            )
+        )
+    for copy in copies:
+        copy.start()
+    for copy in copies:
+        copy.wait()
+
+
+def share_windows(rows, width, window, starts):
+    count = starts.shape[0]
+    wide = window + rows.shape[1] - width
+    return pl.pallas_call(
+        functools.partial(window_kernel, width),
+        out_shape=[jax.ShapeDtypeStruct((rows.shape[0], wide), rows.dtype)] * count,
+        in_specs=[pl.BlockSpec(memory_space=pltpu.SMEM), pl.BlockSpec(memory_space=pl.ANY)],
+        out_specs=[pl.BlockSpec(memory_space=pl.ANY)] * count,
+        scratch_shapes=[pltpu.SemaphoreType.DMA((2 * count,))],
+        cost_estimate=pl.CostEstimate(flops=0, bytes_accessed=1024, transcendentals=0),
+    )(starts, rows)
+
+
+def place_kernel(groups_ref, mask_ref, fold_ref, valid_ref, ends_ref, *refs):
+    pieces, out_ref = refs[:-1], refs[-1]
+    f32 = jnp.float32
+    bf = jnp.bfloat16
+    window = out_ref.shape[1]
+    tokens = jnp.concatenate([piece[...] for piece in pieces], axis=0)
+    gate = tokens[:, window:]
+    named = jnp.where(gate.astype(f32) != 0, 1.0, 0.0).astype(bf)
+    hits = lax.dot_general(
+        groups_ref[...], named, (((1,), (1,)), ((), ())), preferred_element_type=f32
+    )
+    hits = jnp.where(hits > 0, 1.0, 0.0)
+    values = jnp.where(valid_ref[...] > 0, tokens[:, :window].astype(f32), 0.0).astype(bf)
+    mask = mask_ref[...].astype(f32)
+    group_mask = groups_ref[...].astype(f32)
+    fold = fold_ref[...]
+    count = groups_ref.shape[0]
+    places = mask.shape[0]
+    for g in range(0, count, 4):
+        placing = jnp.concatenate(
+            [mask * hits[g + i : g + i + 1] for i in range(4)], axis=0
+        ).astype(bf)
+        part = jnp.dot(placing, values, preferred_element_type=f32)
+        row_gate = jnp.dot(placing, gate, preferred_element_type=f32)
+        row_gate = jnp.concatenate(
+            [
+                row_gate[i * places : (i + 1) * places] * group_mask[g + i : g + i + 1]
+                for i in range(4)
+            ],
+            axis=0,
+        ).astype(bf)
+        lanes = jnp.dot(row_gate, fold, preferred_element_type=f32)
+        here = slice(g * places, (g + 4) * places)
+        if window == 128:
+            out_ref[here, :] = (part + lanes).astype(bf)
+        else:
+            out_ref[here, :128] = (part[:, :128] + lanes * ends_ref[0:1, :]).astype(bf)
+            out_ref[here, 128 : window - 128] = part[:, 128 : window - 128].astype(bf)
+            out_ref[here, window - 128 :] = (
+                part[:, window - 128 :] + lanes * ends_ref[1:2, :]
+            ).astype(bf)
+
+
+def place_columns(pieces, window, groups, mask, fold, valid, ends):
+    vmem = pl.BlockSpec(memory_space=pltpu.VMEM)
+    return pl.pallas_call(
+        place_kernel,
+        out_shape=jax.ShapeDtypeStruct((groups.shape[0] * mask.shape[0], window), jnp.bfloat16),
+        in_specs=[vmem] * (5 + len(pieces)),
+        out_specs=vmem,
+        compiler_params=pltpu.CompilerParams(vmem_limit_bytes=24 * 1024 * 1024),
+        cost_estimate=pl.CostEstimate(flops=0, bytes_accessed=1024, transcendentals=0),
+    )(groups, mask, fold, valid, ends, *pieces)
+
+
 def on_device(activations, cotangent, gates, experts, groups, weights):
     reps = lax.axis_size("rep")
     nodes = lax.axis_size("node")
@@ -145,8 +236,6 @@
     own = jnp.concatenate([cotangent, activations, gate_wide], axis=1)
     wide = own.shape[1]
     other = lax.ppermute(own, ("rep", "half"), pairs)
-    own, other = lax.optimization_barrier((own, other))
-    along_z = lax.all_gather(own[:, hidden:], ("half", "rep"), axis=0, tiled=True)
     both = jnp.concatenate([own, other], axis=0)
 
     places = 2 * rows_one
@@ -171,7 +260,8 @@
         send_rows.reshape(nodes, 2 * blocks, wide), "node", 0, 0, tiled=True
     ).reshape(places, wide)
 
-    cap2 = -(-2 * cap // 16) * 16
+    filled = 2 * cap
+    cap2 = -(-filled // 16) * 16
     before = (place_index[:, None] < place_index[None, :]).astype(bf)
     slot_at = jnp.arange(cap2, dtype=jnp.int32).astype(f32)
 
@@ -199,59 +289,53 @@
         preferred_element_type=f32,
     ).astype(bf)
     ring_rows = reps * 2 * blocks
-    row_index = jnp.arange(nodes * ring_rows, dtype=jnp.int32)
-    token_index = jnp.arange(reps * 2 * tokens, dtype=jnp.int32)
-    token_rep = token_index // tokens % reps
-    token_block = token_index % tokens // block
-    token_place = jnp.where(
-        token_index // (tokens * reps) == half_at,
-        token_rep * 2 * blocks + token_block,
-        (token_rep + reps // 2) % reps * 2 * blocks + blocks + token_block,
-    )
+    window = -(-share // 128) * 128
+    offset = rep_at * share % 128
+    gate_start = jnp.where(offset == 0, share, 0)
+    lane = jnp.arange(window, dtype=jnp.int32)
+    steps = jnp.arange(reps, dtype=jnp.int32)
+    pieces = share_windows(
+        both[:, hidden:], width, window, (rep_at + steps) % reps * share // 128 * 128
+    )
+    pieces = [pieces[0]] + [
+        lax.ppermute(pieces[k], "rep", ring(reps, k)) for k in range(1, reps)
+    ]
+    token_place = (
+        ((rep_at + reps - steps) % reps * 2 * blocks)[:, None]
+        + (jnp.arange(2 * tokens, dtype=jnp.int32) // block)[None, :]
+    ).reshape(reps * 2 * tokens)
     expert_index = jnp.arange(total, dtype=jnp.int32)
-    row_expert = (row_index // ring_rows)[:, None] == (expert_index // locals_)[None, :]
-    ring_gates = along_z[:, width:]
-    row_hit = lax.dot_general(
-        row_expert.astype(bf),
-        (ring_gates != 0).astype(bf),
-        (((1,), (1,)), ((), ())),
-        preferred_element_type=f32,
-    )
-    ring_placing = (
-        (row_hit > 0) & ((row_index % ring_rows)[:, None] == token_place[None, :])
-    ).astype(bf)
-    spare = -share % 128
-    fold = ((expert_index % locals_)[:, None] == jnp.arange(spare)[None, :]).astype(bf)
-    row_gates = jnp.where(
-        row_expert, jnp.dot(ring_placing, ring_gates, preferred_element_type=f32), 0.0
-    ).astype(bf)
-    cols = jnp.concatenate(
-        [
-            jnp.dot(
-                ring_placing,
-                lax.dynamic_slice_in_dim(along_z, rep_at * share, share, 1),
-                preferred_element_type=f32,
-            ),
-            jnp.dot(row_gates, fold, preferred_element_type=f32),
-        ],
-        axis=1,
-    ).astype(bf)
-
+    cols = place_columns(
+        pieces,
+        window,
+        (jnp.arange(nodes)[:, None] == (expert_index // locals_)[None, :]).astype(bf),
+        (jnp.arange(ring_rows)[:, None] == token_place[None, :]).astype(bf),
+        (
+            jnp.arange(128)[None, :] == (gate_start % 128 + expert_index % locals_)[:, None]
+        ).astype(bf),
+        ((lane >= offset) & (lane < offset + share)).astype(f32)[None, :],
+        jnp.stack([jnp.where(offset == 0, 0.0, 1.0), jnp.where(offset == 0, 1.0, 0.0)])[
+            :, None
+        ]
+        * jnp.ones((2, 128), f32),
+    )
+
+    rows, group_gates, cols = lax.optimization_barrier((rows, group_gates, cols))
     picker = pickers(group_gates)
     sent = [
         jnp.dot(p, rows, preferred_element_type=f32).astype(bf) for p in picker[1:]
     ]
     moved = [lax.ppermute(sent[j - 1], "x", ring(xs, j)) for j in range(1, xs)]
-    kept, cols = lax.optimization_barrier((picker[0], cols))
+    kept = picker[0]
     slabs = [jnp.dot(kept, rows, preferred_element_type=f32).astype(bf)] + moved
-    taken = xs * cap2
     cols = lax.all_to_all(
-        cols.reshape(nodes, ring_rows, share + spare), "node", 0, 0, tiled=True
+        cols.reshape(nodes, ring_rows, window), "node", 0, 0, tiled=True
     )
 
     mine = jnp.arange(total, dtype=jnp.int32) == node_at * locals_ + x_at * 2 + half_at
     back, grad_pre = expert(slabs, weights, mine.astype(f32)[None, :])
 
+    grad_pre = grad_pre.reshape(xs, cap2, hidden)[:, :filled].reshape(xs * filled, hidden)
     gathered = lax.all_gather(grad_pre, "rep", axis=0, tiled=True)
 
     last = xs - 1
@@ -275,13 +359,12 @@
     ).reshape(places, wide)
 
     cols = (
-        cols.reshape(nodes, reps, 2 * blocks, share + spare)
+        cols.reshape(nodes, reps, 2 * blocks, window)
         .transpose(1, 0, 2, 3)
-        .reshape(reps, places, share + spare)
+        .reshape(reps, places, window)
     )
     gate_lane = (
-        share + jnp.arange(locals_, dtype=jnp.int32)[:, None]
-        == jnp.arange(share + spare, dtype=jnp.int32)[None, :]
+        gate_start + jnp.arange(locals_, dtype=jnp.int32)[:, None] == lane[None, :]
     ).astype(bf)
     all_gates = jnp.einsum("lc,prc->plr", gate_lane, cols, preferred_element_type=f32)
     share_sent = [
@@ -291,8 +374,10 @@
     share_rows = [share_sent[0]] + [
         lax.ppermute(share_sent[j], "x", ring(xs, j)) for j in range(1, xs)
     ]
-    x_cols = jnp.stack(share_rows, axis=1).reshape(reps * taken, cols.shape[2])
-    x_cols = x_cols[:, :share]
+    x_cols = jnp.stack([part[:, :filled] for part in share_rows], axis=1)
+    x_cols = lax.dynamic_slice_in_dim(
+        x_cols.reshape(reps * xs * filled, window), offset, share, 1
+    )
     grad_share = lax.dot_general(
         x_cols, gathered, (((0,), (0,)), ((), ())), preferred_element_type=f32
     )

time: 261 us -> 252 us (0.966)
  waiting for transfers between devices: 117 us -> 69 us
  starting transfers between devices: 80.5 us -> 110 us
  Pallas kernels: 5.25 us -> 19.4 us
  matrix products: 25.9 us -> 21.7 us
    ppermute x0 -> x7, starting transfers between devices: none -> 29.9 us  [on_device(): lax.ppermute(pieces[k], 'rep', ring(reps, k))]
    all_to_all x1, waiting for transfers between devices: 29.2 us -> 0.01 us  [on_device(): lax.all_to_all(send_rows.reshape(nodes, 2 * blocks, wide), 'node', 0, 0,...]
    all_gather x1 -> x0, waiting for transfers between devices: 24.1 us -> none  [on_device(): lax.all_gather(own[:, hidden:], ('half', 'rep'), axis=0, tiled=True)]
    ppermute x3, waiting for transfers between devices: 0.01 us -> 15.8 us  [on_device(): moved = [lax.ppermute(sent[j - 1], 'x', ring(xs, j)) for j in range(1, xs)]]
    pallas_call x0 -> x2, Pallas kernels: none -> 14.2 us  [the longest x1 11.8 us: share_windows(): pl.pallas_call(functools.partial(window_kernel, width), out_shape=[jax.Sh...]
    all_to_all x1, waiting for transfers between devices: 1.79 us -> 14.5 us  [on_device(): lax.all_to_all(back_rows.reshape(nodes, 2 * blocks, wide), 'node', 0, 0,...]
    all_to_all x1, waiting for transfers between devices: 12.4 us -> 0.01 us  [on_device(): lax.all_to_all(cols.reshape(nodes, ring_rows, window), 'node', 0, 0, tile...]
    ppermute x3, waiting for transfers between devices: 10.5 us -> 2.14 us  [on_device(): lax.ppermute(back_last if j == last else back[j], 'x', ring(xs, -j))]
  transfers between devices with their start and end apart: 16 -> 22, of which waited for: 10 -> 8; matrix products, arithmetic and copies ran while one was open for 12% -> 9% of each run, Pallas kernels for 2% -> 8%
where the time goes in v5:
time: 252 us; the launch traced here: 249 us
  starting transfers between devices  110 us (44%)
  waiting for transfers between devices  69 us (27%)
  matrix products  21.7 us (9%)
  Pallas kernels  19.4 us (8%)
  between operations  14.5 us (6%)
  local copies, waits for them, and re-layouts  9.16 us (4%)
  other arithmetic  4.74 us (2%)
    ppermute x7, starting transfers between devices, on_device(): lax.ppermute(pieces[k], 'rep', ring(reps, k))  29.9 us
    ppermute x1, starting transfers between devices, on_device(): other = lax.ppermute(own, ('rep', 'half'), pairs)  18.7 us
    ppermute x3, waiting for transfers between devices, on_device(): moved = [lax.ppermute(sent[j - 1], 'x', ring(xs, j)) for j in range(1, xs)]  15.8 us
    all_to_all x1, waiting for transfers between devices, on_device(): lax.all_to_all(back_rows.reshape(nodes, 2 * blocks, wide), 'node', 0, 0,...  14.5 us
    all_gather x1, waiting for transfers between devices, on_device(): gathered = lax.all_gather(grad_pre, 'rep', axis=0, tiled=True)  14.1 us
    ppermute x1, waiting for transfers between devices, on_device(): other = lax.ppermute(own, ('rep', 'half'), pairs)  12.3 us
    pallas_call x1, Pallas kernels, share_windows(): pl.pallas_call(functools.partial(window_kernel, width), out_shape=[jax.Sh...  11.8 us
    ppermute x3, starting transfers between devices, on_device(): lax.ppermute(back_last if j == last else back[j], 'x', ring(xs, -j))  10.7 us
  transfers between devices with their start and end apart: 22, of which 8 were waited for; matrix products, arithmetic and copies ran while one was open for 9% of the time, Pallas kernels for 8%

profile of v5, /device:TPU:1, one launch (start us, length us, event | category | flops | bytes accessed | tf_op | source)
XLA Modules:
  0.0 248.7 jit_solution(8270926096983192603)
XLA Ops:
  7.2 0.8 copy.18
  7.9 0.7 broadcast_multiply_fusion
  8.6 0.7 add.176
  9.5 0.9 pad_maximum_fusion.2
  10.4 18.7 %collective-permute-start = (bf16[16,4736]{1,0:T(8,128)(2,1)S(1)}, bf16[16,4736]{1,0:T(8,128)(2,1)S(1)}, u32[]{:S(2)}, u32[]{:S(2)}) collective-permute-start(bf16[16,4736]{1,0:T(8,128)(2,1)S(1)} %pad_maximum_fusion.2), channel_id=1, source_target_pairs={{0,513},{128,641},{256,769},{384,897},{512,1},{640,129},{768,257},... | collective-permute-start | bytes 454664 | tf_op jit(solution)/shard_map/ppermute | solution.py:238
  29.2 12.3 %collective-permute-done = bf16[16,4736]{1,0:T(8,128)(2,1)S(1)} collective-permute-done((bf16[16,4736]{1,0:T(8,128)(2,1)S(1)}, bf16[16,4736]{1,0:T(8,128)(2,1)S(1)}, u32[]{:S(2)}, u32[]{:S(2)}) %collective-permute-start) | collective-permute-done | bytes 151584 | tf_op jit(solution)/shard_map/ppermute | solution.py:238
  41.5 0.2 fusion.17
  41.7 2.5 fusion
  44.2 8.8 %all-to-all-start = ((bf16[16,8,4736]{2,1,0:T(8,128)(2,1)}), bf16[16,8,4736]{2,1,0:T(8,128)(2,1)S(1)}, u32[]{:S(2)}, u32[]{:S(2)}) async-start(bf16[16,8,4736]{2,1,0:T(8,128)(2,1)} %fusion), calls=%async_computation | async-start | bytes 2424832 | tf_op jit(solution)/shard_map/all_to_all | solution.py:259
  53.1 0.5 fusion.112.starts_ref
  53.8 0.7 pad_maximum_fusion.1.rows_ref
  54.6 11.8 %shard_map.93 = (bf16[32,640]{1,0:T(8,128)(2,1)}, bf16[32,640]{1,0:T(8,128)(2,1)}, bf16[32,640]{1,0:T(8,128)(2,1)}, bf16[32,640]{1,0:T(8,128)(2,1)}, bf16[32,640...) custom-call(s32[8]{0:T(128)} %fusion.112.starts_ref, ...), custom_call_target="tpu_custom_call" | custom-call | bytes 1024 | tf_op jit(solution)/shard_map/pallas_call | solution.py:139
  66.4 1.9 collective-permute-start.1
  68.3 5.9 %collective-permute-start.2 = (bf16[32,640]{1,0:T(8,128)(2,1)}, bf16[32,640]{1,0:T(8,128)(2,1)S(1)}, u32[]{:S(2)}, u32[]{:S(2)}) collective-permute-start(bf16[32,640]{1,0:T(8,128)(2,1)} %get-tuple-element.26), channel_id=1, source_target_pairs={{0,256},{128,384},{256,512},{384,640},{512,768},{640,896},{768,0},... | collective-permute-start | bytes 122888 | tf_op jit(solution)/shard_map/ppermute | solution.py:301
  74.3 1.9 collective-permute-start.3
  76.2 6.2 %collective-permute-start.4 = (bf16[32,640]{1,0:T(8,128)(2,1)}, bf16[32,640]{1,0:T(8,128)(2,1)S(1)}, u32[]{:S(2)}, u32[]{:S(2)}) collective-permute-start(bf16[32,640]{1,0:T(8,128)(2,1)} %get-tuple-element.28), channel_id=1, source_target_pairs={{0,512},{128,640},{256,768},{384,896},{512,0},{640,128},{768,256},... | collective-permute-start | bytes 122888 | tf_op jit(solution)/shard_map/ppermute | solution.py:301
  82.5 3.8 %collective-permute-start.5 = (bf16[32,640]{1,0:T(8,128)(2,1)}, bf16[32,640]{1,0:T(8,128)(2,1)S(1)}, u32[]{:S(2)}, u32[]{:S(2)}) collective-permute-start(bf16[32,640]{1,0:T(8,128)(2,1)} %get-tuple-element.29), channel_id=1, source_target_pairs={{0,640},{128,768},{256,896},{384,0},{512,128},{640,256},{768,384},... | collective-permute-start | bytes 122888 | tf_op jit(solution)/shard_map/ppermute | solution.py:301
  86.3 6.1 %collective-permute-start.6 = (bf16[32,640]{1,0:T(8,128)(2,1)}, bf16[32,640]{1,0:T(8,128)(2,1)S(1)}, u32[]{:S(2)}, u32[]{:S(2)}) collective-permute-start(bf16[32,640]{1,0:T(8,128)(2,1)} %get-tuple-element.30), channel_id=1, source_target_pairs={{0,768},{128,896},{256,0},{384,128},{512,256},{640,384},{768,512},... | collective-permute-start | bytes 122888 | tf_op jit(solution)/shard_map/ppermute | solution.py:301
  92.5 4.0 %collective-permute-start.7 = (bf16[32,640]{1,0:T(8,128)(2,1)}, bf16[32,640]{1,0:T(8,128)(2,1)S(1)}, u32[]{:S(2)}, u32[]{:S(2)}) collective-permute-start(bf16[32,640]{1,0:T(8,128)(2,1)} %get-tuple-element.31), channel_id=1, source_target_pairs={{0,896},{128,0},{256,128},{384,256},{512,384},{640,512},{768,640},... | collective-permute-start | bytes 122888 | tf_op jit(solution)/shard_map/ppermute | solution.py:301
  96.6 1.3 collective-permute-done.7.refs_7_
  97.9 0.8 copy-done.1
  98.7 2.3 shard_map.94
  101.0 0.2 convolution_convert_fusion.9
  101.3 0.1 convolution_bitcast_fusion.2
  101.4 0.4 convolution_convert_fusion.4
  101.8 3.1 %collective-permute-start.8 = (bf16[48,4736]{1,0:T(8,128)(2,1)S(1)}, bf16[48,4736]{1,0:T(8,128)(2,1)S(1)}, u32[]{:S(2)}, u32[]{:S(2)}) collective-permute-start(bf16[48,4736]{1,0:T(8,128)(2,1)S(1)} %convolution_convert_fusion.4), channel_id=1, source_target_pairs={{0,2},{2,4},{4,6},{6,0},{1,3},{3,5},{5,7},{7,1},{8,10},{10,12},{12... | collective-permute-start | bytes 1363976 | tf_op jit(solution)/shard_map/ppermute | solution.py:328
  104.9 9.8 %all-to-all-start.1 = ((bf16[16,64,512]{2,1,0:T(8,128)(2,1)}), bf16[16,64,512]{2,1,0:T(8,128)(2,1)}, u32[]{:S(2)}, u32[]{:S(2)}) async-start(bf16[16,64,512]{2,1,0:T(8,128)(2,1)} %bitcast.13), calls=%async_computation.1 | async-start | bytes 2097152 | tf_op jit(solution)/shard_map/all_to_all | solution.py:331
  114.7 0.1 convolution_bitcast_fusion.1
  114.9 0.4 convolution_convert_fusion.3
  115.2 4.4 %collective-permute-start.9 = (bf16[48,4736]{1,0:T(8,128)(2,1)S(1)}, bf16[48,4736]{1,0:T(8,128)(2,1)S(1)}, u32[]{:S(2)}, u32[]{:S(2)}) collective-permute-start(bf16[48,4736]{1,0:T(8,128)(2,1)S(1)} %convolution_convert_fusion.3), channel_id=1, source_target_pairs={{0,4},{2,6},{4,0},{6,2},{1,5},{3,7},{5,1},{7,3},{8,12},{10,14},{12... | collective-permute-start | bytes 1363976 | tf_op jit(solution)/shard_map/ppermute | solution.py:328
  119.7 0.4 convolution_convert_fusion.2
  120.1 3.1 %collective-permute-start.10 = (bf16[48,4736]{1,0:T(8,128)(2,1)S(1)}, bf16[48,4736]{1,0:T(8,128)(2,1)S(1)}, u32[]{:S(2)}, u32[]{:S(2)}) collective-permute-start(bf16[48,4736]{1,0:T(8,128)(2,1)S(1)} %convolution_convert_fusion.2), channel_id=1, source_target_pairs={{0,6},{2,0},{4,2},{6,4},{1,7},{3,1},{5,3},{7,5},{8,14},{10,8},{12,... | collective-permute-start | bytes 1363976 | tf_op jit(solution)/shard_map/ppermute | solution.py:328
  123.3 0.4 convolution_convert_fusion.5.refs_0_
  123.7 6.9 %collective-permute-done.9.refs_2_ = bf16[48,4736]{1,0:T(8,128)(2,1)S(1)} collective-permute-done((bf16[48,4736]{1,0:T(8,128)(2,1)S(1)}, bf16[48,4736]{1,0:T(8,128)(2,1)S(1)}, u32[]{:S(2)}, u32[]{:S(2)}) %collective-permute-start.9) | collective-permute-done | bytes 454688 | tf_op jit(solution)/shard_map/ppermute | solution.py:328
  130.6 8.9 %collective-permute-done.10.refs_3_ = bf16[48,4736]{1,0:T(8,128)(2,1)S(1)} collective-permute-done((bf16[48,4736]{1,0:T(8,128)(2,1)S(1)}, bf16[48,4736]{1,0:T(8,128)(2,1)S(1)}, u32[]{:S(2)}, u32[]{:S(2)}) %collective-permute-start.10) | collective-permute-done | bytes 454688 | tf_op jit(solution)/shard_map/ppermute | solution.py:328
  139.5 3.1 %copy-done = bf16[1,3584,1024]{2,1,0:T(8,128)(2,1)S(1)} copy-done((bf16[1,3584,1024]{2,1,0:T(8,128)(2,1)S(1)}, bf16[1,3584,1024]{2,1,0:T(8,128)(2,1)}, u32[]{:S(2)}) %copy-start) | copy-done | bytes 7340056
  142.5 5.3 %shard_map.95 = (bf16[48,4736]{1,0:T(8,128)(2,1)S(1)}, bf16[48,4736]{1,0:T(8,128)(2,1)S(1)}, bf16[48,4736]{1,0:T(8,128)(2,1)S(1)}, bf16[48,4736]{1,0:T(8,128)(2,1)S(1)}, bf16[192,1024]{1,0:T(8,128)(2,1)S(1)}) custom-call(f32[1,128]{1,0:T(1,128)S(1)} %compare_convert_fusion.mine_ref, bf16[48,4736]{1,0:T(8,128)(2,1)S(1)} %convolution_convert_fusion.5.refs_0_, ...), custom_call_target="tpu_custom_call" | custom-call | bytes 1024 | tf_op jit(solution)/shard_map/pallas_call | solution.py:96
  147.8 0.9 reshape.237
  148.8 4.7 %collective-permute-start.12 = (bf16[48,4736]{1,0:T(8,128)(2,1)S(1)}, bf16[48,4736]{1,0:T(8,128)(2,1)}, u32[]{:S(2)}, u32[]{:S(2)}) collective-permute-start(bf16[48,4736]{1,0:T(8,128)(2,1)S(1)} %get-tuple-element.36), channel_id=1, source_target_pairs={{0,4},{2,6},{4,0},{6,2},{1,5},{3,7},{5,1},{7,3},{8,12},{10,14},{12... | collective-permute-start | bytes 1363976 | tf_op jit(solution)/shard_map/ppermute | solution.py:346
  153.5 4.1 %collective-permute-start.11 = (bf16[48,4736]{1,0:T(8,128)(2,1)S(1)}, bf16[48,4736]{1,0:T(8,128)(2,1)}, u32[]{:S(2)}, u32[]{:S(2)}) collective-permute-start(bf16[48,4736]{1,0:T(8,128)(2,1)S(1)} %get-tuple-element.35), channel_id=1, source_target_pairs={{0,6},{2,0},{4,2},{6,4},{1,7},{3,1},{5,3},{7,5},{8,14},{10,8},{12,... | collective-permute-start | bytes 1363976 | tf_op jit(solution)/shard_map/ppermute | solution.py:346
  157.6 1.9 collective-permute-start.13
  159.5 1.6 fusion.16
  161.4 1.6 convolution_convert_fusion.6
  162.9 4.6 %collective-permute-start.17 = (bf16[8,48,512]{2,1,0:T(8,128)(2,1)S(1)}, bf16[8,48,512]{2,1,0:T(8,128)(2,1)S(1)}, u32[]{:S(2)}, u32[]{:S(2)}) collective-permute-start(bf16[8,48,512]{2,1,0:T(8,128)(2,1)S(1)} %convolution_convert_fusion.6), channel_id=1, source_target_pairs={{0,6},{2,0},{4,2},{6,4},{1,7},{3,1},{5,3},{7,5},{8,14},{10,8},{12,... | collective-permute-start | bytes 1179656 | tf_op jit(solution)/shard_map/ppermute | solution.py:375
  167.7 2.3 convolution_convert_fusion.7
  170.0 1.9 collective-permute-start.16
  172.0 2.1 collective-permute-done.11
  174.2 2.7 %fusion.1 = bf16[16,8,4736]{2,1,0:T(8,128)(2,1)} fusion(bf16[48,4736]{1,0:T(8,128)(2,1)S(1)} %collective-permute-done.13, bf16[48,4736]{1,0:T(8,128)(2,1)} %collective-permute-done.12, bf16[48,4736]{1,0:T(8,128)(2,1)} %collective-permute-done.11, bf16[48,4736]{1,0:T(8,128)(2,1)S(1)} %get-tuple-element.34, pred[48,128]{1,0:T(8,128)(4,1)S(1)} %get-tuple-element.61, ...), kind=kOutput, calls=%fused_computation.3 | convolution fusion | flops 240738304 | bytes 3055616 | tf_op jit(solution)/shard_map/dot_general | solution.py:351
  176.9 8.9 %all-to-all-start.2 = ((bf16[16,8,4736]{2,1,0:T(8,128)(2,1)}), bf16[16,8,4736]{2,1,0:T(8,128)(2,1)S(1)}, u32[]{:S(2)}, u32[]{:S(2)}) async-start(bf16[16,8,4736]{2,1,0:T(8,128)(2,1)} %fusion.1), calls=%async_computation.2 | async-start | bytes 2424832 | tf_op jit(solution)/shard_map/all_to_all | solution.py:357
  185.8 1.6 convolution_convert_fusion.8
  187.4 3.1 %collective-permute-start.15 = (bf16[8,48,512]{2,1,0:T(8,128)(2,1)S(1)}, bf16[8,48,512]{2,1,0:T(8,128)(2,1)S(1)}, u32[]{:S(2)}, u32[]{:S(2)}) collective-permute-start(bf16[8,48,512]{2,1,0:T(8,128)(2,1)S(1)} %convolution_convert_fusion.8), channel_id=1, source_target_pairs={{0,2},{2,4},{4,6},{6,0},{1,3},{3,5},{5,7},{7,1},{8,10},{10,12},{12... | collective-permute-start | bytes 1179656 | tf_op jit(solution)/shard_map/ppermute | solution.py:375
  190.7 1.6 fusion.21
  192.3 8.9 %collective-permute-done.15 = bf16[8,48,512]{2,1,0:T(8,128)(2,1)S(1)} collective-permute-done((bf16[8,48,512]{2,1,0:T(8,128)(2,1)S(1)}, bf16[8,48,512]{2,1,0:T(8,128)(2,1)S(1)}, u32[]{:S(2)}, u32[]{:S(2)}) %collective-permute-start.15) | collective-permute-done | bytes 393248 | tf_op jit(solution)/shard_map/ppermute | solution.py:375
  201.3 0.2 pad_maximum_fusion
  201.6 1.3 reshape.235
  202.9 14.5 %all-to-all-done.2 = bf16[16,8,4736]{2,1,0:T(8,128)(2,1)S(1)} async-done(((bf16[16,8,4736]{2,1,0:T(8,128)(2,1)}), bf16[16,8,4736]{2,1,0:T(8,128)(2,1)S(1)}, u32[]{:S(2)}, u32[]{:S(2)}) %all-to-all-start.2) | async-done | bytes 1212448 | tf_op jit(solution)/shard_map/all_to_all | solution.py:357
  217.4 0.3 fusion.11
  217.7 3.1 %collective-permute-start.14 = (bf16[16,4736]{1,0:T(8,128)(2,1)S(1)}, bf16[16,4736]{1,0:T(8,128)(2,1)S(1)}, u32[]{:S(2)}, u32[]{:S(2)}) collective-permute-start(bf16[16,4736]{1,0:T(8,128)(2,1)S(1)} %slice.76), channel_id=1, source_target_pairs={{0,513},{128,641},{256,769},{384,897},{512,1},{640,129},{768,257},... | collective-permute-start | bytes 454664 | tf_op jit(solution)/shard_map/ppermute | solution.py:387
  220.9 14.1 %all-gather.2.cloned.1.call-done = bf16[1344,1024]{1,0:T(8,128)(2,1)} async-done(((bf16[168,1024]{1,0:T(8,128)(2,1)}), bf16[1344,1024]{1,0:T(8,128)(2,1)}) %all-gather.2.cloned.1.call-update) | async-done | bytes 2752528 | tf_op jit(solution)/shard_map/all_gather | solution.py:339
  234.9 4.7 %fusion.9 = f32[448,1024]{1,0:T(8,128)} fusion(bf16[1344,1024]{1,0:T(8,128)(2,1)} %all-gather.2.cloned.1.call-done, bf16[1344,512]{1,0:T(8,128)(2,1)S(1)} %copy-done.3, s32[]{:T(128)S(6)} %select_n.179), kind=kOutput, calls=%fused_computation.16 | convolution fusion | flops 1233125376 | bytes 5963780 | tf_op jit(solution)/shard_map/dot_general | solution.py:381
  239.7 0.6 slice.63
  240.3 0.7 slice.64
  241.0 0.2 select_reduce_fusion
  241.2 0.7 copy.21
  (71 shorter events, 2.2 us)
Async XLA Ops:
  10.4 31.1 %collective-permute-start = (bf16[16,4736]{1,0:T(8,128)(2,1)S(1)}, bf16[16,4736]{1,0:T(8,128)(2,1)S(1)}, u32[]{:S(2)}, u32[]{:S(2)}) collective-permute-start(bf16[16,4736]{1,0:T(8,128)(2,1)S(1)} %pad_maximum_fusion.2), channel_id=1, source_target_pairs={{0,513},{128,641},{256,769},{384,897},{512,1},{640,129},{768,257},... | collective-permute-start | bytes 454664 | tf_op jit(solution)/shard_map/ppermute | solution.py:238
  44.2 9.7 %copy-start.2 = (bf16[16,3584]{1,0:T(8,128)(2,1)S(1)}, bf16[16,3584]{1,0:T(8,128)(2,1)}, u32[]{:S(2)}) copy-start(bf16[16,3584]{1,0:T(8,128)(2,1)} %param.6) | copy-start | bytes 344068
  44.2 9.7 %copy-start.4 = (bf16[16,1024]{1,0:T(8,128)(2,1)S(1)}, bf16[16,1024]{1,0:T(8,128)(2,1)}, u32[]{:S(2)}) copy-start(bf16[16,1024]{1,0:T(8,128)(2,1)} %param.7) | copy-start | bytes 98308
  44.2 56.9 %all-to-all-start = ((bf16[16,8,4736]{2,1,0:T(8,128)(2,1)}), bf16[16,8,4736]{2,1,0:T(8,128)(2,1)S(1)}, u32[]{:S(2)}, u32[]{:S(2)}) async-start(bf16[16,8,4736]{2,1,0:T(8,128)(2,1)} %fusion), calls=%async_computation | async-start | bytes 2424832 | tf_op jit(solution)/shard_map/all_to_all | solution.py:259
  66.4 19.9 %collective-permute-start.1 = (bf16[32,640]{1,0:T(8,128)(2,1)}, bf16[32,640]{1,0:T(8,128)(2,1)S(1)}, u32[]{:S(2)}, u32[]{:S(2)}) collective-permute-start(bf16[32,640]{1,0:T(8,128)(2,1)} %get-tuple-element.25), channel_id=1, source_target_pairs={{0,128},{128,256},{256,384},{384,512},{512,640},{640,768},{768,896... | collective-permute-start | bytes 122888 | tf_op jit(solution)/shard_map/ppermute | solution.py:301
  68.3 24.1 %collective-permute-start.2 = (bf16[32,640]{1,0:T(8,128)(2,1)}, bf16[32,640]{1,0:T(8,128)(2,1)S(1)}, u32[]{:S(2)}, u32[]{:S(2)}) collective-permute-start(bf16[32,640]{1,0:T(8,128)(2,1)} %get-tuple-element.26), channel_id=1, source_target_pairs={{0,256},{128,384},{256,512},{384,640},{512,768},{640,896},{768,0},... | collective-permute-start | bytes 122888 | tf_op jit(solution)/shard_map/ppermute | solution.py:301
  74.3 22.2 %collective-permute-start.3 = (bf16[32,640]{1,0:T(8,128)(2,1)}, bf16[32,640]{1,0:T(8,128)(2,1)S(1)}, u32[]{:S(2)}, u32[]{:S(2)}) collective-permute-start(bf16[32,640]{1,0:T(8,128)(2,1)} %get-tuple-element.27), channel_id=1, source_target_pairs={{0,384},{128,512},{256,640},{384,768},{512,896},{640,0},{768,128},... | collective-permute-start | bytes 122888 | tf_op jit(solution)/shard_map/ppermute | solution.py:301
  76.2 20.3 %collective-permute-start.4 = (bf16[32,640]{1,0:T(8,128)(2,1)}, bf16[32,640]{1,0:T(8,128)(2,1)S(1)}, u32[]{:S(2)}, u32[]{:S(2)}) collective-permute-start(bf16[32,640]{1,0:T(8,128)(2,1)} %get-tuple-element.28), channel_id=1, source_target_pairs={{0,512},{128,640},{256,768},{384,896},{512,0},{640,128},{768,256},... | collective-permute-start | bytes 122888 | tf_op jit(solution)/shard_map/ppermute | solution.py:301
  82.5 14.1 %collective-permute-start.5 = (bf16[32,640]{1,0:T(8,128)(2,1)}, bf16[32,640]{1,0:T(8,128)(2,1)S(1)}, u32[]{:S(2)}, u32[]{:S(2)}) collective-permute-start(bf16[32,640]{1,0:T(8,128)(2,1)} %get-tuple-element.29), channel_id=1, source_target_pairs={{0,640},{128,768},{256,896},{384,0},{512,128},{640,256},{768,384},... | collective-permute-start | bytes 122888 | tf_op jit(solution)/shard_map/ppermute | solution.py:301
  86.3 10.2 %collective-permute-start.6 = (bf16[32,640]{1,0:T(8,128)(2,1)}, bf16[32,640]{1,0:T(8,128)(2,1)S(1)}, u32[]{:S(2)}, u32[]{:S(2)}) collective-permute-start(bf16[32,640]{1,0:T(8,128)(2,1)} %get-tuple-element.30), channel_id=1, source_target_pairs={{0,768},{128,896},{256,0},{384,128},{512,256},{640,384},{768,512},... | collective-permute-start | bytes 122888 | tf_op jit(solution)/shard_map/ppermute | solution.py:301
  92.5 5.4 %collective-permute-start.7 = (bf16[32,640]{1,0:T(8,128)(2,1)}, bf16[32,640]{1,0:T(8,128)(2,1)S(1)}, u32[]{:S(2)}, u32[]{:S(2)}) collective-permute-start(bf16[32,640]{1,0:T(8,128)(2,1)} %get-tuple-element.31), channel_id=1, source_target_pairs={{0,896},{128,0},{256,128},{384,256},{512,384},{640,512},{768,640},... | collective-permute-start | bytes 122888 | tf_op jit(solution)/shard_map/ppermute | solution.py:301
  97.9 0.8 copy-start.1
  101.8 21.9 %collective-permute-start.8 = (bf16[48,4736]{1,0:T(8,128)(2,1)S(1)}, bf16[48,4736]{1,0:T(8,128)(2,1)S(1)}, u32[]{:S(2)}, u32[]{:S(2)}) collective-permute-start(bf16[48,4736]{1,0:T(8,128)(2,1)S(1)} %convolution_convert_fusion.4), channel_id=1, source_target_pairs={{0,2},{2,4},{4,6},{6,0},{1,3},{3,5},{5,7},{7,1},{8,10},{10,12},{12... | collective-permute-start | bytes 1363976 | tf_op jit(solution)/shard_map/ppermute | solution.py:328
  104.9 52.6 %all-to-all-start.1 = ((bf16[16,64,512]{2,1,0:T(8,128)(2,1)}), bf16[16,64,512]{2,1,0:T(8,128)(2,1)}, u32[]{:S(2)}, u32[]{:S(2)}) async-start(bf16[16,64,512]{2,1,0:T(8,128)(2,1)} %bitcast.13), calls=%async_computation.1 | async-start | bytes 2097152 | tf_op jit(solution)/shard_map/all_to_all | solution.py:331
  114.7 120.3 %all-gather.2.cloned.1.call-start = ((), (), s32[]{:S(2)}) async-start(), calls=%async_computation.3 | async-start | bytes 3096576 | tf_op jit(solution)/shard_map/all_gather | solution.py:339
  115.2 15.4 %collective-permute-start.9 = (bf16[48,4736]{1,0:T(8,128)(2,1)S(1)}, bf16[48,4736]{1,0:T(8,128)(2,1)S(1)}, u32[]{:S(2)}, u32[]{:S(2)}) collective-permute-start(bf16[48,4736]{1,0:T(8,128)(2,1)S(1)} %convolution_convert_fusion.3), channel_id=1, source_target_pairs={{0,4},{2,6},{4,0},{6,2},{1,5},{3,7},{5,1},{7,3},{8,12},{10,14},{12... | collective-permute-start | bytes 1363976 | tf_op jit(solution)/shard_map/ppermute | solution.py:328
  120.1 19.4 %collective-permute-start.10 = (bf16[48,4736]{1,0:T(8,128)(2,1)S(1)}, bf16[48,4736]{1,0:T(8,128)(2,1)S(1)}, u32[]{:S(2)}, u32[]{:S(2)}) collective-permute-start(bf16[48,4736]{1,0:T(8,128)(2,1)S(1)} %convolution_convert_fusion.2), channel_id=1, source_target_pairs={{0,6},{2,0},{4,2},{6,4},{1,7},{3,1},{5,3},{7,5},{8,14},{10,8},{12,... | collective-permute-start | bytes 1363976 | tf_op jit(solution)/shard_map/ppermute | solution.py:328
  139.5 3.1 %copy-start = (bf16[1,3584,1024]{2,1,0:T(8,128)(2,1)S(1)}, bf16[1,3584,1024]{2,1,0:T(8,128)(2,1)}, u32[]{:S(2)}) copy-start(bf16[1,3584,1024]{2,1,0:T(8,128)(2,1)} %refs_4_.1) | copy-start | bytes 22020100
  148.8 23.2 %collective-permute-start.12 = (bf16[48,4736]{1,0:T(8,128)(2,1)S(1)}, bf16[48,4736]{1,0:T(8,128)(2,1)}, u32[]{:S(2)}, u32[]{:S(2)}) collective-permute-start(bf16[48,4736]{1,0:T(8,128)(2,1)S(1)} %get-tuple-element.36), channel_id=1, source_target_pairs={{0,4},{2,6},{4,0},{6,2},{1,5},{3,7},{5,1},{7,3},{8,12},{10,14},{12... | collective-permute-start | bytes 1363976 | tf_op jit(solution)/shard_map/ppermute | solution.py:346
  153.5 20.7 %collective-permute-start.11 = (bf16[48,4736]{1,0:T(8,128)(2,1)S(1)}, bf16[48,4736]{1,0:T(8,128)(2,1)}, u32[]{:S(2)}, u32[]{:S(2)}) collective-permute-start(bf16[48,4736]{1,0:T(8,128)(2,1)S(1)} %get-tuple-element.35), channel_id=1, source_target_pairs={{0,6},{2,0},{4,2},{6,4},{1,7},{3,1},{5,3},{7,5},{8,14},{10,8},{12,... | collective-permute-start | bytes 1363976 | tf_op jit(solution)/shard_map/ppermute | solution.py:346
  157.6 16.6 %collective-permute-start.13 = (bf16[48,4736]{1,0:T(8,128)(2,1)S(1)}, bf16[48,4736]{1,0:T(8,128)(2,1)S(1)}, u32[]{:S(2)}, u32[]{:S(2)}) collective-permute-start(bf16[48,4736]{1,0:T(8,128)(2,1)S(1)} %get-tuple-element.39), channel_id=1, source_target_pairs={{0,2},{2,4},{4,6},{6,0},{1,3},{3,5},{5,7},{7,1},{8,10},{10,12},{12... | collective-permute-start | bytes 1363976 | tf_op jit(solution)/shard_map/ppermute | solution.py:346
  162.9 29.3 %collective-permute-start.17 = (bf16[8,48,512]{2,1,0:T(8,128)(2,1)S(1)}, bf16[8,48,512]{2,1,0:T(8,128)(2,1)S(1)}, u32[]{:S(2)}, u32[]{:S(2)}) collective-permute-start(bf16[8,48,512]{2,1,0:T(8,128)(2,1)S(1)} %convolution_convert_fusion.6), channel_id=1, source_target_pairs={{0,6},{2,0},{4,2},{6,4},{1,7},{3,1},{5,3},{7,5},{8,14},{10,8},{12,... | collective-permute-start | bytes 1179656 | tf_op jit(solution)/shard_map/ppermute | solution.py:375
  170.0 22.3 %collective-permute-start.16 = (bf16[8,48,512]{2,1,0:T(8,128)(2,1)}, bf16[8,48,512]{2,1,0:T(8,128)(2,1)S(1)}, u32[]{:S(2)}, u32[]{:S(2)}) collective-permute-start(bf16[8,48,512]{2,1,0:T(8,128)(2,1)} %convolution_convert_fusion.7), channel_id=1, source_target_pairs={{0,4},{2,6},{4,0},{6,2},{1,5},{3,7},{5,1},{7,3},{8,12},{10,14},{12... | collective-permute-start | bytes 1179656 | tf_op jit(solution)/shard_map/ppermute | solution.py:375
  176.9 40.5 %all-to-all-start.2 = ((bf16[16,8,4736]{2,1,0:T(8,128)(2,1)}), bf16[16,8,4736]{2,1,0:T(8,128)(2,1)S(1)}, u32[]{:S(2)}, u32[]{:S(2)}) async-start(bf16[16,8,4736]{2,1,0:T(8,128)(2,1)} %fusion.1), calls=%async_computation.2 | async-start | bytes 2424832 | tf_op jit(solution)/shard_map/all_to_all | solution.py:357
  187.4 13.9 %collective-permute-start.15 = (bf16[8,48,512]{2,1,0:T(8,128)(2,1)S(1)}, bf16[8,48,512]{2,1,0:T(8,128)(2,1)S(1)}, u32[]{:S(2)}, u32[]{:S(2)}) collective-permute-start(bf16[8,48,512]{2,1,0:T(8,128)(2,1)S(1)} %convolution_convert_fusion.8), channel_id=1, source_target_pairs={{0,2},{2,4},{4,6},{6,0},{1,3},{3,5},{5,7},{7,1},{8,10},{10,12},{12... | collective-permute-start | bytes 1179656 | tf_op jit(solution)/shard_map/ppermute | solution.py:375
  202.9 32.1 %copy-start.3 = (bf16[1344,512]{1,0:T(8,128)(2,1)S(1)}, bf16[1344,512]{1,0:T(8,128)(2,1)}, u32[]{:S(2)}) copy-start(bf16[1344,512]{1,0:T(8,128)(2,1)} %reshape.235) | copy-start | bytes 4128772
  217.7 22.0 %collective-permute-start.14 = (bf16[16,4736]{1,0:T(8,128)(2,1)S(1)}, bf16[16,4736]{1,0:T(8,128)(2,1)S(1)}, u32[]{:S(2)}, u32[]{:S(2)}) collective-permute-start(bf16[16,4736]{1,0:T(8,128)(2,1)S(1)} %slice.76), channel_id=1, source_target_pairs={{0,513},{128,641},{256,769},{384,897},{512,1},{640,129},{768,257},... | collective-permute-start | bytes 454664 | tf_op jit(solution)/shard_map/ppermute | solution.py:387
Sparse Core Ops, SparseCore 0:
  148.8 86.0 all-gather.1

commit v6 on v4

--- a/solution.py
+++ b/solution.py
@@ -110,6 +110,44 @@
     return result[:count], result[count]
 
 
+def window_kernel(hidden, width, starts, rows_ref, fold_ref, out_ref):
+    f32 = jnp.float32
+    bf = jnp.bfloat16
+    window = out_ref.shape[2]
+    gates = jnp.dot(
+        rows_ref[:, hidden + width :], fold_ref[...], preferred_element_type=f32
+    )
+    lane = lax.broadcasted_iota(jnp.int32, gates.shape, 1)
+    for k, (start, spare_first) in enumerate(starts):
+        at = hidden + start
+        if spare_first:
+            edge = jnp.where(lane < 64, gates, rows_ref[:, at : at + 128].astype(f32))
+            out_ref[k, :, :128] = edge.astype(bf)
+            if window > 128:
+                out_ref[k, :, 128:] = rows_ref[:, at + 128 : at + window]
+        else:
+            last = at + window - 128
+            edge = jnp.where(lane < 64, rows_ref[:, last : last + 128].astype(f32), gates)
+            out_ref[k, :, window - 128 :] = edge.astype(bf)
+            if window > 128:
+                out_ref[k, :, : window - 128] = rows_ref[:, at:last]
+
+
+def share_windows(rows, fold, hidden, width, reps):
+    share = width // reps
+    window = share + 64
+    starts = tuple((k * share // 128 * 128, k * share % 128 != 0) for k in range(reps))
+    vmem = pl.BlockSpec(memory_space=pltpu.VMEM)
+    return pl.pallas_call(
+        functools.partial(window_kernel, hidden, width, starts),
+        out_shape=jax.ShapeDtypeStruct((reps, rows.shape[0], window), jnp.bfloat16),
+        in_specs=[vmem, vmem],
+        out_specs=vmem,
+        compiler_params=pltpu.CompilerParams(vmem_limit_bytes=16 * 1024 * 1024),
+        cost_estimate=pl.CostEstimate(flops=0, bytes_accessed=1024, transcendentals=0),
+    )(rows, fold)
+
+
 def on_device(activations, cotangent, gates, experts, groups, weights):
     reps = lax.axis_size("rep")
     nodes = lax.axis_size("node")
@@ -145,8 +183,6 @@
     own = jnp.concatenate([cotangent, activations, gate_wide], axis=1)
     wide = own.shape[1]
     other = lax.ppermute(own, ("rep", "half"), pairs)
-    own, other = lax.optimization_barrier((own, other))
-    along_z = lax.all_gather(own[:, hidden:], ("half", "rep"), axis=0, tiled=True)
     both = jnp.concatenate([own, other], axis=0)
 
     places = 2 * rows_one
@@ -171,7 +207,8 @@
         send_rows.reshape(nodes, 2 * blocks, wide), "node", 0, 0, tiled=True
     ).reshape(places, wide)
 
-    cap2 = -(-2 * cap // 16) * 16
+    filled = 2 * cap
+    cap2 = -(-filled // 16) * 16
     before = (place_index[:, None] < place_index[None, :]).astype(bf)
     slot_at = jnp.arange(cap2, dtype=jnp.int32).astype(f32)
 
@@ -198,68 +235,34 @@
         (((1,), (1,)), ((), ())),
         preferred_element_type=f32,
     ).astype(bf)
-    ring_rows = reps * 2 * blocks
-    row_index = jnp.arange(nodes * ring_rows, dtype=jnp.int32)
-    token_index = jnp.arange(reps * 2 * tokens, dtype=jnp.int32)
-    token_rep = token_index // tokens % reps
-    token_block = token_index % tokens // block
-    token_place = jnp.where(
-        token_index // (tokens * reps) == half_at,
-        token_rep * 2 * blocks + token_block,
-        (token_rep + reps // 2) % reps * 2 * blocks + blocks + token_block,
-    )
-    expert_index = jnp.arange(total, dtype=jnp.int32)
-    row_expert = (row_index // ring_rows)[:, None] == (expert_index // locals_)[None, :]
-    ring_gates = along_z[:, width:]
-    row_hit = lax.dot_general(
-        row_expert.astype(bf),
-        (ring_gates != 0).astype(bf),
-        (((1,), (1,)), ((), ())),
-        preferred_element_type=f32,
-    )
-    ring_placing = (
-        (row_hit > 0) & ((row_index % ring_rows)[:, None] == token_place[None, :])
-    ).astype(bf)
-    spare = -share % 128
-    fold = ((expert_index % locals_)[:, None] == jnp.arange(spare)[None, :]).astype(bf)
-    row_gates = jnp.where(
-        row_expert, jnp.dot(ring_placing, ring_gates, preferred_element_type=f32), 0.0
-    ).astype(bf)
-    cols = jnp.concatenate(
-        [
-            jnp.dot(
-                ring_placing,
-                lax.dynamic_slice_in_dim(along_z, rep_at * share, share, 1),
-                preferred_element_type=f32,
-            ),
-            jnp.dot(row_gates, fold, preferred_element_type=f32),
-        ],
-        axis=1,
-    ).astype(bf)
+    window = share + 64
+    offset = rep_at * share % 128
+    gate_start = jnp.where(offset == 0, share, 0)
+    lane = jnp.arange(window, dtype=jnp.int32)
+    narrow = jnp.arange(128, dtype=jnp.int32)
+    fold = (
+        (jnp.arange(total, dtype=jnp.int32)[:, None] == (node_at * locals_ + narrow % 64)[None, :])
+        & (narrow % 64 < locals_)[None, :]
+    ).astype(bf)
+    cols = share_windows(rows, fold, hidden, width, reps)
+    cols = lax.all_to_all(cols, "rep", 0, 0, tiled=True)
 
     picker = pickers(group_gates)
     sent = [
         jnp.dot(p, rows, preferred_element_type=f32).astype(bf) for p in picker[1:]
     ]
     moved = [lax.ppermute(sent[j - 1], "x", ring(xs, j)) for j in range(1, xs)]
-    kept, cols = lax.optimization_barrier((picker[0], cols))
-    slabs = [jnp.dot(kept, rows, preferred_element_type=f32).astype(bf)] + moved
-    taken = xs * cap2
-    cols = lax.all_to_all(
-        cols.reshape(nodes, ring_rows, share + spare), "node", 0, 0, tiled=True
-    )
+    slabs = [jnp.dot(picker[0], rows, preferred_element_type=f32).astype(bf)] + moved
 
     mine = jnp.arange(total, dtype=jnp.int32) == node_at * locals_ + x_at * 2 + half_at
     back, grad_pre = expert(slabs, weights, mine.astype(f32)[None, :])
 
     gathered = lax.all_gather(grad_pre, "rep", axis=0, tiled=True)
 
-    last = xs - 1
-    back_last, cols = lax.optimization_barrier((back[last], cols))
     back_slots = jnp.concatenate(
         [back[0]]
         + [
-            lax.ppermute(back_last if j == last else back[j], "x", ring(xs, -j))
+            lax.ppermute(back[j], "x", ring(xs, -j))
             for j in range(1, xs)
         ],
         axis=0,
@@ -270,18 +273,13 @@
         (((0,), (0,)), ((), ())),
         preferred_element_type=f32,
     ).astype(bf)
+    back_rows, cols = lax.optimization_barrier((back_rows, cols))
     home_rows = lax.all_to_all(
         back_rows.reshape(nodes, 2 * blocks, wide), "node", 0, 0, tiled=True
     ).reshape(places, wide)
 
-    cols = (
-        cols.reshape(nodes, reps, 2 * blocks, share + spare)
-        .transpose(1, 0, 2, 3)
-        .reshape(reps, places, share + spare)
-    )
     gate_lane = (
-        share + jnp.arange(locals_, dtype=jnp.int32)[:, None]
-        == jnp.arange(share + spare, dtype=jnp.int32)[None, :]
+        gate_start + jnp.arange(locals_, dtype=jnp.int32)[:, None] == lane[None, :]
     ).astype(bf)
     all_gates = jnp.einsum("lc,prc->plr", gate_lane, cols, preferred_element_type=f32)
     share_sent = [
@@ -291,8 +289,10 @@
     share_rows = [share_sent[0]] + [
         lax.ppermute(share_sent[j], "x", ring(xs, j)) for j in range(1, xs)
     ]
-    x_cols = jnp.stack(share_rows, axis=1).reshape(reps * taken, cols.shape[2])
-    x_cols = x_cols[:, :share]
+    x_cols = jnp.stack(share_rows, axis=1)
+    x_cols = lax.dynamic_slice_in_dim(
+        x_cols.reshape(reps * xs * cap2, window), offset, share, 1
+    )
     grad_share = lax.dot_general(
         x_cols, gathered, (((0,), (0,)), ((), ())), preferred_element_type=f32
     )

time: 261 us -> 230 us (0.88)
  waiting for transfers between devices: 117 us -> 101 us
  matrix products: 25.9 us -> 19.9 us
  starting transfers between devices: 80.5 us -> 77.3 us
  other arithmetic: 6.21 us -> 3.13 us
  local copies, waits for them, and re-layouts: 8.98 us -> 6.01 us
    all_gather x1 -> x0, waiting for transfers between devices: 24.1 us -> none  [on_device(): lax.all_gather(own[:, hidden:], ('half', 'rep'), axis=0, tiled=True)]
    ppermute x3, waiting for transfers between devices: 0.01 us -> 16.3 us  [on_device(): moved = [lax.ppermute(sent[j - 1], 'x', ring(xs, j)) for j in range(1, xs)]]
    all_to_all x1, waiting for transfers between devices: 12.4 us -> 0.01 us  [on_device(): cols = lax.all_to_all(cols, 'rep', 0, 0, tiled=True)]
    all_to_all x1, starting transfers between devices: 16.5 us -> 5.42 us  [on_device(): cols = lax.all_to_all(cols, 'rep', 0, 0, tiled=True)]
    dot_general x4 -> x1, matrix products: 6.59 us -> 0.36 us  [on_device(): jnp.dot(picker[0], rows, preferred_element_type=f32).astype(bf)]
    ppermute x3, waiting for transfers between devices: 10.5 us -> 16.2 us  [on_device(): lax.ppermute(back[j], 'x', ring(xs, -j))]
    ppermute x1, starting transfers between devices: 4.61 us -> 8.92 us  [on_device(): returned = lax.ppermute(home[tokens:].astype(bf), ('rep', 'half'), pairs)]
  transfers between devices with their start and end apart: 16 -> 15, of which waited for: 10 -> 10; matrix products, arithmetic and copies ran while one was open for 12% -> 8% of each run, Pallas kernels for 2% -> 3%
where the time goes in v6:
time: 230 us; the launch traced here: 229 us
  waiting for transfers between devices  101 us (44%)
  starting transfers between devices  77.3 us (34%)
  matrix products  19.9 us (9%)
  between operations  14.4 us (6%)
  Pallas kernels  6.43 us (3%)
  local copies, waits for them, and re-layouts  6.01 us (3%)
  other arithmetic  3.13 us (1%)
    all_to_all x1, waiting for transfers between devices, on_device(): lax.all_to_all(send_rows.reshape(nodes, 2 * blocks, wide), 'node', 0, 0,...  31.1 us
    ppermute x1, starting transfers between devices, on_device(): other = lax.ppermute(own, ('rep', 'half'), pairs)  18.7 us
    ppermute x3, waiting for transfers between devices, on_device(): moved = [lax.ppermute(sent[j - 1], 'x', ring(xs, j)) for j in range(1, xs)]  16.3 us
    ppermute x3, waiting for transfers between devices, on_device(): lax.ppermute(back[j], 'x', ring(xs, -j))  16.2 us
    ppermute x3, waiting for transfers between devices, on_device(): lax.ppermute(share_sent[j], 'x', ring(xs, j))  14.1 us
    ppermute x1, waiting for transfers between devices, on_device(): other = lax.ppermute(own, ('rep', 'half'), pairs)  12.3 us
    all_gather x1, waiting for transfers between devices, on_device(): gathered = lax.all_gather(grad_pre, 'rep', axis=0, tiled=True)  11.3 us
    ppermute x3, starting transfers between devices, on_device(): moved = [lax.ppermute(sent[j - 1], 'x', ring(xs, j)) for j in range(1, xs)]  10.5 us
  transfers between devices with their start and end apart: 15, of which 10 were waited for; matrix products, arithmetic and copies ran while one was open for 8% of the time, Pallas kernels for 3%

profile of v6, /device:TPU:1, one launch (start us, length us, event | category | flops | bytes accessed | tf_op | source)
XLA Modules:
  0.0 228.6 jit_solution(1006527452471668707)
XLA Ops:
  7.2 0.8 copy.16
  7.9 0.7 broadcast_multiply_fusion
  8.6 0.7 add.133
  9.3 0.1 copy.15
  9.4 0.1 select_reduce_fusion.1
  9.5 0.9 pad_maximum_fusion.1
  10.4 18.7 %collective-permute-start = (bf16[16,4736]{1,0:T(8,128)(2,1)S(1)}, bf16[16,4736]{1,0:T(8,128)(2,1)S(1)}, u32[]{:S(2)}, u32[]{:S(2)}) collective-permute-start(bf16[16,4736]{1,0:T(8,128)(2,1)S(1)} %pad_maximum_fusion.1), channel_id=1, source_target_pairs={{0,513},{128,641},{256,769},{384,897},{512,1},{640,129},{768,257},... | collective-permute-start | bytes 454664 | tf_op jit(solution)/shard_map/ppermute | solution.py:185
  29.2 12.3 %collective-permute-done = bf16[16,4736]{1,0:T(8,128)(2,1)S(1)} collective-permute-done((bf16[16,4736]{1,0:T(8,128)(2,1)S(1)}, bf16[16,4736]{1,0:T(8,128)(2,1)S(1)}, u32[]{:S(2)}, u32[]{:S(2)}) %collective-permute-start) | collective-permute-done | bytes 151584 | tf_op jit(solution)/shard_map/ppermute | solution.py:185
  41.5 0.2 fusion.17
  41.7 2.5 %fusion = bf16[16,8,4736]{2,1,0:T(8,128)(2,1)} fusion(pred[128,32]{0,1:T(32,128)(4,1)S(1)} %fusion.17, bf16[16,4736]{1,0:T(8,128)(2,1)S(1)} %collective-permute-done, bf16[16,128]{1,0:T(8,128)(2,1)S(1)} %select_reduce_fusion.1, bf16[16,3584]{1,0:T(8,128)(2,1)} %param.6, bf16[16,1024]{1,0:T(8,128)(2,1)} %param.7), kind=kOutput, calls=%fused_computation.2 | convolution fusion | flops 40615936 | bytes 1519616 | tf_op jit(solution)/shard_map/dot_general | solution.py:205
  44.1 8.7 %all-to-all-start = ((bf16[16,8,4736]{2,1,0:T(8,128)(2,1)}), bf16[16,8,4736]{2,1,0:T(8,128)(2,1)S(1)}, u32[]{:S(2)}, u32[]{:S(2)}) async-start(bf16[16,8,4736]{2,1,0:T(8,128)(2,1)} %fusion), calls=%async_computation | async-start | bytes 2424832 | tf_op jit(solution)/shard_map/all_to_all | solution.py:206
  52.9 31.1 %all-to-all-done = bf16[16,8,4736]{2,1,0:T(8,128)(2,1)S(1)} async-done(((bf16[16,8,4736]{2,1,0:T(8,128)(2,1)}), bf16[16,8,4736]{2,1,0:T(8,128)(2,1)S(1)}, u32[]{:S(2)}, u32[]{:S(2)}) %all-to-all-start) | async-done | bytes 1212448 | tf_op jit(solution)/shard_map/all_to_all | solution.py:206
  84.0 0.2 select_reduce_fusion.2
  84.2 0.1 convolution_bitcast_fusion.2
  84.4 0.4 convolution_convert_fusion.4
  84.8 3.1 %collective-permute-start.1 = (bf16[48,4736]{1,0:T(8,128)(2,1)S(1)}, bf16[48,4736]{1,0:T(8,128)(2,1)S(1)}, u32[]{:S(2)}, u32[]{:S(2)}) collective-permute-start(bf16[48,4736]{1,0:T(8,128)(2,1)S(1)} %convolution_convert_fusion.4), channel_id=1, source_target_pairs={{0,2},{2,4},{4,6},{6,0},{1,3},{3,5},{5,7},{7,1},{8,10},{10,12},{12... | collective-permute-start | bytes 1363976 | tf_op jit(solution)/shard_map/ppermute | solution.py:254
  87.9 1.2 shard_map.94
  89.0 5.4 %all-to-all-start.1 = ((bf16[8,128,512]{2,1,0:T(8,128)(2,1)}), bf16[8,128,512]{2,1,0:T(8,128)(2,1)}, u32[]{:S(2)}, u32[]{:S(2)}) async-start(bf16[8,128,512]{2,1,0:T(8,128)(2,1)} %shard_map.94), calls=%async_computation.1 | async-start | bytes 2097152 | tf_op jit(solution)/shard_map/all_to_all | solution.py:248
  94.5 0.1 convolution_bitcast_fusion.1
  94.7 0.4 convolution_convert_fusion.3
  95.0 4.4 %collective-permute-start.2 = (bf16[48,4736]{1,0:T(8,128)(2,1)S(1)}, bf16[48,4736]{1,0:T(8,128)(2,1)S(1)}, u32[]{:S(2)}, u32[]{:S(2)}) collective-permute-start(bf16[48,4736]{1,0:T(8,128)(2,1)S(1)} %convolution_convert_fusion.3), channel_id=1, source_target_pairs={{0,4},{2,6},{4,0},{6,2},{1,5},{3,7},{5,1},{7,3},{8,12},{10,14},{12... | collective-permute-start | bytes 1363976 | tf_op jit(solution)/shard_map/ppermute | solution.py:254
  99.4 0.1 convolution_bitcast_fusion
  99.5 0.4 convolution_convert_fusion.2
  99.9 3.1 %collective-permute-start.3 = (bf16[48,4736]{1,0:T(8,128)(2,1)S(1)}, bf16[48,4736]{1,0:T(8,128)(2,1)S(1)}, u32[]{:S(2)}, u32[]{:S(2)}) collective-permute-start(bf16[48,4736]{1,0:T(8,128)(2,1)S(1)} %convolution_convert_fusion.2), channel_id=1, source_target_pairs={{0,6},{2,0},{4,2},{6,4},{1,7},{3,1},{5,3},{7,5},{8,14},{10,8},{12,... | collective-permute-start | bytes 1363976 | tf_op jit(solution)/shard_map/ppermute | solution.py:254
  103.0 0.1 convolution_bitcast_fusion.3
  103.1 0.4 convolution_convert_fusion.5.refs_0_
  103.5 7.5 %collective-permute-done.2.refs_2_ = bf16[48,4736]{1,0:T(8,128)(2,1)S(1)} collective-permute-done((bf16[48,4736]{1,0:T(8,128)(2,1)S(1)}, bf16[48,4736]{1,0:T(8,128)(2,1)S(1)}, u32[]{:S(2)}, u32[]{:S(2)}) %collective-permute-start.2) | collective-permute-done | bytes 454688 | tf_op jit(solution)/shard_map/ppermute | solution.py:254
  110.9 8.9 %collective-permute-done.3.refs_3_ = bf16[48,4736]{1,0:T(8,128)(2,1)S(1)} collective-permute-done((bf16[48,4736]{1,0:T(8,128)(2,1)S(1)}, bf16[48,4736]{1,0:T(8,128)(2,1)S(1)}, u32[]{:S(2)}, u32[]{:S(2)}) %collective-permute-start.3) | collective-permute-done | bytes 454688 | tf_op jit(solution)/shard_map/ppermute | solution.py:254
  119.8 3.1 %copy-done = bf16[1,3584,1024]{2,1,0:T(8,128)(2,1)S(1)} copy-done((bf16[1,3584,1024]{2,1,0:T(8,128)(2,1)S(1)}, bf16[1,3584,1024]{2,1,0:T(8,128)(2,1)}, u32[]{:S(2)}) %copy-start) | copy-done | bytes 7340056
  122.9 5.3 %shard_map.93 = (bf16[48,4736]{1,0:T(8,128)(2,1)S(1)}, bf16[48,4736]{1,0:T(8,128)(2,1)S(1)}, bf16[48,4736]{1,0:T(8,128)(2,1)S(1)}, bf16[48,4736]{1,0:T(8,128)(2,1)S(1)}, bf16[192,1024]{1,0:T(8,128)(2,1)}) custom-call(f32[1,128]{1,0:T(1,128)S(1)} %compare_convert_fusion.mine_ref, bf16[48,4736]{1,0:T(8,128)(2,1)S(1)} %convolution_convert_fusion.5.refs_0_, ...), custom_call_target="tpu_custom_call" | custom-call | bytes 1024 | tf_op jit(solution)/shard_map/pallas_call | solution.py:96
  128.2 4.0 %collective-permute-start.6 = (bf16[48,4736]{1,0:T(8,128)(2,1)S(1)}, bf16[48,4736]{1,0:T(8,128)(2,1)S(1)}, u32[]{:S(2)}, u32[]{:S(2)}) collective-permute-start(bf16[48,4736]{1,0:T(8,128)(2,1)S(1)} %get-tuple-element.16), channel_id=1, source_target_pairs={{0,2},{2,4},{4,6},{6,0},{1,3},{3,5},{5,7},{7,1},{8,10},{10,12},{12... | collective-permute-start | bytes 1363976 | tf_op jit(solution)/shard_map/ppermute | solution.py:265
  132.2 3.4 %collective-permute-start.5 = (bf16[48,4736]{1,0:T(8,128)(2,1)S(1)}, bf16[48,4736]{1,0:T(8,128)(2,1)S(1)}, u32[]{:S(2)}, u32[]{:S(2)}) collective-permute-start(bf16[48,4736]{1,0:T(8,128)(2,1)S(1)} %get-tuple-element.15), channel_id=1, source_target_pairs={{0,4},{2,6},{4,0},{6,2},{1,5},{3,7},{5,1},{7,3},{8,12},{10,14},{12... | collective-permute-start | bytes 1363976 | tf_op jit(solution)/shard_map/ppermute | solution.py:265
  135.5 3.2 %collective-permute-start.4 = (bf16[48,4736]{1,0:T(8,128)(2,1)S(1)}, bf16[48,4736]{1,0:T(8,128)(2,1)S(1)}, u32[]{:S(2)}, u32[]{:S(2)}) collective-permute-start(bf16[48,4736]{1,0:T(8,128)(2,1)S(1)} %get-tuple-element.14), channel_id=1, source_target_pairs={{0,6},{2,0},{4,2},{6,4},{1,7},{3,1},{5,3},{7,5},{8,14},{10,8},{12,... | collective-permute-start | bytes 1363976 | tf_op jit(solution)/shard_map/ppermute | solution.py:265
  138.7 0.1 compare_and_fusion.3
  138.8 4.3 %collective-permute-done.6 = bf16[48,4736]{1,0:T(8,128)(2,1)S(1)} collective-permute-done((bf16[48,4736]{1,0:T(8,128)(2,1)S(1)}, bf16[48,4736]{1,0:T(8,128)(2,1)S(1)}, u32[]{:S(2)}, u32[]{:S(2)}) %collective-permute-start.6) | collective-permute-done | bytes 454688 | tf_op jit(solution)/shard_map/ppermute | solution.py:265
  143.1 10.6 %collective-permute-done.5 = bf16[48,4736]{1,0:T(8,128)(2,1)S(1)} collective-permute-done((bf16[48,4736]{1,0:T(8,128)(2,1)S(1)}, bf16[48,4736]{1,0:T(8,128)(2,1)S(1)}, u32[]{:S(2)}, u32[]{:S(2)}) %collective-permute-start.5) | collective-permute-done | bytes 454688 | tf_op jit(solution)/shard_map/ppermute | solution.py:265
  153.7 1.4 collective-permute-done.4
  155.1 1.6 convolution_convert_fusion
  156.6 4.8 %all-to-all-start.2 = ((bf16[16,8,4736]{2,1,0:T(8,128)(2,1)}), bf16[16,8,4736]{2,1,0:T(8,128)(2,1)S(1)}, u32[]{:S(2)}, u32[]{:S(2)}) async-start(bf16[16,8,4736]{2,1,0:T(8,128)(2,1)} %bitcast.11), calls=%async_computation.2 | async-start | bytes 2424832 | tf_op jit(solution)/shard_map/all_to_all | solution.py:277
  161.5 1.6 fusion.16
  163.1 0.1 fusion.61
  163.2 0.1 fusion.54
  163.4 1.6 convolution_convert_fusion.6
  164.9 4.3 %collective-permute-start.10 = (bf16[8,48,512]{2,1,0:T(8,128)(2,1)S(1)}, bf16[8,48,512]{2,1,0:T(8,128)(2,1)S(1)}, u32[]{:S(2)}, u32[]{:S(2)}) collective-permute-start(bf16[8,48,512]{2,1,0:T(8,128)(2,1)S(1)} %convolution_convert_fusion.6), channel_id=1, source_target_pairs={{0,6},{2,0},{4,2},{6,4},{1,7},{3,1},{5,3},{7,5},{8,14},{10,8},{12,... | collective-permute-start | bytes 1179656 | tf_op jit(solution)/shard_map/ppermute | solution.py:290
  169.2 0.1 fusion.55
  169.3 1.6 convolution_convert_fusion.7
  170.9 3.4 %collective-permute-start.9 = (bf16[8,48,512]{2,1,0:T(8,128)(2,1)S(1)}, bf16[8,48,512]{2,1,0:T(8,128)(2,1)S(1)}, u32[]{:S(2)}, u32[]{:S(2)}) collective-permute-start(bf16[8,48,512]{2,1,0:T(8,128)(2,1)S(1)} %convolution_convert_fusion.7), channel_id=1, source_target_pairs={{0,4},{2,6},{4,0},{6,2},{1,5},{3,7},{5,1},{7,3},{8,12},{10,14},{12... | collective-permute-start | bytes 1179656 | tf_op jit(solution)/shard_map/ppermute | solution.py:290
  174.4 0.1 fusion.56
  174.5 1.6 convolution_convert_fusion.8
  176.1 1.9 collective-permute-start.8
  178.0 0.1 fusion.57
  178.1 1.6 fusion.12
  179.7 4.9 %collective-permute-done.9 = bf16[8,48,512]{2,1,0:T(8,128)(2,1)S(1)} collective-permute-done((bf16[8,48,512]{2,1,0:T(8,128)(2,1)S(1)}, bf16[8,48,512]{2,1,0:T(8,128)(2,1)S(1)}, u32[]{:S(2)}, u32[]{:S(2)}) %collective-permute-start.9) | collective-permute-done | bytes 393248 | tf_op jit(solution)/shard_map/ppermute | solution.py:290
  184.6 9.2 %collective-permute-done.8 = bf16[8,48,512]{2,1,0:T(8,128)(2,1)S(1)} collective-permute-done((bf16[8,48,512]{2,1,0:T(8,128)(2,1)S(1)}, bf16[8,48,512]{2,1,0:T(8,128)(2,1)S(1)}, u32[]{:S(2)}, u32[]{:S(2)}) %collective-permute-start.8) | collective-permute-done | bytes 393248 | tf_op jit(solution)/shard_map/ppermute | solution.py:290
  193.9 0.2 pad_maximum_fusion
  194.1 0.1 copy.17
  194.2 0.3 fusion.10
  194.5 8.9 %collective-permute-start.7 = (bf16[16,4736]{1,0:T(8,128)(2,1)S(1)}, bf16[16,4736]{1,0:T(8,128)(2,1)S(1)}, u32[]{:S(2)}, u32[]{:S(2)}) collective-permute-start(bf16[16,4736]{1,0:T(8,128)(2,1)S(1)} %slice.41), channel_id=1, source_target_pairs={{0,513},{128,641},{256,769},{384,897},{512,1},{640,129},{768,257},... | collective-permute-start | bytes 454664 | tf_op jit(solution)/shard_map/ppermute | solution.py:302
  203.5 11.3 %all-gather.2.cloned.1.call-done = bf16[1536,1024]{1,0:T(8,128)(2,1)} async-done(((bf16[192,1024]{1,0:T(8,128)(2,1)}), bf16[1536,1024]{1,0:T(8,128)(2,1)}) %all-gather.2.cloned.1.call-update) | async-done | bytes 3145744 | tf_op jit(solution)/shard_map/all_gather | solution.py:260
  214.8 4.9 %fusion.8 = f32[448,1024]{1,0:T(8,128)} fusion(bf16[1536,1024]{1,0:T(8,128)(2,1)} %all-gather.2.cloned.1.call-done, bf16[1536,512]{1,0:T(8,128)(2,1)S(1)} %bitcast.56, s32[]{:T(128)S(6)} %select_n.143), kind=kOutput, calls=%fused_computation.15 | convolution fusion | flops 1409286144 | bytes 6553604 | tf_op jit(solution)/shard_map/dot_general | solution.py:296
  219.7 0.6 slice.34
  220.3 0.7 slice.35
  220.9 0.2 select_reduce_fusion
  221.1 0.7 copy.18
  (31 shorter events, 0.2 us)
Async XLA Ops:
  10.4 31.1 %collective-permute-start = (bf16[16,4736]{1,0:T(8,128)(2,1)S(1)}, bf16[16,4736]{1,0:T(8,128)(2,1)S(1)}, u32[]{:S(2)}, u32[]{:S(2)}) collective-permute-start(bf16[16,4736]{1,0:T(8,128)(2,1)S(1)} %pad_maximum_fusion.1), channel_id=1, source_target_pairs={{0,513},{128,641},{256,769},{384,897},{512,1},{640,129},{768,257},... | collective-permute-start | bytes 454664 | tf_op jit(solution)/shard_map/ppermute | solution.py:185
  44.1 39.9 %all-to-all-start = ((bf16[16,8,4736]{2,1,0:T(8,128)(2,1)}), bf16[16,8,4736]{2,1,0:T(8,128)(2,1)S(1)}, u32[]{:S(2)}, u32[]{:S(2)}) async-start(bf16[16,8,4736]{2,1,0:T(8,128)(2,1)} %fusion), calls=%async_computation | async-start | bytes 2424832 | tf_op jit(solution)/shard_map/all_to_all | solution.py:206
  84.8 18.7 %collective-permute-start.1 = (bf16[48,4736]{1,0:T(8,128)(2,1)S(1)}, bf16[48,4736]{1,0:T(8,128)(2,1)S(1)}, u32[]{:S(2)}, u32[]{:S(2)}) collective-permute-start(bf16[48,4736]{1,0:T(8,128)(2,1)S(1)} %convolution_convert_fusion.4), channel_id=1, source_target_pairs={{0,2},{2,4},{4,6},{6,0},{1,3},{3,5},{5,7},{7,1},{8,10},{10,12},{12... | collective-permute-start | bytes 1363976 | tf_op jit(solution)/shard_map/ppermute | solution.py:254
  89.0 67.6 %all-to-all-start.1 = ((bf16[8,128,512]{2,1,0:T(8,128)(2,1)}), bf16[8,128,512]{2,1,0:T(8,128)(2,1)}, u32[]{:S(2)}, u32[]{:S(2)}) async-start(bf16[8,128,512]{2,1,0:T(8,128)(2,1)} %shard_map.94), calls=%async_computation.1 | async-start | bytes 2097152 | tf_op jit(solution)/shard_map/all_to_all | solution.py:248
  94.5 120.3 %all-gather.2.cloned.1.call-start = ((), (), s32[]{:S(2)}) async-start(), calls=%async_computation.3 | async-start | bytes 3538944 | tf_op jit(solution)/shard_map/all_gather | solution.py:260
  95.0 15.9 %collective-permute-start.2 = (bf16[48,4736]{1,0:T(8,128)(2,1)S(1)}, bf16[48,4736]{1,0:T(8,128)(2,1)S(1)}, u32[]{:S(2)}, u32[]{:S(2)}) collective-permute-start(bf16[48,4736]{1,0:T(8,128)(2,1)S(1)} %convolution_convert_fusion.3), channel_id=1, source_target_pairs={{0,4},{2,6},{4,0},{6,2},{1,5},{3,7},{5,1},{7,3},{8,12},{10,14},{12... | collective-permute-start | bytes 1363976 | tf_op jit(solution)/shard_map/ppermute | solution.py:254
  99.9 19.9 %collective-permute-start.3 = (bf16[48,4736]{1,0:T(8,128)(2,1)S(1)}, bf16[48,4736]{1,0:T(8,128)(2,1)S(1)}, u32[]{:S(2)}, u32[]{:S(2)}) collective-permute-start(bf16[48,4736]{1,0:T(8,128)(2,1)S(1)} %convolution_convert_fusion.2), channel_id=1, source_target_pairs={{0,6},{2,0},{4,2},{6,4},{1,7},{3,1},{5,3},{7,5},{8,14},{10,8},{12,... | collective-permute-start | bytes 1363976 | tf_op jit(solution)/shard_map/ppermute | solution.py:254
  119.8 3.1 %copy-start = (bf16[1,3584,1024]{2,1,0:T(8,128)(2,1)S(1)}, bf16[1,3584,1024]{2,1,0:T(8,128)(2,1)}, u32[]{:S(2)}) copy-start(bf16[1,3584,1024]{2,1,0:T(8,128)(2,1)} %refs_4_.1) | copy-start | bytes 22020100
  128.2 14.9 %collective-permute-start.6 = (bf16[48,4736]{1,0:T(8,128)(2,1)S(1)}, bf16[48,4736]{1,0:T(8,128)(2,1)S(1)}, u32[]{:S(2)}, u32[]{:S(2)}) collective-permute-start(bf16[48,4736]{1,0:T(8,128)(2,1)S(1)} %get-tuple-element.16), channel_id=1, source_target_pairs={{0,2},{2,4},{4,6},{6,0},{1,3},{3,5},{5,7},{7,1},{8,10},{10,12},{12... | collective-permute-start | bytes 1363976 | tf_op jit(solution)/shard_map/ppermute | solution.py:265
  132.2 21.5 %collective-permute-start.5 = (bf16[48,4736]{1,0:T(8,128)(2,1)S(1)}, bf16[48,4736]{1,0:T(8,128)(2,1)S(1)}, u32[]{:S(2)}, u32[]{:S(2)}) collective-permute-start(bf16[48,4736]{1,0:T(8,128)(2,1)S(1)} %get-tuple-element.15), channel_id=1, source_target_pairs={{0,4},{2,6},{4,0},{6,2},{1,5},{3,7},{5,1},{7,3},{8,12},{10,14},{12... | collective-permute-start | bytes 1363976 | tf_op jit(solution)/shard_map/ppermute | solution.py:265
  135.5 19.5 %collective-permute-start.4 = (bf16[48,4736]{1,0:T(8,128)(2,1)S(1)}, bf16[48,4736]{1,0:T(8,128)(2,1)S(1)}, u32[]{:S(2)}, u32[]{:S(2)}) collective-permute-start(bf16[48,4736]{1,0:T(8,128)(2,1)S(1)} %get-tuple-element.14), channel_id=1, source_target_pairs={{0,6},{2,0},{4,2},{6,4},{1,7},{3,1},{5,3},{7,5},{8,14},{10,8},{12,... | collective-permute-start | bytes 1363976 | tf_op jit(solution)/shard_map/ppermute | solution.py:265
  156.6 37.6 %all-to-all-start.2 = ((bf16[16,8,4736]{2,1,0:T(8,128)(2,1)}), bf16[16,8,4736]{2,1,0:T(8,128)(2,1)S(1)}, u32[]{:S(2)}, u32[]{:S(2)}) async-start(bf16[16,8,4736]{2,1,0:T(8,128)(2,1)} %bitcast.11), calls=%async_computation.2 | async-start | bytes 2424832 | tf_op jit(solution)/shard_map/all_to_all | solution.py:277
  164.9 14.8 %collective-permute-start.10 = (bf16[8,48,512]{2,1,0:T(8,128)(2,1)S(1)}, bf16[8,48,512]{2,1,0:T(8,128)(2,1)S(1)}, u32[]{:S(2)}, u32[]{:S(2)}) collective-permute-start(bf16[8,48,512]{2,1,0:T(8,128)(2,1)S(1)} %convolution_convert_fusion.6), channel_id=1, source_target_pairs={{0,6},{2,0},{4,2},{6,4},{1,7},{3,1},{5,3},{7,5},{8,14},{10,8},{12,... | collective-permute-start | bytes 1179656 | tf_op jit(solution)/shard_map/ppermute | solution.py:290
  170.9 13.7 %collective-permute-start.9 = (bf16[8,48,512]{2,1,0:T(8,128)(2,1)S(1)}, bf16[8,48,512]{2,1,0:T(8,128)(2,1)S(1)}, u32[]{:S(2)}, u32[]{:S(2)}) collective-permute-start(bf16[8,48,512]{2,1,0:T(8,128)(2,1)S(1)} %convolution_convert_fusion.7), channel_id=1, source_target_pairs={{0,4},{2,6},{4,0},{6,2},{1,5},{3,7},{5,1},{7,3},{8,12},{10,14},{12... | collective-permute-start | bytes 1179656 | tf_op jit(solution)/shard_map/ppermute | solution.py:290
  176.1 17.8 %collective-permute-start.8 = (bf16[8,48,512]{2,1,0:T(8,128)(2,1)S(1)}, bf16[8,48,512]{2,1,0:T(8,128)(2,1)S(1)}, u32[]{:S(2)}, u32[]{:S(2)}) collective-permute-start(bf16[8,48,512]{2,1,0:T(8,128)(2,1)S(1)} %convolution_convert_fusion.8), channel_id=1, source_target_pairs={{0,2},{2,4},{4,6},{6,0},{1,3},{3,5},{5,7},{7,1},{8,10},{10,12},{12... | collective-permute-start | bytes 1179656 | tf_op jit(solution)/shard_map/ppermute | solution.py:290
  194.5 25.1 %collective-permute-start.7 = (bf16[16,4736]{1,0:T(8,128)(2,1)S(1)}, bf16[16,4736]{1,0:T(8,128)(2,1)S(1)}, u32[]{:S(2)}, u32[]{:S(2)}) collective-permute-start(bf16[16,4736]{1,0:T(8,128)(2,1)S(1)} %slice.41), channel_id=1, source_target_pairs={{0,513},{128,641},{256,769},{384,897},{512,1},{640,129},{768,257},... | collective-permute-start | bytes 454664 | tf_op jit(solution)/shard_map/ppermute | solution.py:302
Sparse Core Ops, SparseCore 0:
  128.3 86.4 all-gather.1
